TPU v7x, 256 devices: a whole 4x4x8 slice. The times are simulated.
256 devices in a mesh: dp: 8 (over y, core), row: 4 (over x), col: 8 (over z).
Axes of the slice: x: 4, y: 4, z: 8, core: 2. Of those that a mesh axis runs over, the one named last changes fastest.
Arguments:
- activations: bfloat16 [12288, 4096], P('dp', 'row'), may hold values from -12.7 to 12.7
- cotangent: bfloat16 [12288, 16384], P('dp', 'col'), may hold values from -0.11456794 to 0.11456794
- param: float32 [4096, 16384], P('row', ('col', 'dp')), may hold values from -6 to 6
- row_state: float32 [4096], P('row'), may hold values from 0.02 to 0.3
- col_state: float32 [16384], P(('col', 'dp')), may hold values from 0.02 to 0.3
Outputs:
- new_param: float32 [4096, 16384], P('row', ('col', 'dp'))
- new_row: float32 [4096], P('row')
- new_col: float32 [16384], P(('col', 'dp'))
All inputs are finite; a program needn't handle non-finite values.
Results may differ from a plain program's by a relative error of at most 0.0003.
Values may be sent and summed in bfloat16 or wider, within the bound.
No kernel may reach another device: no remote copies, remote signals or barrier semaphores. Data moves between devices by JAX's collectives and lax.ppermute only.
A program may use at most 128 MiB of HBM per device.

v0:
```python
import jax
import jax.numpy as jnp
from jax import lax
from jax.sharding import PartitionSpec as P

D = 4096
FF = 16384


decay_rate = 0.9
step_size = 0.3


def contract_tokens(left, right):
    return lax.dot_general(
        left, right, (((0,), (0,)), ((), ())), preferred_element_type=jnp.float32
    )


def per_device(activations, cotangent, param, row_state, col_state):
    gradient = lax.psum_scatter(
        contract_tokens(cotangent, activations), "dp", scatter_dimension=0, tiled=True
    ).T
    squares = gradient * gradient
    row_part = jnp.sum(squares, axis=1)
    col_part = jnp.sum(squares, axis=0)
    row_total = lax.psum(row_part, ("dp", "col"))
    col_total = lax.psum(col_part, "row")
    new_row = decay_rate * row_state + (1.0 - decay_rate) * row_total / FF
    new_col = decay_rate * col_state + (1.0 - decay_rate) * col_total / D
    row_level = lax.psum(jnp.sum(new_row), "row") / D
    update = gradient * lax.rsqrt(new_row[:, None] * new_col[None, :] / row_level)
    update_sum, param_sum = lax.psum(
        (jnp.sum(update * update), jnp.sum(param * param)), ("dp", "row", "col")
    )
    entries = D * FF
    clip = jnp.maximum(1.0, jnp.sqrt(update_sum / entries))
    scale = jnp.sqrt(param_sum / entries)
    new_param = param - step_size * scale * update / clip
    return (new_param, new_row, new_col)


def solution(mesh):
    in_specs = (P("dp", "row"), P("dp", "col"), P("row", ("col", "dp")), P("row"), P(("col", "dp")))
    out_specs = (P("row", ("col", "dp")), P("row"), P(("col", "dp")))
    return jax.shard_map(
        per_device, mesh=mesh, in_specs=in_specs, out_specs=out_specs, check_vma=False
    )
```

profile of v0, /device:TPU:32, one launch (start us, length us, event | category | flops | bytes accessed | tf_op | source)
XLA Modules:
  0.0 308.7 jit_solution(23275046761253372)
XLA Ops:
  7.2 0.0 copy-start
  7.2 0.0 reduce-scatter.2.cloned.1.call-start
  7.2 1.8 copy-done
  9.1 10.8 %fusion.3 = f32[2048,1024]{1,0:T(8,128)} fusion(bf16[1536,2048]{1,0:T(8,128)(2,1)} %param.6, bf16[1536,1024]{1,0:T(8,128)(2,1)S(1)} %copy-done), kind=kOutput, calls=%fused_computation.10 | convolution fusion | flops 6442450944 | bytes 17825792 | tf_op jit(solution)/shard_map/dot_general | solution.py:15
  19.9 0.0 copy-start.3
  19.9 0.0 copy-start.4
  19.9 0.0 reduce-scatter.2.cloned.1.call-update
  19.9 2.1 multiply_reduce_fusion.1
  22.1 55.6 %reduce-scatter.2.cloned.1.call-done = f32[256,1024]{1,0:T(8,128)} async-done(((f32[2048,1024]{1,0:T(8,128)}), f32[256,1024]{1,0:T(8,128)}) %reduce-scatter.2.cloned.1.call-update) | async-done | bytes 1048592 | tf_op jit(solution)/shard_map/reduce_scatter | solution.py:21
  77.7 1.4 fusion
  79.1 124.8 %psum.36 = f32[1024]{0:T(1024)S(1)} all-reduce(f32[1024]{0:T(1024)S(1)} %get-tuple-element.7), channel_id=1, replica_groups=mesh['dp'=8,'row'=4,'col'=8] {'dp','col'}, use_global_device_ids=true, to_apply=%region_4.0 | all-reduce | flops 1024 | bytes 8192 | tf_op jit(solution)/shard_map/psum | solution.py:27
  203.9 0.0 copy-done.3
  203.9 0.6 fusion.2
  204.5 0.0 copy-start.1
  204.5 11.0 %all-reduce.1 = (f32[]{:T(128)}, f32[256]{0:T(256)S(1)}) all-reduce(f32[]{:T(128)} %get-tuple-element.12, f32[256]{0:T(256)S(1)} %get-tuple-element.6), channel_id=1, replica_groups=mesh['dp'=8,'row'=4,'col'=8] {'row'}, use_global_device_ids=true, to_apply=%region_8.0 | all-reduce | flops 257 | bytes 2056 | tf_op jit(solution)/shard_map/psum | solution.py:31
  215.6 0.0 copy-done.4
  215.6 0.0 copy-start.2
  216.2 2.3 multiply_reduce_fusion
  218.5 2.5 copy.8
  221.0 74.0 %all-reduce = (f32[]{:T(128)}, f32[]{:T(128)}) all-reduce(f32[]{:T(128)} %multiply_reduce_fusion, f32[]{:T(128)} %multiply_reduce_fusion.1), channel_id=1, replica_groups=mesh['dp'=8,'row'=4,'col'=8] {'dp','row','col'}, use_global_device_ids=true, to_apply=%region_10.0 | all-reduce | flops 2 | bytes 16 | tf_op jit(solution)/shard_map/psum | solution.py:33
  296.5 2.8 divide_subtract_fusion
  299.3 2.5 copy.9
  301.9 0.0 copy-done.1
  301.9 0.0 copy-done.2
  (1 shorter events, 0.0 us)
Async XLA Ops:
  7.2 1.9 copy-start
  7.2 70.5 %reduce-scatter.2.cloned.1.call-start = ((), (), s32[]{:S(2)}) async-start(), calls=%async_computation.1 | async-start | bytes 9437184 | tf_op jit(solution)/shard_map/reduce_scatter | solution.py:21
  19.9 184.0 %copy-start.3 = (f32[1024]{0:T(1024)S(1)}, f32[1024]{0:T(1024)}, u32[]{:S(2)}) copy-start(f32[1024]{0:T(1024)} %param.8) | copy-start | bytes 12292
  19.9 195.7 %copy-start.4 = (f32[256]{0:T(256)S(1)}, f32[256]{0:T(256)}, u32[]{:S(2)}) copy-start(f32[256]{0:T(256)} %param.9) | copy-start | bytes 3076
  204.5 97.3 %copy-start.1 = (f32[1024]{0:T(1024)}, f32[1024]{0:T(1024)S(1)}, u32[]{:S(2)}) copy-start(f32[1024]{0:T(1024)S(1)} %get-tuple-element.13) | copy-start | bytes 12292
  215.6 86.3 %copy-start.2 = (f32[256]{0:T(256)}, f32[256]{0:T(256)S(1)}, u32[]{:S(2)}) copy-start(f32[256]{0:T(256)S(1)} %multiply_add_fusion.1) | copy-start | bytes 3076
Sparse Core Ops, SparseCore 0:
  20.0 57.5 reduce-scatter.1
where the time goes:
time: 310 us; the launch traced here: 309 us
  blocking collectives  210 us (68%)
  waiting for transfers between devices  55.6 us (18%)
  between operations  16.1 us (5%)
  matrix products  10.8 us (3%)
  other arithmetic  9.29 us (3%)
  local copies, waits for them, and re-layouts  6.92 us (2%)
    psum x1, blocking collectives, per_device(): row_total = lax.psum(row_part, ('dp', 'col'))  125 us
    psum x1, blocking collectives, per_device(): lax.psum((jnp.sum(update * update), jnp.sum(param * param)), ('dp', 'row'...  74 us
    reduce_scatter x1, waiting for transfers between devices, per_device(): lax.psum_scatter(contract_tokens(cotangent, activations), 'dp', scatter_d...  55.6 us
    psum x1, blocking collectives, per_device(): row_level = lax.psum(jnp.sum(new_row), 'row') / D  11 us
    dot_general x1, matrix products, contract_tokens(): lax.dot_general(left, right, (((0,), (0,)), ((), ())), preferred_element_...  10.8 us
    unnamed x12, local copies, waits for them, and re-layouts  6.92 us
  transfers between devices with their start and end apart: 1, of which 1 were waited for; matrix products, arithmetic and copies ran while one was open for 1% of the time, Pallas kernels for 0%

commit v1 on v0

v1 whole, which is shorter than its diff:
```python
import jax
import jax.numpy as jnp
from jax import lax
from jax.sharding import Mesh, PartitionSpec as P

D = 4096
FF = 16384

decay_rate = 0.9
step_size = 0.3

Y, C, X, Z = 4, 2, 4, 8
OWN = 256
HALF = 512
WIRE = jnp.float16

swap_core = [(0, 1), (1, 0)]
to_left = [(i, (i - 1) % Y) for i in range(Y)]
to_right = [(i, (i + 1) % Y) for i in range(Y)]
pair_near = [(i, i ^ 1) for i in range(X)]
pair_wrap = [(i, X - 1 - i) for i in range(X)]


def sum_over_x(value):
    value = value + lax.ppermute(value, "x", pair_near)
    return value + lax.ppermute(value, "x", pair_wrap)


def per_device(activations, cotangent, param, row_state, col_state):
    y = lax.axis_index("y")
    c = lax.axis_index("c")

    def partial(owner_y, owner_c):
        start = (lax.rem(owner_y + Y, Y) * C + owner_c) * OWN
        block = lax.dynamic_slice_in_dim(cotangent, start, OWN, axis=1)
        return lax.dot_general(
            activations, block, (((0,), (0,)), ((), ())), preferred_element_type=jnp.float32
        )

    def chip_sum(owner_y):
        away = partial(owner_y, 1 - c).astype(WIRE)
        came = lax.ppermute(away, "c", swap_core)
        return partial(owner_y, c) + came.astype(jnp.float32)

    far = chip_sum(y + 2).astype(WIRE)
    far_left = lax.ppermute(far[:HALF], "y", to_left)
    far_right = lax.ppermute(far[HALF:], "y", to_right)
    left = chip_sum(y - 1)
    right = chip_sum(y + 1)
    near_left = lax.ppermute(left[HALF:].astype(WIRE), "y", to_left)
    near_right = lax.ppermute(right[:HALF].astype(WIRE), "y", to_right)
    own = chip_sum(y)
    last_left = lax.ppermute((left[:HALF] + far_left).astype(WIRE), "y", to_left)
    last_right = lax.ppermute((right[HALF:] + far_right).astype(WIRE), "y", to_right)
    top = own[:HALF] + near_right.astype(jnp.float32) + last_left.astype(jnp.float32)
    low = own[HALF:] + near_left.astype(jnp.float32) + last_right.astype(jnp.float32)
    gradient = jnp.concatenate([top, low], axis=0)

    squares = gradient * gradient
    row_part = jnp.sum(squares, axis=1)
    col_part = jnp.sum(squares, axis=0)
    new_col = decay_rate * col_state + (1.0 - decay_rate) * sum_over_x(col_part) / D
    weighted = jnp.sum(squares * (1.0 / new_col)[None, :], axis=1)
    param_part = jnp.sum(param * param)
    packed = jnp.concatenate(
        [row_part.reshape(8, 128), weighted.reshape(8, 128), jnp.full((8, 128), param_part)]
    )
    packed = packed + lax.ppermute(packed, "c", swap_core)
    spread = jnp.broadcast_to(packed[None], (Y * Z,) + packed.shape)
    packed = jnp.sum(lax.all_to_all(spread, ("y", "z"), 0, 0, tiled=True), axis=0)
    row_total = packed[:8].reshape(1024)
    weighted_total = packed[8:16].reshape(1024)
    new_row = decay_rate * row_state + (1.0 - decay_rate) * row_total / FF
    sums = jnp.stack([jnp.sum(weighted_total / new_row), jnp.sum(new_row), packed[16, 0]])
    sums = sum_over_x(jnp.broadcast_to(sums[:, None], (3, 128)))
    row_level = sums[1, 0] / D
    entries = D * FF
    clip = jnp.maximum(1.0, jnp.sqrt(row_level * sums[0, 0] / entries))
    scale = jnp.sqrt(sums[2, 0] / entries)
    factor = step_size * scale * jnp.sqrt(row_level) / clip
    update = gradient * (factor * lax.rsqrt(new_row))[:, None] * lax.rsqrt(new_col)[None, :]
    return (param - update, new_row, new_col)


def solution(mesh):
    split = Mesh(mesh.devices.reshape(Y, C, X, Z), ("y", "c", "x", "z"))
    tokens = ("y", "c")
    columns = ("z", "y", "c")
    in_specs = (P(tokens, "x"), P(tokens, "z"), P("x", columns), P("x"), P(columns))
    out_specs = (P("x", columns), P("x"), P(columns))
    return jax.shard_map(
        per_device, mesh=split, in_specs=in_specs, out_specs=out_specs, check_vma=False
    )
```

time: 310 us -> 101 us (0.33)
  blocking collectives: 210 us -> 26.5 us
  waiting for transfers between devices: 55.6 us -> 15.2 us
  starting transfers between devices: 0.04 us -> 17.1 us
  between operations: 16.1 us -> 2.87 us
  matrix products: 10.8 us -> 20.9 us
    psum x3 -> x0, blocking collectives: 210 us -> none  [the longest x1 125 us: per_device(): row_total = lax.psum(row_part, ('dp', 'col'))]
    reduce_scatter x1 -> x0, waiting for transfers between devices: 55.6 us -> none  [per_device(): lax.psum_scatter(contract_tokens(cotangent, activations), 'dp', scatter_d...]
    all_to_all x0 -> x1, blocking collectives: none -> 26.5 us  [per_device(): lax.all_to_all(spread, ('y', 'z'), 0, 0, tiled=True)]
    ppermute x0 -> x15, starting transfers between devices: none -> 17.1 us  [the longest x2 5.5 us: sum_over_x(): return value + lax.ppermute(value, 'x', pair_wrap)]
    ppermute x0 -> x15, waiting for transfers between devices: none -> 15.2 us  [the longest x2 5.43 us: sum_over_x(): value = value + lax.ppermute(value, 'x', pair_near)]
    dot_general x1 -> x8, matrix products: 10.8 us -> 20.9 us  [partial(): lax.dot_general(activations, block, (((0,), (0,)), ((), ())), preferred_e...]
    reduce_sum x3 -> x4, other arithmetic: 5.03 us -> 1.73 us  [the longest x1 0.87 us: per_device(): param_part = jnp.sum(param * param)]
    unnamed x12 -> x16, local copies, waits for them, and re-layouts: 6.92 us -> 6.96 us
  transfers between devices with their start and end apart: 1 -> 15, of which waited for: 1 -> 8; matrix products, arithmetic and copies ran while one was open for 1% -> 23% of each run, Pallas kernels for 0% -> 0%
where the time goes in v1:
time: 101 us; the launch traced here: 100 us
  blocking collectives  26.5 us (26%)
  matrix products  20.9 us (21%)
  starting transfers between devices  17.1 us (17%)
  waiting for transfers between devices  15.2 us (15%)
  local copies, waits for them, and re-layouts  9.7 us (10%)
  other arithmetic  7.88 us (8%)
  between operations  2.87 us (3%)
    all_to_all x1, blocking collectives, per_device(): lax.all_to_all(spread, ('y', 'z'), 0, 0, tiled=True)  26.5 us
    dot_general x8, matrix products, partial(): lax.dot_general(activations, block, (((0,), (0,)), ((), ())), preferred_e...  20.9 us
    unnamed x16, local copies, waits for them, and re-layouts  6.96 us
    ppermute x2, starting transfers between devices, sum_over_x(): return value + lax.ppermute(value, 'x', pair_wrap)  5.5 us
    ppermute x2, waiting for transfers between devices, sum_over_x(): value = value + lax.ppermute(value, 'x', pair_near)  5.43 us
    ppermute x1, waiting for transfers between devices, per_device(): near_left = lax.ppermute(left[HALF:].astype(WIRE), 'y', to_left)  3.3 us
    ppermute x1, starting transfers between devices, per_device(): lax.ppermute((left[:HALF] + far_left).astype(WIRE), 'y', to_left)  3.01 us
    sub x1, other arithmetic, per_device(): return (param - update, new_row, new_col)  2.65 us
  transfers between devices with their start and end apart: 15, of which 8 were waited for; matrix products, arithmetic and copies ran while one was open for 23% of the time, Pallas kernels for 0%

profile of v1, /device:TPU:32, one launch (start us, length us, event | category | flops | bytes accessed | tf_op | source)
XLA Modules:
  0.0 100.0 jit_solution(16896736468459920603)
XLA Ops:
  0.7 1.9 %copy-done = bf16[1536,1024]{1,0:T(8,128)(2,1)S(1)} copy-done((bf16[1536,1024]{1,0:T(8,128)(2,1)S(1)}, bf16[1536,1024]{1,0:T(8,128)(2,1)}, u32[]{:S(2)}) %copy-start) | copy-done | bytes 3145752
  2.5 2.9 %fusion.3 = f16[1024,256]{0,1:T(8,128)(2,1)} fusion(bf16[1536,1024]{1,0:T(8,128)(2,1)S(1)} %copy-done, bf16[1536,2048]{1,0:T(8,128)(2,1)} %param.6, s32[]{:T(128)S(6)} %select_n.31), kind=kOutput, calls=%fused_computation.11 | convolution fusion | flops 805568512 | bytes 4456452 | tf_op jit(solution)/shard_map/dot_general | solution.py:36
  5.4 2.9 %fusion.1 = f16[1024,256]{0,1:T(8,128)(2,1)} fusion(bf16[1536,1024]{1,0:T(8,128)(2,1)S(1)} %copy-done, bf16[1536,2048]{1,0:T(8,128)(2,1)} %param.6, s32[]{:T(128)S(6)} %select_n.27), kind=kOutput, calls=%fused_computation.9 | convolution fusion | flops 805568512 | bytes 4456452 | tf_op jit(solution)/shard_map/dot_general | solution.py:36
  8.4 0.5 collective-permute-start.1
  8.9 2.9 %fusion.2 = f16[1024,256]{0,1:T(8,128)(2,1)} fusion(bf16[1536,1024]{1,0:T(8,128)(2,1)S(1)} %copy-done, bf16[1536,2048]{1,0:T(8,128)(2,1)} %param.6, s32[]{:T(128)S(6)} %select_n.29), kind=kOutput, calls=%fused_computation.10 | convolution fusion | flops 805568512 | bytes 4456452 | tf_op jit(solution)/shard_map/dot_general | solution.py:36
  11.8 2.9 %fusion = f16[1024,256]{0,1:T(8,128)(2,1)} fusion(bf16[1536,1024]{1,0:T(8,128)(2,1)S(1)} %copy-done, bf16[1536,2048]{1,0:T(8,128)(2,1)} %param.6, s32[]{:T(128)S(6)} %select_n.25), kind=kOutput, calls=%fused_computation.8 | convolution fusion | flops 805568512 | bytes 4456452 | tf_op jit(solution)/shard_map/dot_general | solution.py:36
  14.7 0.5 collective-permute-start
  15.3 2.3 %add_convert_fusion = f16[1024,256]{0,1:T(8,128)(2,1)S(1)} fusion(f16[1024,256]{0,1:T(8,128)(2,1)} %collective-permute-done.4, bf16[1536,1024]{1,0:T(8,128)(2,1)S(1)} %copy-done, bf16[1536,2048]{1,0:T(8,128)(2,1)} %param.6, s32[]{:T(128)S(6)} %select_n.30), kind=kOutput, calls=%fused_computation.16 | convolution fusion | flops 806092800 | bytes 4980740 | tf_op jit(solution)/shard_map/dot_general | solution.py:36
  17.6 0.1 fusion.38
  17.7 1.7 %collective-permute-start.8 = (f16[512,256]{0,1:T(8,128)(2,1)S(1)}, f16[512,256]{0,1:T(8,128)(2,1)S(1)}, u32[]{:S(2)}, u32[]{:S(2)}) collective-permute-start(f16[512,256]{0,1:T(8,128)(2,1)S(1)} %get-tuple-element.23), channel_id=1, source_target_pairs={{0,64},{64,128},{128,192},{192,0},{1,65},{65,129},{129,193},{193,1... | collective-permute-start | bytes 786440 | tf_op jit(solution)/shard_map/ppermute | solution.py:47
  19.3 1.7 %collective-permute-start.5 = (f16[512,256]{0,1:T(8,128)(2,1)S(1)}, f16[512,256]{0,1:T(8,128)(2,1)S(1)}, u32[]{:S(2)}, u32[]{:S(2)}) collective-permute-start(f16[512,256]{0,1:T(8,128)(2,1)S(1)} %get-tuple-element.22), channel_id=1, source_target_pairs={{0,192},{64,0},{128,64},{192,128},{1,193},{65,1},{129,65},{193,129... | collective-permute-start | bytes 786440 | tf_op jit(solution)/shard_map/ppermute | solution.py:46
  21.0 2.3 %convert_add_fusion.1 = f32[1024,256]{0,1:T(8,128)S(1)} fusion(f16[1024,256]{0,1:T(8,128)(2,1)} %collective-permute-done.1, bf16[1536,1024]{1,0:T(8,128)(2,1)S(1)} %copy-done, bf16[1536,2048]{1,0:T(8,128)(2,1)} %param.6, s32[]{:T(128)S(6)} %select_n.26), kind=kOutput, calls=%fused_computation.18 | convolution fusion | flops 805830656 | bytes 5505028 | tf_op jit(solution)/shard_map/dot_general | solution.py:36
  23.3 2.3 %convert_add_fusion = f32[1024,256]{0,1:T(8,128)S(1)} fusion(f16[1024,256]{0,1:T(8,128)(2,1)} %collective-permute-done.3, bf16[1536,1024]{1,0:T(8,128)(2,1)S(1)} %copy-done, bf16[1536,2048]{1,0:T(8,128)(2,1)} %param.6, s32[]{:T(128)S(6)} %select_n.28), kind=kOutput, calls=%fused_computation.17 | convolution fusion | flops 805830656 | bytes 5505028 | tf_op jit(solution)/shard_map/dot_general | solution.py:36
  25.6 1.6 %collective-permute-done.8 = f16[512,256]{0,1:T(8,128)(2,1)S(1)} collective-permute-done((f16[512,256]{0,1:T(8,128)(2,1)S(1)}, f16[512,256]{0,1:T(8,128)(2,1)S(1)}, u32[]{:S(2)}, u32[]{:S(2)}) %collective-permute-start.8) | collective-permute-done | bytes 262176 | tf_op jit(solution)/shard_map/ppermute | solution.py:47
  27.2 0.1 slice_convert_fusion.1
  27.4 0.4 collective-permute-start.2
  27.8 0.1 fusion.22
  27.9 3.0 %collective-permute-start.6 = (f16[512,256]{0,1:T(8,128)(2,1)S(1)}, f16[512,256]{0,1:T(8,128)(2,1)S(1)}, u32[]{:S(2)}, u32[]{:S(2)}) collective-permute-start(f16[512,256]{0,1:T(8,128)(2,1)S(1)} %get-tuple-element.20), channel_id=1, source_target_pairs={{0,192},{64,0},{128,64},{192,128},{1,193},{65,1},{129,65},{193,129... | collective-permute-start | bytes 786440 | tf_op jit(solution)/shard_map/ppermute | solution.py:53
  30.9 0.5 collective-permute-start.7
  31.4 1.5 %collective-permute-start.9 = (f16[512,256]{0,1:T(8,128)(2,1)S(1)}, f16[512,256]{0,1:T(8,128)(2,1)S(1)}, u32[]{:S(2)}, u32[]{:S(2)}) collective-permute-start(f16[512,256]{0,1:T(8,128)(2,1)S(1)} %get-tuple-element.19), channel_id=1, source_target_pairs={{0,64},{64,128},{128,192},{192,0},{1,65},{65,129},{129,193},{193,1... | collective-permute-start | bytes 786440 | tf_op jit(solution)/shard_map/ppermute | solution.py:54
  32.9 2.3 %convert_add_fusion.2 = f32[1024,256]{0,1:T(8,128)S(1)} fusion(f16[1024,256]{0,1:T(8,128)(2,1)} %collective-permute-done, bf16[1536,1024]{1,0:T(8,128)(2,1)S(1)} %copy-done, bf16[1536,2048]{1,0:T(8,128)(2,1)} %param.6, s32[]{:T(128)S(6)} %select_n.24), kind=kOutput, calls=%fused_computation.19 | convolution fusion | flops 805830656 | bytes 5505028 | tf_op jit(solution)/shard_map/dot_general | solution.py:36
  35.2 2.7 %collective-permute-done.2 = f16[512,256]{0,1:T(8,128)(2,1)S(1)} collective-permute-done((f16[512,256]{0,1:T(8,128)(2,1)S(1)}, f16[512,256]{0,1:T(8,128)(2,1)S(1)}, u32[]{:S(2)}, u32[]{:S(2)}) %collective-permute-start.2) | collective-permute-done | bytes 262176 | tf_op jit(solution)/shard_map/ppermute | solution.py:51
  37.9 3.3 %collective-permute-done.7 = f16[512,256]{0,1:T(8,128)(2,1)S(1)} collective-permute-done((f16[512,256]{0,1:T(8,128)(2,1)S(1)}, f16[512,256]{0,1:T(8,128)(2,1)S(1)}, u32[]{:S(2)}, u32[]{:S(2)}) %collective-permute-start.7) | collective-permute-done | bytes 262176 | tf_op jit(solution)/shard_map/ppermute | solution.py:50
  41.2 0.5 collective-permute-done.9
  41.7 0.2 fusion.23
  42.0 0.1 multiply_reduce_fusion.2
  42.1 1.5 %collective-permute-start.10 = (f32[256]{0:T(256)S(1)}, f32[256]{0:T(256)S(1)}, u32[]{:S(2)}, u32[]{:S(2)}) collective-permute-start(f32[256]{0:T(256)S(1)} %multiply_reduce_fusion.2), channel_id=1, source_target_pairs={{0,8},{8,0},{16,24},{24,16},{1,9},{9,1},{17,25},{25,17},{2,10},{10... | collective-permute-start | bytes 3080 | tf_op jit(solution)/shard_map/ppermute | solution.py:25
  43.7 2.1 %collective-permute-done.10 = f32[256]{0:T(256)S(1)} collective-permute-done((f32[256]{0:T(256)S(1)}, f32[256]{0:T(256)S(1)}, u32[]{:S(2)}, u32[]{:S(2)}) %collective-permute-start.10) | collective-permute-done | bytes 1056 | tf_op jit(solution)/shard_map/ppermute | solution.py:25
  45.8 2.8 %collective-permute-start.11 = (f32[256]{0:T(256)S(1)}, f32[256]{0:T(256)S(1)}, u32[]{:S(2)}, u32[]{:S(2)}) collective-permute-start(f32[256]{0:T(256)S(1)} %add.154), channel_id=1, source_target_pairs={{0,24},{8,16},{16,8},{24,0},{1,25},{9,17},{17,9},{25,1},{2,26},{10... | collective-permute-start | bytes 3080 | tf_op jit(solution)/shard_map/ppermute | solution.py:26
  48.5 0.9 multiply_reduce_fusion
  49.4 0.6 broadcast_in_dim.6
  50.1 0.1 pad.5.clone
  50.1 0.4 collective-permute-done.11
  50.6 0.6 broadcast_divide_fusion
  51.1 0.2 multiply_reduce_fusion.3
  51.4 1.2 %collective-permute-done.12 = f32[24,128]{1,0:T(8,128)S(1)} collective-permute-done((f32[24,128]{1,0:T(8,128)S(1)}, f32[24,128]{1,0:T(8,128)S(1)}, u32[]{:S(2)}, u32[]{:S(2)}) %collective-permute-start.12) | collective-permute-done | bytes 12320 | tf_op jit(solution)/shard_map/ppermute | solution.py:68
  52.7 26.5 %all_to_all.5 = f32[32,24,128]{2,1,0:T(8,128)S(1)} all-to-all(f32[32,24,128]{2,1,0:T(8,128)S(1)} %broadcast_in_dim.7), channel_id=1, replica_groups=mesh['y'=4,'c'=2,'x'=4,'z'=8] {'y','z'}, dimensions={0} | all-to-all | bytes 786432 | tf_op jit(solution)/shard_map/all_to_all | solution.py:70
  79.2 0.5 slice.68
  79.8 0.7 fusion.27
  80.4 2.0 %pad_maximum_fusion.1 = f32[3]{0:T(128)S(1)} fusion(f32[1]{0:T(128)} %bitcast.14, f32[1]{0:T(128)} %bitcast.13, f32[1]{0:T(128)} %bitcast.12), kind=kLoop, calls=%fused_computation.58 | loop fusion | flops 6 | bytes 24 | tf_op jit(solution)/shard_map/stack | solution.py:74
  82.5 0.3 collective-permute-start.13
  82.8 3.3 %collective-permute-done.13 = f32[3,128]{1,0:T(4,128)S(1)} collective-permute-done((f32[3,128]{1,0:T(4,128)S(1)}, f32[3,128]{1,0:T(4,128)S(1)}, u32[]{:S(2)}, u32[]{:S(2)}) %collective-permute-start.13) | collective-permute-done | bytes 1568 | tf_op jit(solution)/shard_map/ppermute | solution.py:25
  86.2 2.8 %collective-permute-start.14 = (f32[3,128]{1,0:T(4,128)S(1)}, f32[3,128]{1,0:T(4,128)S(1)}, u32[]{:S(2)}, u32[]{:S(2)}) collective-permute-start(f32[3,128]{1,0:T(4,128)S(1)} %broadcast_add_fusion), channel_id=1, source_target_pairs={{0,24},{8,16},{16,8},{24,0},{1,25},{9,17},{17,9},{25,1},{2,26},{10... | collective-permute-start | bytes 4616 | tf_op jit(solution)/shard_map/ppermute | solution.py:26
  88.9 2.5 %copy.10 = f32[1024,256]{0,1:T(8,128)} copy(f32[1024,256]{1,0:T(8,128)} %param.7) | data formatting | bytes 2097152 | tf_op args[2]
  91.4 0.7 rsqrt.7
  92.2 0.6 fusion.39
  94.9 2.7 %multiply_subtract_fusion = f32[1024,256]{0,1:T(8,128)} fusion(f32[1024,256]{0,1:T(8,128)} %copy.10, f32[256]{0:T(256)S(1)} %rsqrt.7, f32[1024]{0:T(1024)S(1)} %rsqrt_multiply_fusion, f32[512,256]{0,1:T(8,128)} %copy-done.2, f32[512,256]{0,1:T(8,128)} %copy-done.1), kind=kLoop, calls=%fused_computation.13 | loop fusion | flops 1048576 | bytes 3150848 | tf_op jit(solution)/shard_map/sub | solution.py:82
  97.5 2.5 %copy.11 = f32[1024,256]{1,0:T(8,128)} copy(f32[1024,256]{0,1:T(8,128)} %multiply_subtract_fusion) | data formatting | bytes 2097152
  (32 shorter events, 0.5 us)
Async XLA Ops:
  0.6 1.9 %copy-start = (bf16[1536,1024]{1,0:T(8,128)(2,1)S(1)}, bf16[1536,1024]{1,0:T(8,128)(2,1)}, u32[]{:S(2)}) copy-start(bf16[1536,1024]{1,0:T(8,128)(2,1)} %param.5) | copy-start | bytes 9437188
  5.4 9.8 %collective-permute-start.4 = (f16[1024,256]{0,1:T(8,128)(2,1)}, f16[1024,256]{0,1:T(8,128)(2,1)}, u32[]{:S(2)}, u32[]{:S(2)}) collective-permute-start(f16[1024,256]{0,1:T(8,128)(2,1)} %fusion.3), channel_id=1, source_target_pairs={{0,32},{32,0},{1,33},{33,1},{2,34},{34,2},{3,35},{35,3},{4,36},{36... | collective-permute-start | bytes 1572872 | tf_op jit(solution)/shard_map/ppermute | solution.py:42
  8.4 12.6 %collective-permute-start.1 = (f16[1024,256]{0,1:T(8,128)(2,1)}, f16[1024,256]{0,1:T(8,128)(2,1)}, u32[]{:S(2)}, u32[]{:S(2)}) collective-permute-start(f16[1024,256]{0,1:T(8,128)(2,1)} %fusion.1), channel_id=1, source_target_pairs={{0,32},{32,0},{1,33},{33,1},{2,34},{34,2},{3,35},{35,3},{4,36},{36... | collective-permute-start | bytes 1572872 | tf_op jit(solution)/shard_map/ppermute | solution.py:42
  11.8 11.5 %collective-permute-start.3 = (f16[1024,256]{0,1:T(8,128)(2,1)}, f16[1024,256]{0,1:T(8,128)(2,1)}, u32[]{:S(2)}, u32[]{:S(2)}) collective-permute-start(f16[1024,256]{0,1:T(8,128)(2,1)} %fusion.2), channel_id=1, source_target_pairs={{0,32},{32,0},{1,33},{33,1},{2,34},{34,2},{3,35},{35,3},{4,36},{36... | collective-permute-start | bytes 1572872 | tf_op jit(solution)/shard_map/ppermute | solution.py:42
  14.7 18.2 %collective-permute-start = (f16[1024,256]{0,1:T(8,128)(2,1)}, f16[1024,256]{0,1:T(8,128)(2,1)}, u32[]{:S(2)}, u32[]{:S(2)}) collective-permute-start(f16[1024,256]{0,1:T(8,128)(2,1)} %fusion), channel_id=1, source_target_pairs={{0,32},{32,0},{1,33},{33,1},{2,34},{34,2},{3,35},{35,3},{4,36},{36... | collective-permute-start | bytes 1572872 | tf_op jit(solution)/shard_map/ppermute | solution.py:42
  17.7 9.6 %collective-permute-start.8 = (f16[512,256]{0,1:T(8,128)(2,1)S(1)}, f16[512,256]{0,1:T(8,128)(2,1)S(1)}, u32[]{:S(2)}, u32[]{:S(2)}) collective-permute-start(f16[512,256]{0,1:T(8,128)(2,1)S(1)} %get-tuple-element.23), channel_id=1, source_target_pairs={{0,64},{64,128},{128,192},{192,0},{1,65},{65,129},{129,193},{193,1... | collective-permute-start | bytes 786440 | tf_op jit(solution)/shard_map/ppermute | solution.py:47
  19.3 8.4 %collective-permute-start.5 = (f16[512,256]{0,1:T(8,128)(2,1)S(1)}, f16[512,256]{0,1:T(8,128)(2,1)S(1)}, u32[]{:S(2)}, u32[]{:S(2)}) collective-permute-start(f16[512,256]{0,1:T(8,128)(2,1)S(1)} %get-tuple-element.22), channel_id=1, source_target_pairs={{0,192},{64,0},{128,64},{192,128},{1,193},{65,1},{129,65},{193,129... | collective-permute-start | bytes 786440 | tf_op jit(solution)/shard_map/ppermute | solution.py:46
  27.4 10.5 %collective-permute-start.2 = (f16[512,256]{0,1:T(8,128)(2,1)S(1)}, f16[512,256]{0,1:T(8,128)(2,1)S(1)}, u32[]{:S(2)}, u32[]{:S(2)}) collective-permute-start(f16[512,256]{0,1:T(8,128)(2,1)S(1)} %get-tuple-element.18), channel_id=1, source_target_pairs={{0,64},{64,128},{128,192},{192,0},{1,65},{65,129},{129,193},{193,1... | collective-permute-start | bytes 786440 | tf_op jit(solution)/shard_map/ppermute | solution.py:51
  27.9 10.0 %collective-permute-start.6 = (f16[512,256]{0,1:T(8,128)(2,1)S(1)}, f16[512,256]{0,1:T(8,128)(2,1)S(1)}, u32[]{:S(2)}, u32[]{:S(2)}) collective-permute-start(f16[512,256]{0,1:T(8,128)(2,1)S(1)} %get-tuple-element.20), channel_id=1, source_target_pairs={{0,192},{64,0},{128,64},{192,128},{1,193},{65,1},{129,65},{193,129... | collective-permute-start | bytes 786440 | tf_op jit(solution)/shard_map/ppermute | solution.py:53
  30.9 10.3 %collective-permute-start.7 = (f16[512,256]{0,1:T(8,128)(2,1)S(1)}, f16[512,256]{0,1:T(8,128)(2,1)S(1)}, u32[]{:S(2)}, u32[]{:S(2)}) collective-permute-start(f16[512,256]{0,1:T(8,128)(2,1)S(1)} %get-tuple-element.21), channel_id=1, source_target_pairs={{0,192},{64,0},{128,64},{192,128},{1,193},{65,1},{129,65},{193,129... | collective-permute-start | bytes 786440 | tf_op jit(solution)/shard_map/ppermute | solution.py:50
  31.4 10.3 %collective-permute-start.9 = (f16[512,256]{0,1:T(8,128)(2,1)S(1)}, f16[512,256]{0,1:T(8,128)(2,1)S(1)}, u32[]{:S(2)}, u32[]{:S(2)}) collective-permute-start(f16[512,256]{0,1:T(8,128)(2,1)S(1)} %get-tuple-element.19), channel_id=1, source_target_pairs={{0,64},{64,128},{128,192},{192,0},{1,65},{65,129},{129,193},{193,1... | collective-permute-start | bytes 786440 | tf_op jit(solution)/shard_map/ppermute | solution.py:54
  35.2 13.3 %copy-start.3 = (f32[1024,256]{1,0:T(8,128)S(1)}, f32[1024,256]{1,0:T(8,128)}, u32[]{:S(2)}) copy-start(f32[1024,256]{1,0:T(8,128)} %param.7) | copy-start | bytes 3145732
  35.2 15.3 %copy-start.6 = (f32[256]{0:T(256)S(1)}, f32[256]{0:T(256)}, u32[]{:S(2)}) copy-start(f32[256]{0:T(256)} %param.9) | copy-start | bytes 3076
  42.0 9.2 %copy-start.1 = (f32[512,256]{0,1:T(8,128)}, f32[512,256]{0,1:T(8,128)S(1)}, u32[]{:S(2)}) copy-start(f32[512,256]{0,1:T(8,128)S(1)} %get-tuple-element.16) | copy-start | bytes 1572868
  42.0 9.4 %copy-start.2 = (f32[512,256]{0,1:T(8,128)}, f32[512,256]{0,1:T(8,128)S(1)}, u32[]{:S(2)}) copy-start(f32[512,256]{0,1:T(8,128)S(1)} %get-tuple-element.17) | copy-start | bytes 1572868
  42.0 37.8 %copy-start.5 = (f32[1024]{0:T(1024)S(1)}, f32[1024]{0:T(1024)}, u32[]{:S(2)}) copy-start(f32[1024]{0:T(1024)} %param.8) | copy-start | bytes 12292
  42.1 3.6 %collective-permute-start.10 = (f32[256]{0:T(256)S(1)}, f32[256]{0:T(256)S(1)}, u32[]{:S(2)}, u32[]{:S(2)}) collective-permute-start(f32[256]{0:T(256)S(1)} %multiply_reduce_fusion.2), channel_id=1, source_target_pairs={{0,8},{8,0},{16,24},{24,16},{1,9},{9,1},{17,25},{25,17},{2,10},{10... | collective-permute-start | bytes 3080 | tf_op jit(solution)/shard_map/ppermute | solution.py:25
  45.8 4.8 %collective-permute-start.11 = (f32[256]{0:T(256)S(1)}, f32[256]{0:T(256)S(1)}, u32[]{:S(2)}, u32[]{:S(2)}) collective-permute-start(f32[256]{0:T(256)S(1)} %add.154), channel_id=1, source_target_pairs={{0,24},{8,16},{16,8},{24,0},{1,25},{9,17},{17,9},{25,1},{2,26},{10... | collective-permute-start | bytes 3080 | tf_op jit(solution)/shard_map/ppermute | solution.py:26
  51.4 1.2 %collective-permute-start.12 = (f32[24,128]{1,0:T(8,128)S(1)}, f32[24,128]{1,0:T(8,128)S(1)}, u32[]{:S(2)}, u32[]{:S(2)}) collective-permute-start(f32[24,128]{1,0:T(8,128)S(1)} %maximum_maximum_fusion), channel_id=1, source_target_pairs={{0,32},{32,0},{1,33},{33,1},{2,34},{34,2},{3,35},{35,3},{4,36},{36... | collective-permute-start | bytes 36872 | tf_op jit(solution)/shard_map/ppermute | solution.py:68
  80.4 19.6 %copy-start.4 = (f32[1024]{0:T(1024)}, f32[1024]{0:T(1024)S(1)}, u32[]{:S(2)}) copy-start(f32[1024]{0:T(1024)S(1)} %get-tuple-element.13) | copy-start | bytes 12292
  82.5 3.6 %collective-permute-start.13 = (f32[3,128]{1,0:T(4,128)S(1)}, f32[3,128]{1,0:T(4,128)S(1)}, u32[]{:S(2)}, u32[]{:S(2)}) collective-permute-start(f32[3,128]{1,0:T(4,128)S(1)} %broadcast_in_dim.8), channel_id=1, source_target_pairs={{0,8},{8,0},{16,24},{24,16},{1,9},{9,1},{17,25},{25,17},{2,10},{10... | collective-permute-start | bytes 4616 | tf_op jit(solution)/shard_map/ppermute | solution.py:25
  86.2 6.0 %collective-permute-start.14 = (f32[3,128]{1,0:T(4,128)S(1)}, f32[3,128]{1,0:T(4,128)S(1)}, u32[]{:S(2)}, u32[]{:S(2)}) collective-permute-start(f32[3,128]{1,0:T(4,128)S(1)} %broadcast_add_fusion), channel_id=1, source_target_pairs={{0,24},{8,16},{16,8},{24,0},{1,25},{9,17},{17,9},{25,1},{2,26},{10... | collective-permute-start | bytes 4616 | tf_op jit(solution)/shard_map/ppermute | solution.py:26

commit v2 on v0

v2 whole, which is shorter than its diff:
```python
import jax
import jax.numpy as jnp
from jax import lax
from jax.experimental import pallas as pl
from jax.experimental.pallas import tpu as pltpu
from jax.sharding import Mesh, PartitionSpec as P

D = 4096
FF = 16384
TOKENS = 12288

decay_rate = 0.9
step_size = 0.3

Y, C, X, Z = 4, 2, 4, 8
ROWS = D // X
OWN = FF // (Z * Y * C)
DEPTH = TOKENS // (Y * C)
HALF = ROWS // 2
LANES = 128
GROUPS = ROWS // LANES
SHARE = GROUPS // C
STEPS = 3
WIRE = jnp.float16
F32 = jnp.float32
BF16 = jnp.bfloat16
TILE = (8, LANES)

swap_core = [(0, 1), (1, 0)]
to_left = [(i, (i - 1) % Y) for i in range(Y)]
to_right = [(i, (i + 1) % Y) for i in range(Y)]
pair_near = [(i, i ^ 1) for i in range(X)]
pair_wrap = [(i, X - 1 - i) for i in range(X)]

VMEM = pl.BlockSpec(memory_space=pltpu.VMEM)
SMEM = pl.BlockSpec(memory_space=pltpu.SMEM)
LIMIT = 14 * 2**20


def call(kernel, name, outs, *operands, scalars=0, micros=1):
    return pl.pallas_call(
        kernel,
        name=name,
        in_specs=[SMEM] * scalars + [VMEM] * (len(operands) - scalars),
        out_specs=[VMEM] * len(outs),
        out_shape=[jax.ShapeDtypeStruct(shape, kind) for shape, kind in outs],
        compiler_params=pltpu.CompilerParams(vmem_limit_bytes=LIMIT),
        cost_estimate=pl.CostEstimate(
            flops=0, bytes_accessed=micros * 2 * 2**20, transcendentals=0
        ),
    )(*operands)


def matmul_kernel(place, activations, block, out):
    del place
    step = pl.program_id(0)
    depth = block.shape[0]
    rows = activations[pl.ds(pl.multiple_of(step * depth, depth), depth), :]
    product = lax.dot_general(
        rows, block[...], (((0,), (0,)), ((), ())), preferred_element_type=F32
    )

    @pl.when(step == 0)
    def first():
        out[...] = product

    @pl.when(step > 0)
    def later():
        out[...] += product


def block_matmul(place, activations, cotangent):
    return pl.pallas_call(
        matmul_kernel,
        name="block_matmul",
        grid_spec=pltpu.PrefetchScalarGridSpec(
            num_scalar_prefetch=1,
            grid=(STEPS,),
            in_specs=[VMEM, pl.BlockSpec((DEPTH // STEPS, OWN), lambda k, place: (k, place[0]))],
            out_specs=pl.BlockSpec((ROWS, OWN), lambda k, place: (0, 0)),
        ),
        out_shape=jax.ShapeDtypeStruct((ROWS, OWN), F32),
        compiler_params=pltpu.CompilerParams(vmem_limit_bytes=LIMIT),
        cost_estimate=pl.CostEstimate(
            flops=2 * DEPTH * ROWS * OWN, bytes_accessed=2 * DEPTH * OWN, transcendentals=0
        ),
    )(place, activations, cotangent)


def lane_sums(block):
    folded = block[:, :LANES] + block[:, LANES:]
    return jnp.sum(folded.T, axis=0, keepdims=True)


def square_sum_kernel(param, out):
    value = param[...]
    out[...] = jnp.full(TILE, jnp.sum(value * value))


def row_sums_kernel(core, top, low, col_a, col_b, col_state, param_sum, new_col, mine, away):
    col = decay_rate * col_state[...] + (1.0 - decay_rate) * (col_a[...] + col_b[...]) / D
    new_col[...] = col
    inverse = 1.0 / col
    first = core[0] == 0
    for group in range(SHARE):
        sums = []
        for part in (top, low):
            block = part[group * LANES : (group + 1) * LANES, :]
            squares = block * block
            sums.append((lane_sums(squares), lane_sums(squares * inverse)))
        for k in range(2):
            at = k * SHARE + group
            mine[at : at + 1, :] = jnp.where(first, sums[0][k], sums[1][k])
            away[at : at + 1, :] = jnp.where(first, sums[1][k], sums[0][k])
    mine[2 * SHARE :, :] = param_sum[...]
    away[2 * SHARE :, :] = param_sum[...]


def message_kernel(mine, came, out):
    packed = mine[...] + came[...]
    high = packed.astype(BF16)
    rest = (packed - high.astype(F32)).astype(BF16)
    pieces = [
        high[:SHARE],
        rest[:SHARE],
        high[SHARE : 2 * SHARE],
        high[2 * SHARE : 2 * SHARE + 2],
        rest[2 * SHARE : 2 * SHARE + 2],
    ]
    message = jnp.concatenate([piece.astype(F32) for piece in pieces], axis=0).astype(BF16)
    for k in range(Y * Z):
        out[k] = message


def reduce_kernel(core, came, row_state, out):
    total = jnp.sum(came[...].astype(F32), axis=0)
    squares = total[:SHARE] + total[SHARE : 2 * SHARE]
    weighted = total[2 * SHARE : 3 * SHARE]
    state = jnp.where(core[0] == 0, row_state[:SHARE, :], row_state[SHARE:, :])
    row = decay_rate * state + (1.0 - decay_rate) * squares / FF
    param_total = total[3 * SHARE : 3 * SHARE + 1] + total[3 * SHARE + 2 : 3 * SHARE + 3]
    out[:SHARE, :] = row
    out[SHARE : SHARE + 1, :] = jnp.full((1, LANES), jnp.sum(weighted / row))
    out[SHARE + 1 : SHARE + 2, :] = jnp.full((1, LANES), jnp.sum(row))
    out[SHARE + 2 :, :] = jnp.broadcast_to(0.5 * param_total, (2, LANES))


def merge_kernel(core, mine, twin, new_row, scalars):
    first = core[0] == 0
    a, b = mine[:SHARE, :], twin[:SHARE, :]
    new_row[:SHARE, :] = jnp.where(first, a, b)
    new_row[SHARE:, :] = jnp.where(first, b, a)
    scalars[...] = mine[...] + twin[...]


def normalise_kernel(top, low, new_row, new_col, update):
    col_factor = lax.rsqrt(new_col[...])
    row_factor = lax.rsqrt(new_row[...])
    for group in range(GROUPS):
        part = top if group < SHARE else low
        at = group % SHARE
        block = part[at * LANES : (at + 1) * LANES, :]
        along = jnp.broadcast_to(row_factor[group : group + 1, :], (LANES, LANES)).T
        factor = jnp.concatenate([along, along], axis=1) * col_factor
        update[group * LANES : (group + 1) * LANES, :] = block * factor


def step_kernel(scalars_a, scalars_b, param, update, new_param):
    sums = scalars_a[...] + scalars_b[...]
    entries = D * FF
    row_level = sums[SHARE + 1 : SHARE + 2] / D
    clip = jnp.maximum(1.0, jnp.sqrt(row_level * sums[SHARE : SHARE + 1] / entries))
    scale = jnp.sqrt(sums[SHARE + 2 : SHARE + 3] / entries)
    factor = step_size * scale * jnp.sqrt(row_level) / clip
    factor = jnp.concatenate([factor, factor], axis=1)
    new_param[...] = param[...] - factor * update[...]


def per_device(activations, cotangent, param, row_state, col_state):
    y = lax.axis_index("y")
    c = lax.axis_index("c")
    barrier = lax.optimization_barrier
    places = [
        ((lax.rem(y + hop, Y) * C) + core)[None] for hop in (2, 3, 1, 0) for core in (1 - c, c)
    ]
    *places, core = barrier((*places, c[None]))

    def partial(place):
        return block_matmul(place, activations, cotangent)

    def swapped(place):
        return lax.ppermute(partial(place), "c", swap_core)

    def wide(value):
        return value.astype(F32)

    far_came = swapped(places[0])
    far_own = partial(places[1])
    far_top = barrier((far_own[:HALF] + far_came[:HALF]).astype(WIRE))
    far_low = barrier((far_own[HALF:] + far_came[HALF:]).astype(WIRE))
    far_left = lax.ppermute(far_top, "y", to_left)
    far_right = lax.ppermute(far_low, "y", to_right)
    *places, _, _ = barrier((*places, far_top, far_low))
    left_came = swapped(places[2])
    right_came = swapped(places[4])
    left = partial(places[3])
    right = partial(places[5])
    near_low = barrier((left[HALF:] + left_came[HALF:]).astype(WIRE))
    near_top = barrier((right[:HALF] + right_came[:HALF]).astype(WIRE))
    near_left = lax.ppermute(near_low, "y", to_left)
    near_right = lax.ppermute(near_top, "y", to_right)
    *places, _, _ = barrier((*places, near_low, near_top))
    own_came = swapped(places[6])
    own = partial(places[7])
    last_top = (left[:HALF] + left_came[:HALF] + wide(far_left)).astype(WIRE)
    last_low = (right[HALF:] + right_came[HALF:] + wide(far_right)).astype(WIRE)
    last_left = lax.ppermute(barrier(last_top), "y", to_left)
    last_right = lax.ppermute(barrier(last_low), "y", to_right)
    top = own[:HALF] + own_came[:HALF] + wide(near_right) + wide(last_left)
    low = own[HALF:] + own_came[HALF:] + wide(near_left) + wide(last_right)

    (param_sum,) = call(square_sum_kernel, "square_sum", [(TILE, F32)], param)
    col_part = jnp.sum(top * top, axis=0) + jnp.sum(low * low, axis=0)
    col_part = col_part.reshape(1, OWN)
    col_part = col_part + lax.ppermute(col_part, "x", pair_near)
    col_came = lax.ppermute(col_part, "x", pair_wrap)
    new_col, mine, away = call(
        row_sums_kernel,
        "row_sums",
        [((1, OWN), F32), ((2 * 8, LANES), F32), ((2 * 8, LANES), F32)],
        core,
        top,
        low,
        col_part,
        col_came,
        col_state.reshape(1, OWN),
        param_sum,
        scalars=1,
    )
    came = lax.ppermute(away, "c", swap_core)
    (message,) = call(message_kernel, "message", [((Y * Z, 16, LANES), BF16)], mine, came)
    came = lax.all_to_all(message, ("y", "z"), 0, 0, tiled=True)
    (reduced,) = call(
        reduce_kernel,
        "row_reduce",
        [(TILE, F32)],
        core,
        came,
        row_state.reshape(TILE),
        scalars=1,
    )
    twin = lax.ppermute(reduced, "c", swap_core)
    new_row, scalars = call(
        merge_kernel, "merge", [(TILE, F32), (TILE, F32)], core, reduced, twin, scalars=1
    )
    scalars = scalars + lax.ppermute(scalars, "x", pair_near)
    scalars_came = lax.ppermute(scalars, "x", pair_wrap)
    (update,) = call(
        normalise_kernel, "normalise", [((ROWS, OWN), F32)], top, low, new_row, new_col
    )
    (new_param,) = call(
        step_kernel, "step", [((ROWS, OWN), F32)], scalars, scalars_came, param, update
    )
    return (new_param, new_row.reshape(ROWS), new_col.reshape(OWN))


def solution(mesh):
    split = Mesh(mesh.devices.reshape(Y, C, X, Z), ("y", "c", "x", "z"))
    tokens = ("y", "c")
    columns = ("z", "y", "c")
    in_specs = (P(tokens, "x"), P(tokens, "z"), P("x", columns), P("x"), P(columns))
    out_specs = (P("x", columns), P("x"), P(columns))
    return jax.shard_map(
        per_device, mesh=split, in_specs=in_specs, out_specs=out_specs, check_vma=False
    )
```

time: 310 us -> 87.4 us (0.28)
  blocking collectives: 210 us -> 18.6 us
  waiting for transfers between devices: 55.6 us -> 25 us
  Pallas kernels: 0 us -> 19.6 us
  starting transfers between devices: 0.04 us -> 15.5 us
  between operations: 16.1 us -> 0.85 us
  matrix products: 10.8 us -> 0 us
  other arithmetic: 9.29 us -> 0.79 us
    psum x3 -> x0, blocking collectives: 210 us -> none  [the longest x1 125 us: per_device(): row_total = lax.psum(row_part, ('dp', 'col'))]
    reduce_scatter x1 -> x0, waiting for transfers between devices: 55.6 us -> none  [per_device(): lax.psum_scatter(contract_tokens(cotangent, activations), 'dp', scatter_d...]
    ppermute x0 -> x16, waiting for transfers between devices: none -> 25 us  [the longest x1 4.75 us: per_device(): last_right = lax.ppermute(barrier(last_low), 'y', to_right)]
    pallas_call x0 -> x15, Pallas kernels: none -> 19.6 us  [the longest x8 16.3 us: block_matmul(): pl.pallas_call(matmul_kernel, name='block_matmul', grid_spec=pltpu.Prefet...]
    all_to_all x0 -> x1, blocking collectives: none -> 18.6 us  [per_device(): came = lax.all_to_all(message, ('y', 'z'), 0, 0, tiled=True)]
    ppermute x0 -> x16, starting transfers between devices: none -> 15.5 us  [the longest x1 3.02 us: per_device(): far_left = lax.ppermute(far_top, 'y', to_left)]
    dot_general x1 -> x0, matrix products: 10.8 us -> none  [contract_tokens(): lax.dot_general(left, right, (((0,), (0,)), ((), ())), preferred_element_...]
    reduce_sum x4 -> x1, other arithmetic: 6.44 us -> 0.25 us  [per_device(): col_part = jnp.sum(top * top, axis=0) + jnp.sum(low * low, axis=0)]
  transfers between devices with their start and end apart: 1 -> 16, of which waited for: 1 -> 12; matrix products, arithmetic and copies ran while one was open for 1% -> 0% of each run, Pallas kernels for 0% -> 12%
where the time goes in v2:
time: 87.4 us; the launch traced here: 86.4 us
  waiting for transfers between devices  25 us (29%)
  Pallas kernels  19.6 us (22%)
  blocking collectives  18.6 us (21%)
  starting transfers between devices  15.5 us (18%)
  local copies, waits for them, and re-layouts  6.07 us (7%)
    all_to_all x1, blocking collectives, per_device(): came = lax.all_to_all(message, ('y', 'z'), 0, 0, tiled=True)  18.6 us
    pallas_call x8, Pallas kernels, block_matmul(): pl.pallas_call(matmul_kernel, name='block_matmul', grid_spec=pltpu.Prefet...  16.3 us
    unnamed x20, local copies, waits for them, and re-layouts  6.07 us
    ppermute x1, waiting for transfers between devices, per_device(): last_right = lax.ppermute(barrier(last_low), 'y', to_right)  4.75 us
    ppermute x1, waiting for transfers between devices, per_device(): last_left = lax.ppermute(barrier(last_top), 'y', to_left)  3.4 us
    ppermute x1, waiting for transfers between devices, per_device(): scalars = scalars + lax.ppermute(scalars, 'x', pair_near)  3.33 us
    pallas_call x7, Pallas kernels, call(): pl.pallas_call(kernel, name=name, in_specs=[SMEM] * scalars + [VMEM] * (l...  3.32 us
    ppermute x1, waiting for transfers between devices, per_device(): far_right = lax.ppermute(far_low, 'y', to_right)  3.22 us
  transfers between devices with their start and end apart: 16, of which 12 were waited for; matrix products, arithmetic and copies ran while one was open for 0% of the time, Pallas kernels for 12%

profile of v2, /device:TPU:32, one launch (start us, length us, event | category | flops | bytes accessed | tf_op | source)
XLA Modules:
  0.0 86.4 jit_solution(11023077593980058297)
XLA Ops:
  0.7 2.8 %copy-done = bf16[1536,2048]{1,0:T(8,128)(2,1)S(1)} copy-done((bf16[1536,2048]{1,0:T(8,128)(2,1)S(1)}, bf16[1536,2048]{1,0:T(8,128)(2,1)}, u32[]{:S(2)}) %copy-start) | copy-done | bytes 6291480
  3.4 1.9 %copy-done.1 = bf16[1536,1024]{1,0:T(8,128)(2,1)S(1)} copy-done((bf16[1536,1024]{1,0:T(8,128)(2,1)S(1)}, bf16[1536,1024]{1,0:T(8,128)(2,1)}, u32[]{:S(2)}) %copy-start.1) | copy-done | bytes 3145752
  5.3 2.0 %block_matmul.9 = f32[1024,256]{1,0:T(8,128)S(1)} custom-call(s32[1]{0:T(128)} %bitcast.place, bf16[1536,1024]{1,0:T(8,128)(2,1)S(1)} %copy-done.1, bf16[1536,2048]{1,0:T(8,128)(2,1)S(1)} %copy-done), custom_call_target="tpu_custom_call" | custom-call | flops 805306368 | bytes 786432 | tf_op jit(solution)/shard_map/block_matmul/pallas_call | solution.py:73
  7.5 2.0 %block_matmul.8 = f32[1024,256]{1,0:T(8,128)S(1)} custom-call(s32[1]{0:T(128)} %bitcast.1.place, bf16[1536,1024]{1,0:T(8,128)(2,1)S(1)} %copy-done.1, bf16[1536,2048]{1,0:T(8,128)(2,1)S(1)} %copy-done), custom_call_target="tpu_custom_call" | custom-call | flops 805306368 | bytes 786432 | tf_op jit(solution)/shard_map/block_matmul/pallas_call | solution.py:73
  9.5 0.6 collective-permute-done
  10.1 0.2 fusion.10
  10.3 2.1 %block_matmul.11 = f32[1024,256]{1,0:T(8,128)S(1)} custom-call(s32[1]{0:T(128)} %bitcast.2.place, bf16[1536,1024]{1,0:T(8,128)(2,1)S(1)} %copy-done.2, bf16[1536,2048]{1,0:T(8,128)(2,1)S(1)} %copy-done), custom_call_target="tpu_custom_call" | custom-call | flops 805306368 | bytes 786432 | tf_op jit(solution)/shard_map/block_matmul/pallas_call | solution.py:73
  12.4 0.2 collective-permute-start.1
  12.6 2.0 %block_matmul.13 = f32[1024,256]{1,0:T(8,128)S(1)} custom-call(s32[1]{0:T(128)} %bitcast.4.place, bf16[1536,1024]{1,0:T(8,128)(2,1)S(1)} %copy-done.2, bf16[1536,2048]{1,0:T(8,128)(2,1)S(1)} %bitcast.15), custom_call_target="tpu_custom_call" | custom-call | flops 805306368 | bytes 786432 | tf_op jit(solution)/shard_map/block_matmul/pallas_call | solution.py:73
  14.6 0.5 collective-permute-start.2
  15.1 3.0 %collective-permute-start.5 = (f16[512,256]{1,0:T(8,128)(2,1)S(1)}, f16[512,256]{1,0:T(8,128)(2,1)S(1)}, u32[]{:S(2)}, u32[]{:S(2)}) collective-permute-start(f16[512,256]{1,0:T(8,128)(2,1)S(1)} %get-tuple-element.58), channel_id=1, source_target_pairs={{0,192},{64,0},{128,64},{192,128},{1,193},{65,1},{129,65},{193,129... | collective-permute-start | bytes 786440 | tf_op jit(solution)/shard_map/ppermute | solution.py:201
  18.1 2.0 %block_matmul.12 = f32[1024,256]{1,0:T(8,128)S(1)} custom-call(s32[1]{0:T(128)} %bitcast.5.place, bf16[1536,1024]{1,0:T(8,128)(2,1)S(1)} %copy-done.2, bf16[1536,2048]{1,0:T(8,128)(2,1)S(1)} %bitcast.15), custom_call_target="tpu_custom_call" | custom-call | flops 805306368 | bytes 786432 | tf_op jit(solution)/shard_map/block_matmul/pallas_call | solution.py:73
  20.1 2.1 %block_matmul.10 = f32[1024,256]{1,0:T(8,128)S(1)} custom-call(s32[1]{0:T(128)} %bitcast.3.place, bf16[1536,1024]{1,0:T(8,128)(2,1)S(1)} %copy-done.2, bf16[1536,2048]{1,0:T(8,128)(2,1)S(1)} %bitcast.15), custom_call_target="tpu_custom_call" | custom-call | flops 805306368 | bytes 786432 | tf_op jit(solution)/shard_map/block_matmul/pallas_call | solution.py:73
  22.2 1.8 %collective-permute-done.5 = f16[512,256]{1,0:T(8,128)(2,1)S(1)} collective-permute-done((f16[512,256]{1,0:T(8,128)(2,1)S(1)}, f16[512,256]{1,0:T(8,128)(2,1)S(1)}, u32[]{:S(2)}, u32[]{:S(2)}) %collective-permute-start.5) | collective-permute-done | bytes 262176 | tf_op jit(solution)/shard_map/ppermute | solution.py:201
  23.9 0.2 fusion.9
  24.1 3.2 %collective-permute-done.8 = f16[512,256]{1,0:T(8,128)(2,1)S(1)} collective-permute-done((f16[512,256]{1,0:T(8,128)(2,1)S(1)}, f16[512,256]{1,0:T(8,128)(2,1)S(1)}, u32[]{:S(2)}, u32[]{:S(2)}) %collective-permute-start.8) | collective-permute-done | bytes 262176 | tf_op jit(solution)/shard_map/ppermute | solution.py:202
  27.4 0.2 fusion.1
  27.5 2.1 %block_matmul.15 = f32[1024,256]{1,0:T(8,128)S(1)} custom-call(s32[1]{0:T(128)} %bitcast.6.place, bf16[1536,1024]{1,0:T(8,128)(2,1)S(1)} %copy-done.2, bf16[1536,2048]{1,0:T(8,128)(2,1)S(1)} %bitcast.15), custom_call_target="tpu_custom_call" | custom-call | flops 805306368 | bytes 786432 | tf_op jit(solution)/shard_map/block_matmul/pallas_call | solution.py:73
  29.6 0.1 collective-permute-start.3
  29.7 0.6 collective-permute-start.7
  30.3 1.5 %collective-permute-start.9 = (f16[512,256]{1,0:T(8,128)(2,1)S(1)}, f16[512,256]{1,0:T(8,128)(2,1)S(1)}, u32[]{:S(2)}, u32[]{:S(2)}) collective-permute-start(f16[512,256]{1,0:T(8,128)(2,1)S(1)} %get-tuple-element.53), channel_id=1, source_target_pairs={{0,64},{64,128},{128,192},{192,0},{1,65},{65,129},{129,193},{193,1... | collective-permute-start | bytes 786440 | tf_op jit(solution)/shard_map/ppermute | solution.py:218
  31.8 1.7 %collective-permute-start.6 = (f16[512,256]{1,0:T(8,128)(2,1)S(1)}, f16[512,256]{1,0:T(8,128)(2,1)S(1)}, u32[]{:S(2)}, u32[]{:S(2)}) collective-permute-start(f16[512,256]{1,0:T(8,128)(2,1)S(1)} %get-tuple-element.56), channel_id=1, source_target_pairs={{0,192},{64,0},{128,64},{192,128},{1,193},{65,1},{129,65},{193,129... | collective-permute-start | bytes 786440 | tf_op jit(solution)/shard_map/ppermute | solution.py:217
  33.5 0.3 collective-permute-start.4
  33.8 2.0 %block_matmul.14 = f32[1024,256]{1,0:T(8,128)S(1)} custom-call(s32[1]{0:T(128)} %bitcast.7.place, bf16[1536,1024]{1,0:T(8,128)(2,1)S(1)} %copy-done.2, bf16[1536,2048]{1,0:T(8,128)(2,1)S(1)} %bitcast.15), custom_call_target="tpu_custom_call" | custom-call | flops 805306368 | bytes 786432 | tf_op jit(solution)/shard_map/block_matmul/pallas_call | solution.py:73
  35.9 4.7 %collective-permute-done.9 = f16[512,256]{1,0:T(8,128)(2,1)S(1)} collective-permute-done((f16[512,256]{1,0:T(8,128)(2,1)S(1)}, f16[512,256]{1,0:T(8,128)(2,1)S(1)}, u32[]{:S(2)}, u32[]{:S(2)}) %collective-permute-start.9) | collective-permute-done | bytes 262176 | tf_op jit(solution)/shard_map/ppermute | solution.py:218
  40.6 3.4 %collective-permute-done.6 = f16[512,256]{1,0:T(8,128)(2,1)S(1)} collective-permute-done((f16[512,256]{1,0:T(8,128)(2,1)S(1)}, f16[512,256]{1,0:T(8,128)(2,1)S(1)}, u32[]{:S(2)}, u32[]{:S(2)}) %collective-permute-start.6) | collective-permute-done | bytes 262176 | tf_op jit(solution)/shard_map/ppermute | solution.py:217
  44.0 1.4 %collective-permute-done.4 = f16[512,256]{1,0:T(8,128)(2,1)S(1)} collective-permute-done((f16[512,256]{1,0:T(8,128)(2,1)S(1)}, f16[512,256]{1,0:T(8,128)(2,1)S(1)}, u32[]{:S(2)}, u32[]{:S(2)}) %collective-permute-start.4) | collective-permute-done | bytes 262176 | tf_op jit(solution)/shard_map/ppermute | solution.py:211
  45.5 0.3 multiply_reduce_fusion
  45.7 1.6 %collective-permute-start.10 = (f32[1,256]{1,0:T(1,128)S(1)}, f32[1,256]{1,0:T(1,128)S(1)}, u32[]{:S(2)}, u32[]{:S(2)}) collective-permute-start(f32[1,256]{1,0:T(1,128)S(1)} %bitcast.20), channel_id=1, source_target_pairs={{0,8},{8,0},{16,24},{24,16},{1,9},{9,1},{17,25},{25,17},{2,10},{10... | collective-permute-start | bytes 3080 | tf_op jit(solution)/shard_map/ppermute | solution.py:225
  47.3 2.1 %collective-permute-done.10 = f32[1,256]{1,0:T(1,128)S(1)} collective-permute-done((f32[1,256]{1,0:T(1,128)S(1)}, f32[1,256]{1,0:T(1,128)S(1)}, u32[]{:S(2)}, u32[]{:S(2)}) %collective-permute-start.10) | collective-permute-done | bytes 1056 | tf_op jit(solution)/shard_map/ppermute | solution.py:225
  49.4 2.7 %collective-permute-start.11 = (f32[1,256]{1,0:T(1,128)S(1)}, f32[1,256]{1,0:T(1,128)S(1)}, u32[]{:S(2)}, u32[]{:S(2)}) collective-permute-start(f32[1,256]{1,0:T(1,128)S(1)} %add.124.col_a), channel_id=1, source_target_pairs={{0,24},{8,16},{16,8},{24,0},{1,25},{9,17},{17,9},{25,1},{2,26},{10... | collective-permute-start | bytes 3080 | tf_op jit(solution)/shard_map/ppermute | solution.py:226
  52.1 0.4 square_sum.1.param_sum
  52.5 1.6 %collective-permute-done.11.col_b = f32[1,256]{1,0:T(1,128)S(1)} collective-permute-done((f32[1,256]{1,0:T(1,128)S(1)}, f32[1,256]{1,0:T(1,128)S(1)}, u32[]{:S(2)}, u32[]{:S(2)}) %collective-permute-start.11) | collective-permute-done | bytes 1056 | tf_op jit(solution)/shard_map/ppermute | solution.py:226
  54.2 0.8 row_sums.1
  55.0 1.2 %collective-permute-done.12.came = f32[16,128]{1,0:T(8,128)S(1)} collective-permute-done((f32[16,128]{1,0:T(8,128)S(1)}, f32[16,128]{1,0:T(8,128)S(1)}, u32[]{:S(2)}, u32[]{:S(2)}) %collective-permute-start.12) | collective-permute-done | bytes 8224 | tf_op jit(solution)/shard_map/ppermute | solution.py:240
  56.2 18.6 %all_to_all.5.came = bf16[32,16,128]{2,1,0:T(8,128)(2,1)S(1)} all-to-all(bf16[32,16,128]{2,1,0:T(8,128)(2,1)S(1)} %message.1), channel_id=1, replica_groups=mesh['y'=4,'c'=2,'x'=4,'z'=8] {'y','z'}, dimensions={0} | all-to-all | bytes 262144 | tf_op jit(solution)/shard_map/all_to_all | solution.py:242
  74.8 0.2 row_reduce.1.mine
  75.0 0.1 collective-permute-start.13
  75.1 1.2 %collective-permute-done.13.twin = f32[8,128]{1,0:T(8,128)S(1)} collective-permute-done((f32[8,128]{1,0:T(8,128)S(1)}, f32[8,128]{1,0:T(8,128)S(1)}, u32[]{:S(2)}, u32[]{:S(2)}) %collective-permute-start.13) | collective-permute-done | bytes 4128 | tf_op jit(solution)/shard_map/ppermute | solution.py:252
  76.3 0.6 merge.1
  76.9 0.3 collective-permute-start.14
  77.1 3.3 %collective-permute-done.14 = f32[8,128]{1,0:T(8,128)S(1)} collective-permute-done((f32[8,128]{1,0:T(8,128)S(1)}, f32[8,128]{1,0:T(8,128)S(1)}, u32[]{:S(2)}, u32[]{:S(2)}) %collective-permute-start.14) | collective-permute-done | bytes 4128 | tf_op jit(solution)/shard_map/ppermute | solution.py:256
  80.5 2.8 %collective-permute-start.15 = (f32[8,128]{1,0:T(8,128)S(1)}, f32[8,128]{1,0:T(8,128)S(1)}, u32[]{:S(2)}, u32[]{:S(2)}) collective-permute-start(f32[8,128]{1,0:T(8,128)S(1)} %add.125.scalars_a), channel_id=1, source_target_pairs={{0,24},{8,16},{16,8},{24,0},{1,25},{9,17},{17,9},{25,1},{2,26},{10... | collective-permute-start | bytes 12296 | tf_op jit(solution)/shard_map/ppermute | solution.py:257
  83.2 0.7 copy-done.4
  83.9 0.7 copy-done.7
  84.6 0.2 normalise.1.update
  84.8 0.5 collective-permute-done.15.scalars_b
  85.3 1.1 %step.1 = f32[1024,256]{1,0:T(8,128)} custom-call(f32[8,128]{1,0:T(8,128)S(1)} %add.125.scalars_a, f32[8,128]{1,0:T(8,128)S(1)} %collective-permute-done.15.scalars_b, f32[1024,256]{1,0:T(8,128)S(1)} %copy-done.3, f32[1024,256]{1,0:T(8,128)S(1)} %normalise.1.update), custom_call_target="tpu_custom_call" | custom-call | bytes 2097152 | tf_op jit(solution)/shard_map/step/pallas_call | solution.py:41
  (28 shorter events, 0.2 us)
Async XLA Ops:
  0.6 2.8 %copy-start = (bf16[1536,2048]{1,0:T(8,128)(2,1)S(1)}, bf16[1536,2048]{1,0:T(8,128)(2,1)}, u32[]{:S(2)}) copy-start(bf16[1536,2048]{1,0:T(8,128)(2,1)} %block.15) | copy-start | bytes 18874372
  3.4 1.9 %copy-start.1 = (bf16[1536,1024]{1,0:T(8,128)(2,1)S(1)}, bf16[1536,1024]{1,0:T(8,128)(2,1)}, u32[]{:S(2)}) copy-start(bf16[1536,1024]{1,0:T(8,128)(2,1)} %activations.15) | copy-start | bytes 9437188
  7.3 2.9 %copy-start.2 = (bf16[1536,1024]{1,0:T(8,128)(2,1)S(1)}, bf16[1536,1024]{1,0:T(8,128)(2,1)}, u32[]{:S(2)}) copy-start(bf16[1536,1024]{1,0:T(8,128)(2,1)} %activations.15) | copy-start | bytes 9437188
  7.4 2.7 %collective-permute-start = (f32[1024,256]{1,0:T(8,128)S(1)}, f32[1024,256]{1,0:T(8,128)S(1)}, u32[]{:S(2)}, u32[]{:S(2)}) collective-permute-start(f32[1024,256]{1,0:T(8,128)S(1)} %block_matmul.9), channel_id=1, source_target_pairs={{0,32},{32,0},{1,33},{33,1},{2,34},{34,2},{3,35},{35,3},{4,36},{36... | collective-permute-start | bytes 3145736 | tf_op jit(solution)/shard_map/ppermute | solution.py:192
  9.5 3.1 %slice-start = ((s8[6291456]{0:T(1024)(128)(4,1)}), s8[4194304]{0:T(1024)(128)(4,1)S(1)}, s32[]{:S(2)}) async-start(s8[6291456]{0:T(1024)(128)(4,1)} %bitcast.14), calls=%async_computation.1 | async-start | bytes 8388608
  10.3 2.3 %slice-start.1 = ((s8[6291456]{0:T(1024)(128)(4,1)}), s8[2097152]{0:T(1024)(128)(4,1)S(1)}, s32[]{:S(2)}) async-start(s8[6291456]{0:T(1024)(128)(4,1)} %bitcast.14), calls=%async_computation.2 | async-start | bytes 4194304
  12.4 11.6 %collective-permute-start.1 = (f32[1024,256]{1,0:T(8,128)S(1)}, f32[1024,256]{1,0:T(8,128)S(1)}, u32[]{:S(2)}, u32[]{:S(2)}) collective-permute-start(f32[1024,256]{1,0:T(8,128)S(1)} %block_matmul.11), channel_id=1, source_target_pairs={{0,32},{32,0},{1,33},{33,1},{2,34},{34,2},{3,35},{35,3},{4,36},{36... | collective-permute-start | bytes 3145736 | tf_op jit(solution)/shard_map/ppermute | solution.py:192
  14.6 12.8 %collective-permute-start.2 = (f32[1024,256]{1,0:T(8,128)S(1)}, f32[1024,256]{1,0:T(8,128)S(1)}, u32[]{:S(2)}, u32[]{:S(2)}) collective-permute-start(f32[1024,256]{1,0:T(8,128)S(1)} %block_matmul.13), channel_id=1, source_target_pairs={{0,32},{32,0},{1,33},{33,1},{2,34},{34,2},{3,35},{35,3},{4,36},{36... | collective-permute-start | bytes 3145736 | tf_op jit(solution)/shard_map/ppermute | solution.py:192
  15.1 8.9 %collective-permute-start.5 = (f16[512,256]{1,0:T(8,128)(2,1)S(1)}, f16[512,256]{1,0:T(8,128)(2,1)S(1)}, u32[]{:S(2)}, u32[]{:S(2)}) collective-permute-start(f16[512,256]{1,0:T(8,128)(2,1)S(1)} %get-tuple-element.58), channel_id=1, source_target_pairs={{0,192},{64,0},{128,64},{192,128},{1,193},{65,1},{129,65},{193,129... | collective-permute-start | bytes 786440 | tf_op jit(solution)/shard_map/ppermute | solution.py:201
  18.1 9.3 %collective-permute-start.8 = (f16[512,256]{1,0:T(8,128)(2,1)S(1)}, f16[512,256]{1,0:T(8,128)(2,1)S(1)}, u32[]{:S(2)}, u32[]{:S(2)}) collective-permute-start(f16[512,256]{1,0:T(8,128)(2,1)S(1)} %get-tuple-element.57), channel_id=1, source_target_pairs={{0,64},{64,128},{128,192},{192,0},{1,65},{65,129},{129,193},{193,1... | collective-permute-start | bytes 786440 | tf_op jit(solution)/shard_map/ppermute | solution.py:202
  29.6 15.9 %collective-permute-start.3 = (f32[1024,256]{1,0:T(8,128)S(1)}, f32[1024,256]{1,0:T(8,128)S(1)}, u32[]{:S(2)}, u32[]{:S(2)}) collective-permute-start(f32[1024,256]{1,0:T(8,128)S(1)} %block_matmul.15), channel_id=1, source_target_pairs={{0,32},{32,0},{1,33},{33,1},{2,34},{34,2},{3,35},{35,3},{4,36},{36... | collective-permute-start | bytes 3145736 | tf_op jit(solution)/shard_map/ppermute | solution.py:192
  29.7 10.9 %collective-permute-start.7 = (f16[512,256]{1,0:T(8,128)(2,1)S(1)}, f16[512,256]{1,0:T(8,128)(2,1)S(1)}, u32[]{:S(2)}, u32[]{:S(2)}) collective-permute-start(f16[512,256]{1,0:T(8,128)(2,1)S(1)} %get-tuple-element.55), channel_id=1, source_target_pairs={{0,192},{64,0},{128,64},{192,128},{1,193},{65,1},{129,65},{193,129... | collective-permute-start | bytes 786440 | tf_op jit(solution)/shard_map/ppermute | solution.py:210
  30.3 10.4 %collective-permute-start.9 = (f16[512,256]{1,0:T(8,128)(2,1)S(1)}, f16[512,256]{1,0:T(8,128)(2,1)S(1)}, u32[]{:S(2)}, u32[]{:S(2)}) collective-permute-start(f16[512,256]{1,0:T(8,128)(2,1)S(1)} %get-tuple-element.53), channel_id=1, source_target_pairs={{0,64},{64,128},{128,192},{192,0},{1,65},{65,129},{129,193},{193,1... | collective-permute-start | bytes 786440 | tf_op jit(solution)/shard_map/ppermute | solution.py:218
  31.8 20.3 %copy-start.3 = (f32[1024,256]{1,0:T(8,128)S(1)}, f32[1024,256]{1,0:T(8,128)}, u32[]{:S(2)}) copy-start(f32[1024,256]{1,0:T(8,128)} %param.13) | copy-start | bytes 3145732
  31.8 22.4 %copy-start.6 = (f32[256]{0:T(256)S(1)}, f32[256]{0:T(256)}, u32[]{:S(2)}) copy-start(f32[256]{0:T(256)} %param.11) | copy-start | bytes 3076
  31.8 43.0 %copy-start.5 = (f32[1024]{0:T(1024)S(1)}, f32[1024]{0:T(1024)}, u32[]{:S(2)}) copy-start(f32[1024]{0:T(1024)} %param.10) | copy-start | bytes 12292
  31.8 12.2 %collective-permute-start.6 = (f16[512,256]{1,0:T(8,128)(2,1)S(1)}, f16[512,256]{1,0:T(8,128)(2,1)S(1)}, u32[]{:S(2)}, u32[]{:S(2)}) collective-permute-start(f16[512,256]{1,0:T(8,128)(2,1)S(1)} %get-tuple-element.56), channel_id=1, source_target_pairs={{0,192},{64,0},{128,64},{192,128},{1,193},{65,1},{129,65},{193,129... | collective-permute-start | bytes 786440 | tf_op jit(solution)/shard_map/ppermute | solution.py:217
  33.5 11.9 %collective-permute-start.4 = (f16[512,256]{1,0:T(8,128)(2,1)S(1)}, f16[512,256]{1,0:T(8,128)(2,1)S(1)}, u32[]{:S(2)}, u32[]{:S(2)}) collective-permute-start(f16[512,256]{1,0:T(8,128)(2,1)S(1)} %get-tuple-element.54), channel_id=1, source_target_pairs={{0,64},{64,128},{128,192},{192,0},{1,65},{65,129},{129,193},{193,1... | collective-permute-start | bytes 786440 | tf_op jit(solution)/shard_map/ppermute | solution.py:211
  45.7 3.7 %collective-permute-start.10 = (f32[1,256]{1,0:T(1,128)S(1)}, f32[1,256]{1,0:T(1,128)S(1)}, u32[]{:S(2)}, u32[]{:S(2)}) collective-permute-start(f32[1,256]{1,0:T(1,128)S(1)} %bitcast.20), channel_id=1, source_target_pairs={{0,8},{8,0},{16,24},{24,16},{1,9},{9,1},{17,25},{25,17},{2,10},{10... | collective-permute-start | bytes 3080 | tf_op jit(solution)/shard_map/ppermute | solution.py:225
  49.4 4.8 %collective-permute-start.11 = (f32[1,256]{1,0:T(1,128)S(1)}, f32[1,256]{1,0:T(1,128)S(1)}, u32[]{:S(2)}, u32[]{:S(2)}) collective-permute-start(f32[1,256]{1,0:T(1,128)S(1)} %add.124.col_a), channel_id=1, source_target_pairs={{0,24},{8,16},{16,8},{24,0},{1,25},{9,17},{17,9},{25,1},{2,26},{10... | collective-permute-start | bytes 3080 | tf_op jit(solution)/shard_map/ppermute | solution.py:226
  55.0 1.2 %collective-permute-start.12 = (f32[16,128]{1,0:T(8,128)S(1)}, f32[16,128]{1,0:T(8,128)S(1)}, u32[]{:S(2)}, u32[]{:S(2)}) collective-permute-start(f32[16,128]{1,0:T(8,128)S(1)} %get-tuple-element.43), channel_id=1, source_target_pairs={{0,32},{32,0},{1,33},{33,1},{2,34},{34,2},{3,35},{35,3},{4,36},{36... | collective-permute-start | bytes 24584 | tf_op jit(solution)/shard_map/ppermute | solution.py:240
  75.0 1.3 %collective-permute-start.13 = (f32[8,128]{1,0:T(8,128)S(1)}, f32[8,128]{1,0:T(8,128)S(1)}, u32[]{:S(2)}, u32[]{:S(2)}) collective-permute-start(f32[8,128]{1,0:T(8,128)S(1)} %row_reduce.1.mine), channel_id=1, source_target_pairs={{0,32},{32,0},{1,33},{33,1},{2,34},{34,2},{3,35},{35,3},{4,36},{36... | collective-permute-start | bytes 12296 | tf_op jit(solution)/shard_map/ppermute | solution.py:252
  76.9 3.6 %collective-permute-start.14 = (f32[8,128]{1,0:T(8,128)S(1)}, f32[8,128]{1,0:T(8,128)S(1)}, u32[]{:S(2)}, u32[]{:S(2)}) collective-permute-start(f32[8,128]{1,0:T(8,128)S(1)} %get-tuple-element.44), channel_id=1, source_target_pairs={{0,8},{8,0},{16,24},{24,16},{1,9},{9,1},{17,25},{25,17},{2,10},{10... | collective-permute-start | bytes 12296 | tf_op jit(solution)/shard_map/ppermute | solution.py:256
  80.5 4.8 %collective-permute-start.15 = (f32[8,128]{1,0:T(8,128)S(1)}, f32[8,128]{1,0:T(8,128)S(1)}, u32[]{:S(2)}, u32[]{:S(2)}) collective-permute-start(f32[8,128]{1,0:T(8,128)S(1)} %add.125.scalars_a), channel_id=1, source_target_pairs={{0,24},{8,16},{16,8},{24,0},{1,25},{9,17},{17,9},{25,1},{2,26},{10... | collective-permute-start | bytes 12296 | tf_op jit(solution)/shard_map/ppermute | solution.py:257
  83.2 0.7 copy-start.4
  83.9 0.7 copy-start.7

commit v3 on v2

v3 whole, which is shorter than its diff:
```python
import jax
import jax.numpy as jnp
from jax import lax
from jax.experimental import pallas as pl
from jax.experimental.pallas import tpu as pltpu
from jax.sharding import Mesh, PartitionSpec as P

D = 4096
FF = 16384
TOKENS = 12288

decay_rate = 0.9
step_size = 0.3

Y, C, X, Z = 4, 2, 4, 8
ROWS = D // X
OWN = FF // (Z * Y * C)
DEPTH = TOKENS // (Y * C)
LANES = 128
GROUPS = ROWS // LANES
SHARE = GROUPS // C
STEPS = 6
WIRE = jnp.float16
F32 = jnp.float32
BF16 = jnp.bfloat16
TILE = (8, LANES)
TILE32 = (TILE, F32)

swap_core = [(0, 1), (1, 0)]
turn = (-1, 1)
to_ahead = [(i * C + k, (i + turn[k]) % Y * C + k) for i in range(Y) for k in range(C)]
to_behind = [(i * C + k, (i - turn[k]) % Y * C + k) for i in range(Y) for k in range(C)]
pair_near = [(i, i ^ 1) for i in range(X)]
pair_wrap = [(i, X - 1 - i) for i in range(X)]

VMEM = pl.BlockSpec(memory_space=pltpu.VMEM)
SMEM = pl.BlockSpec(memory_space=pltpu.SMEM)
HBM = pl.BlockSpec(memory_space=pltpu.HBM)
LIMIT = 14 * 2**20
FIRST_LIMIT = 48 * 2**20
SECOND_LIMIT = 43 * 2**20
THIRD_LIMIT = 39 * 2**20
NO_COST = pl.CostEstimate(flops=1, bytes_accessed=1, transcendentals=0)


def call(kernel, name, outs, *operands, scalars=0):
    return pl.pallas_call(
        kernel,
        name=name,
        in_specs=[SMEM] * scalars + [VMEM] * (len(operands) - scalars),
        out_specs=[VMEM] * len(outs),
        out_shape=[jax.ShapeDtypeStruct(shape, kind) for shape, kind in outs],
        compiler_params=pltpu.CompilerParams(vmem_limit_bytes=LIMIT),
        cost_estimate=NO_COST,
    )(*operands)


def load_rows(k):
    return pl.ds(k * DEPTH // STEPS, DEPTH // STEPS)


def pair_copies(owner, cotangent, pair, landed):
    width = C * OWN
    columns = pl.ds(pl.multiple_of(owner * width, width), width)
    return [
        pltpu.make_async_copy(
            cotangent.at[load_rows(k), columns], pair.at[load_rows(k), :], landed.at[k]
        )
        for k in range(STEPS)
    ]


def start_all(copies):
    for copy in copies:
        copy.start()


def wait_all(copies):
    for copy in copies:
        copy.wait()


def product(left, right):
    return lax.dot_general(left, right, (((0,), (0,)), ((), ())), preferred_element_type=F32)


def core_columns(core):
    return pl.ds(pl.multiple_of(core * OWN, OWN), OWN)


def first_kernel(owner, core, activations, cotangent, out, kept, pair, arrived, landed):
    blocks = pair_copies(owner[0], cotangent, pair, landed)
    wholes = [
        pltpu.make_async_copy(
            activations.at[load_rows(k), :], kept.at[load_rows(k), :], arrived.at[k]
        )
        for k in range(STEPS)
    ]
    for block, whole in zip(blocks, wholes):
        block.start()
        whole.start()
    away = core_columns(1 - core[0])
    group = STEPS // 3
    for k in range(0, STEPS, group):
        wait_all(blocks[k : k + group] + wholes[k : k + group])
        rows = pl.ds(k * DEPTH // STEPS, group * DEPTH // STEPS)
        value = product(kept[rows, :], pair[rows, away])
        if k == 0:
            out[...] = value
        else:
            out[...] += value


def second_kernel(
    core, owner_a, owner_b, kept, pair, cotangent, out, pair_a, pair_b, landed_a, landed_b
):
    loads = pair_copies(owner_a[0], cotangent, pair_a, landed_a)
    loads += pair_copies(owner_b[0], cotangent, pair_b, landed_b)
    start_all(loads)
    out[...] = product(kept[...], pair[:, core_columns(core[0])])
    wait_all(loads)


def middle_kernel(
    core, owner, kept, pair_a, pair_b, cotangent, away_a, away_b, out_a, out_b, pair, landed
):
    loads = pair_copies(owner[0], cotangent, pair, landed)
    start_all(loads)
    mine, twin = core_columns(core[0]), core_columns(1 - core[0])
    away_a[...] = product(kept[...], pair_b[:, twin])
    away_b[...] = product(kept[...], pair_a[:, twin])
    out_a[...] = product(kept[...], pair_a[:, mine])
    out_b[...] = product(kept[...], pair_b[:, mine])
    wait_all(loads)


def last_kernel(core, kept, pair, away, out):
    away[...] = product(kept[...], pair[:, core_columns(1 - core[0])])
    out[...] = product(kept[...], pair[:, core_columns(core[0])])


BLOCK = ((ROWS, OWN), F32)
KEPT = ((DEPTH, ROWS), BF16)
PAIR = ((DEPTH, C * OWN), BF16)


def loading_call(kernel, name, limit, in_specs, outs, semaphores, *operands):
    return pl.pallas_call(
        kernel,
        name=name,
        in_specs=in_specs,
        out_specs=[VMEM] * len(outs),
        out_shape=[jax.ShapeDtypeStruct(shape, kind) for shape, kind in outs],
        scratch_shapes=[pltpu.SemaphoreType.DMA((count,)) for count in semaphores],
        compiler_params=pltpu.CompilerParams(vmem_limit_bytes=limit),
        cost_estimate=NO_COST,
    )(*operands)


def lane_sums(block):
    folded = block[:, :LANES] + block[:, LANES:]
    return jnp.sum(folded.T, axis=0, keepdims=True)


def split_rows(core, first_row, halves, mine, away):
    first = core[0] == 0
    for group in range(SHARE):
        at = first_row + group
        a, b = halves[0][group], halves[1][group]
        mine[at : at + 1, :] = jnp.where(first, a, b)
        away[at : at + 1, :] = jnp.where(first, b, a)


def gradient_rows(gradient, half, group):
    at = (half * SHARE + group) * LANES
    return gradient[at : at + LANES, :]


def square_rows_kernel(core, gradient, param, mine, away):
    halves = []
    for half in range(C):
        blocks = [gradient_rows(gradient, half, group) for group in range(SHARE)]
        halves.append([lane_sums(block * block) for block in blocks])
    split_rows(core, 0, halves, mine, away)
    value = param[...]
    total = jnp.full((SHARE, LANES), jnp.sum(value * value))
    mine[SHARE:, :] = total
    away[SHARE:, :] = total


def weighted_rows_kernel(
    core, gradient, col_a, col_b, col_state, mine_in, away_in, new_col, mine, away
):
    col = decay_rate * col_state[...] + (1.0 - decay_rate) * (col_a[...] + col_b[...]) / D
    new_col[...] = col
    inverse = 1.0 / col
    halves = []
    for half in range(C):
        blocks = [gradient_rows(gradient, half, group) for group in range(SHARE)]
        halves.append([lane_sums(block * block * inverse) for block in blocks])
    split_rows(core, 2 * SHARE, halves, mine, away)
    mine[: 2 * SHARE, :] = mine_in[...]
    away[: 2 * SHARE, :] = away_in[...]
    mine[3 * SHARE :, :] = jnp.zeros((SHARE, LANES), F32)
    away[3 * SHARE :, :] = jnp.zeros((SHARE, LANES), F32)


def message_kernel(mine, came, out):
    packed = mine[...] + came[...]
    high = packed.astype(BF16)
    rest = (packed - high.astype(F32)).astype(BF16)
    pieces = [
        high[:SHARE],
        rest[:SHARE],
        high[2 * SHARE : 3 * SHARE],
        high[SHARE : SHARE + 2],
        rest[SHARE : SHARE + 2],
    ]
    message = jnp.concatenate([piece.astype(F32) for piece in pieces], axis=0).astype(BF16)
    for k in range(Y * Z):
        out[k] = message


def reduce_kernel(core, came, row_state, out):
    total = jnp.sum(came[...].astype(F32), axis=0)
    squares = total[:SHARE] + total[SHARE : 2 * SHARE]
    weighted = total[2 * SHARE : 3 * SHARE]
    state = jnp.where(core[0] == 0, row_state[:SHARE, :], row_state[SHARE:, :])
    row = decay_rate * state + (1.0 - decay_rate) * squares / FF
    param_total = total[3 * SHARE : 3 * SHARE + 1] + total[3 * SHARE + 2 : 3 * SHARE + 3]
    out[:SHARE, :] = row
    out[SHARE : SHARE + 1, :] = jnp.full((1, LANES), jnp.sum(weighted / row))
    out[SHARE + 1 : SHARE + 2, :] = jnp.full((1, LANES), jnp.sum(row))
    out[SHARE + 2 :, :] = jnp.broadcast_to(0.5 * param_total, (2, LANES))


def merge_kernel(core, mine, twin, new_row):
    first = core[0] == 0
    a, b = mine[:SHARE, :], twin[:SHARE, :]
    new_row[:SHARE, :] = jnp.where(first, a, b)
    new_row[SHARE:, :] = jnp.where(first, b, a)


def normalise_kernel(gradient, new_row, new_col, update):
    col_factor = lax.rsqrt(new_col[...])
    row_factor = lax.rsqrt(new_row[...])
    for group in range(GROUPS):
        block = gradient[group * LANES : (group + 1) * LANES, :]
        along = jnp.broadcast_to(row_factor[group : group + 1, :], (LANES, LANES)).T
        factor = jnp.concatenate([along, along], axis=1) * col_factor
        update[group * LANES : (group + 1) * LANES, :] = block * factor


def step_kernel(scalars_a, scalars_b, param, update, new_param, stage, sent):
    sums = scalars_a[...] + scalars_b[...]
    entries = D * FF
    row_level = sums[SHARE + 1 : SHARE + 2] / D
    clip = jnp.maximum(1.0, jnp.sqrt(row_level * sums[SHARE : SHARE + 1] / entries))
    scale = jnp.sqrt(sums[SHARE + 2 : SHARE + 3] / entries)
    factor = step_size * scale * jnp.sqrt(row_level) / clip
    factor = jnp.concatenate([factor, factor], axis=1)
    copies = []
    for group in range(GROUPS):
        rows = pl.ds(group * LANES, LANES)
        stage[rows, :] = param[rows, :] - factor * update[rows, :]
        copy = pltpu.make_async_copy(stage.at[rows, :], new_param.at[rows, :], sent.at[group])
        copy.start()
        copies.append(copy)
    wait_all(copies)


def per_device(activations, cotangent, param, row_state, col_state):
    y = lax.axis_index("y")
    c = lax.axis_index("c")
    barrier = lax.optimization_barrier
    way = 2 * c - 1
    hops = [lax.rem(y + Y + hop, Y)[None] for hop in (2, -way, way, 0)]
    *hops, core = barrier((*hops, c[None]))

    def wide(value):
        return value.astype(F32)

    def narrow(value):
        return barrier(value.astype(WIRE))

    def swapped(value, count):
        size = ROWS // count
        parts = [narrow(value[k * size : (k + 1) * size]) for k in range(count)]
        parts = [lax.ppermute(part, "c", swap_core) for part in parts]
        return wide(jnp.concatenate(parts))

    far_away, kept, pair = loading_call(
        first_kernel,
        "first_matmul",
        FIRST_LIMIT,
        [SMEM, SMEM, HBM, HBM],
        [BLOCK, KEPT, PAIR],
        [STEPS, STEPS],
        hops[0],
        core,
        activations,
        cotangent,
    )
    far_came = swapped(far_away, 1)
    far, behind_pair, ahead_pair = loading_call(
        second_kernel,
        "second_matmul",
        SECOND_LIMIT,
        [SMEM, SMEM, SMEM, VMEM, VMEM, HBM],
        [BLOCK, PAIR, PAIR],
        [STEPS, STEPS],
        core,
        hops[1],
        hops[2],
        kept,
        pair,
        cotangent,
    )
    far = narrow(far + far_came)
    far_sent = lax.ppermute(far, ("y", "c"), to_ahead)

    behind_pair, _ = barrier((behind_pair, far))
    behind_away, ahead_away, behind, ahead, own_pair = loading_call(
        middle_kernel,
        "middle_matmul",
        THIRD_LIMIT,
        [SMEM, SMEM, VMEM, VMEM, VMEM, HBM],
        [BLOCK, BLOCK, BLOCK, BLOCK, PAIR],
        [STEPS],
        core,
        hops[3],
        kept,
        behind_pair,
        ahead_pair,
        cotangent,
    )
    behind_came = swapped(behind_away, 4)
    ahead_came = swapped(ahead_away, 4)
    behind = narrow(behind + behind_came)
    behind_sent = lax.ppermute(behind, ("y", "c"), to_behind)
    ahead = narrow(ahead + ahead_came + wide(far_sent))
    ahead_sent = lax.ppermute(ahead, ("y", "c"), to_ahead)

    own_pair, _, _ = barrier((own_pair, behind, ahead))
    own_away, own = call(last_kernel, "last_matmul", [BLOCK, BLOCK], core, kept, own_pair, scalars=1)
    own_came = swapped(own_away, 2)
    gradient = own + own_came + wide(behind_sent) + wide(ahead_sent)

    col_part = jnp.sum(gradient * gradient, axis=0)
    col_part = col_part.reshape(1, OWN)
    col_part = col_part + lax.ppermute(col_part, "x", pair_near)
    col_came = lax.ppermute(col_part, "x", pair_wrap)
    mine, away = call(
        square_rows_kernel, "square_rows", [TILE32, TILE32], core, gradient, param, scalars=1
    )
    new_col, mine, away = call(
        weighted_rows_kernel,
        "weighted_rows",
        [((1, OWN), F32), ((2 * 8, LANES), F32), ((2 * 8, LANES), F32)],
        core,
        gradient,
        col_part,
        col_came,
        col_state.reshape(1, OWN),
        mine,
        away,
        scalars=1,
    )
    came = lax.ppermute(away, "c", swap_core)
    (message,) = call(message_kernel, "message", [((Y * Z, 16, LANES), BF16)], mine, came)
    came = lax.all_to_all(message, ("y", "z"), 0, 0, tiled=True)
    (reduced,) = call(
        reduce_kernel,
        "row_reduce",
        [TILE32],
        core,
        came,
        row_state.reshape(TILE),
        scalars=1,
    )
    twin = lax.ppermute(reduced, "c", swap_core)
    (new_row,) = call(merge_kernel, "merge", [TILE32], core, reduced, twin, scalars=1)
    scalars = reduced + twin
    scalars = scalars + lax.ppermute(scalars, "x", pair_near)
    scalars_came = lax.ppermute(scalars, "x", pair_wrap)
    (update,) = call(
        normalise_kernel, "normalise", [BLOCK], gradient, new_row, new_col
    )
    new_param = pl.pallas_call(
        step_kernel,
        name="step",
        in_specs=[VMEM] * 4,
        out_specs=HBM,
        out_shape=jax.ShapeDtypeStruct((ROWS, OWN), F32),
        scratch_shapes=[pltpu.VMEM((ROWS, OWN), F32), pltpu.SemaphoreType.DMA((GROUPS,))],
        compiler_params=pltpu.CompilerParams(vmem_limit_bytes=LIMIT),
        cost_estimate=NO_COST,
    )(scalars, scalars_came, param, update)
    return (new_param, new_row.reshape(ROWS), new_col.reshape(OWN))


def solution(mesh):
    split = Mesh(mesh.devices.reshape(Y, C, X, Z), ("y", "c", "x", "z"))
    tokens = ("y", "c")
    columns = ("z", "y", "c")
    in_specs = (P(tokens, "x"), P(tokens, "z"), P("x", columns), P("x"), P(columns))
    out_specs = (P("x", columns), P("x"), P(columns))
    return jax.shard_map(
        per_device, mesh=split, in_specs=in_specs, out_specs=out_specs, check_vma=False
    )
```

time: 87.4 us -> 74.6 us (0.85)
  waiting for transfers between devices: 25 us -> 19.6 us
  local copies, waits for them, and re-layouts: 6.07 us -> 1.72 us
  Pallas kernels: 19.6 us -> 15.5 us
    ppermute x10 -> x14, waiting for transfers between devices: 15.2 us -> 10.3 us  [the longest x1 9.38 us: per_device(): behind_sent = lax.ppermute(behind, ('y', 'c'), to_behind)]
    pallas_call x8 -> x4, Pallas kernels: 16.3 us -> 11.5 us  [the longest x3 10.5 us: loading_call(): pl.pallas_call(kernel, name=name, in_specs=in_specs, out_specs=[VMEM] * l...]
    unnamed x20 -> x10, local copies, waits for them, and re-layouts: 6.07 us -> 1.38 us
    ppermute x10 -> x14, starting transfers between devices: 8.02 us -> 8.53 us  [the longest x1 3.09 us: per_device(): far_sent = lax.ppermute(far, ('y', 'c'), to_ahead)]
  transfers between devices with their start and end apart: 16 -> 20, of which waited for: 12 -> 11; matrix products, arithmetic and copies ran while one was open for 0% -> 2% of each run, Pallas kernels for 12% -> 14%
where the time goes in v3:
time: 74.6 us; the launch traced here: 73.8 us
  waiting for transfers between devices  19.6 us (26%)
  blocking collectives  18.6 us (25%)
  starting transfers between devices  16 us (21%)
  Pallas kernels  15.5 us (21%)
  local copies, waits for them, and re-layouts  1.72 us (2%)
  other arithmetic  1.41 us (2%)
  between operations  0.97 us (1%)
    all_to_all x1, blocking collectives, per_device(): came = lax.all_to_all(message, ('y', 'z'), 0, 0, tiled=True)  18.6 us
    pallas_call x3, Pallas kernels, loading_call(): pl.pallas_call(kernel, name=name, in_specs=in_specs, out_specs=[VMEM] * l...  10.5 us
    ppermute x1, waiting for transfers between devices, per_device(): behind_sent = lax.ppermute(behind, ('y', 'c'), to_behind)  9.38 us
    pallas_call x7, Pallas kernels, call(): pl.pallas_call(kernel, name=name, in_specs=[SMEM] * scalars + [VMEM] * (l...  3.96 us
    ppermute x1, waiting for transfers between devices, per_device(): scalars = scalars + lax.ppermute(scalars, 'x', pair_near)  3.33 us
    ppermute x1, starting transfers between devices, per_device(): far_sent = lax.ppermute(far, ('y', 'c'), to_ahead)  3.09 us
    ppermute x11, starting transfers between devices, swapped(): parts = [lax.ppermute(part, 'c', swap_core) for part in parts]  2.77 us
    ppermute x1, starting transfers between devices, per_device(): scalars_came = lax.ppermute(scalars, 'x', pair_wrap)  2.76 us
  transfers between devices with their start and end apart: 20, of which 11 were waited for; matrix products, arithmetic and copies ran while one was open for 2% of the time, Pallas kernels for 14%

profile of v3, /device:TPU:32, one launch (start us, length us, event | category | flops | bytes accessed | tf_op | source)
XLA Modules:
  0.0 73.8 jit_solution(17470515778832232222)
XLA Ops:
  0.6 3.3 %first_matmul.1 = (f32[1024,256]{1,0:T(8,128)S(1)}, bf16[1536,1024]{1,0:T(8,128)(2,1)S(1)}, bf16[1536,512]{1,0:T(8,128)(2,1)S(1)}) custom-call(s32[1]{0:T(128)} %bitcast.owner, s32[1]{0:T(128)} %bitcast.4.core, bf16[1536,1024]{1,0:T(8,128)(2,1)} %activations.1, bf16[1536,2048]{1,0:T(8,128)(2,1)} %cotangent.5), custom_call_target="tpu_custom_call" | custom-call | flops 1 | bytes 1 | tf_op jit(solution)/shard_map/first_matmul/pallas_call | solution.py:148
  3.9 0.1 convert_element_type.43
  4.1 2.8 %second_matmul.1 = (f32[1024,256]{1,0:T(8,128)S(1)}, bf16[1536,512]{1,0:T(8,128)(2,1)S(1)}, bf16[1536,512]{1,0:T(8,128)(2,1)S(1)}) custom-call(s32[1]{0:T(128)} %bitcast.4.core, s32[1]{0:T(128)} %bitcast.1.owner_a, s32[1]{0:T(128)} %bitcast.2.owner_b, bf16[1536,1024]{1,0:T(8,128)(2,1)S(1)} %get-tuple-element.30.kept, ...), custom_call_target="tpu_custom_call" | custom-call | flops 1 | bytes 1 | tf_op jit(solution)/shard_map/second_matmul/pallas_call | solution.py:148
  6.9 0.2 add_convert_fusion.2
  7.1 3.1 %collective-permute-start.9 = (f16[1024,256]{1,0:T(8,128)(2,1)S(1)}, f16[1024,256]{1,0:T(8,128)(2,1)S(1)}, u32[]{:S(2)}, u32[]{:S(2)}) collective-permute-start(f16[1024,256]{1,0:T(8,128)(2,1)S(1)} %add_convert_fusion.2), channel_id=1, source_target_pairs={{0,192},{32,96},{64,0},{96,160},{128,64},{160,224},{192,128},{224,... | collective-permute-start | bytes 1572872 | tf_op jit(solution)/shard_map/ppermute | solution.py:320
  10.2 4.4 %middle_matmul.1 = (f32[1024,256]{1,0:T(8,128)S(1)}, f32[1024,256]{1,0:T(8,128)S(1)}, f32[1024,256]{1,0:T(8,128)S(1)}, f32[1024,256]{1,0:T(8,128)S(1)}, bf16[1536,512]{1,0:T(8,128)(2,1)S(1)}) custom-call(s32[1]{0:T(128)} %bitcast.4.core, s32[1]{0:T(128)} %bitcast.3.owner, bf16[1536,1024]{1,0:T(8,128)(2,1)S(1)} %get-tuple-element.30.kept, ...), custom_call_target="tpu_custom_call" | custom-call | flops 1 | bytes 1 | tf_op jit(solution)/shard_map/middle_matmul/pallas_call | solution.py:148
  14.6 0.1 convert.16
  14.7 0.1 fusion.1
  15.0 0.5 collective-permute-start.1
  15.5 0.1 collective-permute-start.3
  15.6 0.4 collective-permute-start.2
  16.1 0.1 fusion.2
  16.2 0.1 collective-permute-done.4
  16.3 0.1 collective-permute-start.8
  16.5 0.3 collective-permute-start.5
  16.8 0.2 collective-permute-start.7
  17.0 0.3 collective-permute-start.6
  17.3 0.2 add_convert_fusion.1
  17.5 0.1 collective-permute-done.8
  17.6 0.1 collective-permute-start.12
  17.8 0.3 collective-permute-done.7
  18.2 0.3 collective-permute-done.6
  18.4 0.3 add_convert_fusion
  18.7 2.5 %collective-permute-start.13 = (f16[1024,256]{1,0:T(8,128)(2,1)S(1)}, f16[1024,256]{1,0:T(8,128)(2,1)S(1)}, u32[]{:S(2)}, u32[]{:S(2)}) collective-permute-start(f16[1024,256]{1,0:T(8,128)(2,1)S(1)} %add_convert_fusion), channel_id=1, source_target_pairs={{0,192},{32,96},{64,0},{96,160},{128,64},{160,224},{192,128},{224,... | collective-permute-start | bytes 1572872 | tf_op jit(solution)/shard_map/ppermute | solution.py:342
  21.3 1.8 %last_matmul.1 = (f32[1024,256]{1,0:T(8,128)S(1)}, f32[1024,256]{1,0:T(8,128)S(1)}) custom-call(s32[1]{0:T(128)} %bitcast.4.core, bf16[1536,1024]{1,0:T(8,128)(2,1)S(1)} %get-tuple-element.30.kept, bf16[1536,512]{1,0:T(8,128)(2,1)S(1)} %get-tuple-element.45.pair), custom_call_target="tpu_custom_call" | custom-call | flops 1 | bytes 1 | tf_op jit(solution)/shard_map/last_matmul/pallas_call | solution.py:47
  23.1 0.1 convert.18
  23.2 0.1 fusion
  23.4 0.5 collective-permute-start.10
  23.9 9.4 %collective-permute-done.12 = f16[1024,256]{1,0:T(8,128)(2,1)S(1)} collective-permute-done((f16[1024,256]{1,0:T(8,128)(2,1)S(1)}, f16[1024,256]{1,0:T(8,128)(2,1)S(1)}, u32[]{:S(2)}, u32[]{:S(2)}) %collective-permute-start.12) | collective-permute-done | bytes 524320 | tf_op jit(solution)/shard_map/ppermute | solution.py:340
  33.3 0.3 multiply_reduce_fusion
  33.7 1.6 %collective-permute-start.14 = (f32[1,256]{1,0:T(1,128)S(1)}, f32[1,256]{1,0:T(1,128)S(1)}, u32[]{:S(2)}, u32[]{:S(2)}) collective-permute-start(f32[1,256]{1,0:T(1,128)S(1)} %bitcast.14), channel_id=1, source_target_pairs={{0,8},{8,0},{16,24},{24,16},{1,9},{9,1},{17,25},{25,17},{2,10},{10... | collective-permute-start | bytes 3080 | tf_op jit(solution)/shard_map/ppermute | solution.py:351
  35.2 2.1 %collective-permute-done.14 = f32[1,256]{1,0:T(1,128)S(1)} collective-permute-done((f32[1,256]{1,0:T(1,128)S(1)}, f32[1,256]{1,0:T(1,128)S(1)}, u32[]{:S(2)}, u32[]{:S(2)}) %collective-permute-start.14) | collective-permute-done | bytes 1056 | tf_op jit(solution)/shard_map/ppermute | solution.py:351
  37.3 2.8 %collective-permute-start.15 = (f32[1,256]{1,0:T(1,128)S(1)}, f32[1,256]{1,0:T(1,128)S(1)}, u32[]{:S(2)}, u32[]{:S(2)}) collective-permute-start(f32[1,256]{1,0:T(1,128)S(1)} %add.59.col_a), channel_id=1, source_target_pairs={{0,24},{8,16},{16,8},{24,0},{1,25},{9,17},{17,9},{25,1},{2,26},{10... | collective-permute-start | bytes 3080 | tf_op jit(solution)/shard_map/ppermute | solution.py:352
  40.1 0.4 square_rows.1
  40.5 1.6 %collective-permute-done.15.col_b = f32[1,256]{1,0:T(1,128)S(1)} collective-permute-done((f32[1,256]{1,0:T(1,128)S(1)}, f32[1,256]{1,0:T(1,128)S(1)}, u32[]{:S(2)}, u32[]{:S(2)}) %collective-permute-start.15) | collective-permute-done | bytes 1056 | tf_op jit(solution)/shard_map/ppermute | solution.py:352
  42.1 0.7 weighted_rows.1
  42.8 1.2 %collective-permute-done.16.came = f32[16,128]{1,0:T(8,128)S(1)} collective-permute-done((f32[16,128]{1,0:T(8,128)S(1)}, f32[16,128]{1,0:T(8,128)S(1)}, u32[]{:S(2)}, u32[]{:S(2)}) %collective-permute-start.16) | collective-permute-done | bytes 8224 | tf_op jit(solution)/shard_map/ppermute | solution.py:369
  44.0 18.6 %all_to_all.5.came = bf16[32,16,128]{2,1,0:T(8,128)(2,1)S(1)} all-to-all(bf16[32,16,128]{2,1,0:T(8,128)(2,1)S(1)} %message.1), channel_id=1, replica_groups=mesh['y'=4,'c'=2,'x'=4,'z'=8] {'y','z'}, dimensions={0} | all-to-all | bytes 262144 | tf_op jit(solution)/shard_map/all_to_all | solution.py:371
  62.6 0.2 row_reduce.1.mine
  62.8 1.2 %collective-permute-done.17.twin = f32[8,128]{1,0:T(8,128)S(1)} collective-permute-done((f32[8,128]{1,0:T(8,128)S(1)}, f32[8,128]{1,0:T(8,128)S(1)}, u32[]{:S(2)}, u32[]{:S(2)}) %collective-permute-start.17) | collective-permute-done | bytes 4128 | tf_op jit(solution)/shard_map/ppermute | solution.py:381
  64.0 0.3 collective-permute-start.18
  64.3 3.3 %collective-permute-done.18 = f32[8,128]{1,0:T(8,128)S(1)} collective-permute-done((f32[8,128]{1,0:T(8,128)S(1)}, f32[8,128]{1,0:T(8,128)S(1)}, u32[]{:S(2)}, u32[]{:S(2)}) %collective-permute-start.18) | collective-permute-done | bytes 4128 | tf_op jit(solution)/shard_map/ppermute | solution.py:384
  67.6 2.8 %collective-permute-start.19 = (f32[8,128]{1,0:T(8,128)S(1)}, f32[8,128]{1,0:T(8,128)S(1)}, u32[]{:S(2)}, u32[]{:S(2)}) collective-permute-start(f32[8,128]{1,0:T(8,128)S(1)} %add.61.scalars_a), channel_id=1, source_target_pairs={{0,24},{8,16},{16,8},{24,0},{1,25},{9,17},{17,9},{25,1},{2,26},{10... | collective-permute-start | bytes 12296 | tf_op jit(solution)/shard_map/ppermute | solution.py:385
  70.4 0.6 merge.1.new_row
  71.0 0.7 copy-done.1
  71.6 0.7 copy-done.4
  72.3 0.2 normalise.1.update
  72.5 1.1 %step.1 = f32[1024,256]{1,0:T(8,128)} custom-call(f32[8,128]{1,0:T(8,128)S(1)} %add.61.scalars_a, f32[8,128]{1,0:T(8,128)S(1)} %collective-permute-done.19.scalars_b, f32[1024,256]{1,0:T(8,128)S(1)} %copy-done, f32[1024,256]{1,0:T(8,128)S(1)} %normalise.1.update), custom_call_target="tpu_custom_call" | custom-call | flops 1 | bytes 1 | tf_op jit(solution)/shard_map/step/pallas_call | solution.py:389
  (28 shorter events, 0.6 us)
Async XLA Ops:
  4.0 2.9 %collective-permute-start = (f16[1024,256]{1,0:T(8,128)(2,1)S(1)}, f16[1024,256]{1,0:T(8,128)(2,1)S(1)}, u32[]{:S(2)}, u32[]{:S(2)}) collective-permute-start(f16[1024,256]{1,0:T(8,128)(2,1)S(1)} %convert_element_type.43), channel_id=1, source_target_pairs={{0,32},{32,0},{1,33},{33,1},{2,34},{34,2},{3,35},{35,3},{4,36},{36... | collective-permute-start | bytes 1572872 | tf_op jit(solution)/shard_map/ppermute | solution.py:289
  7.1 11.3 %collective-permute-start.9 = (f16[1024,256]{1,0:T(8,128)(2,1)S(1)}, f16[1024,256]{1,0:T(8,128)(2,1)S(1)}, u32[]{:S(2)}, u32[]{:S(2)}) collective-permute-start(f16[1024,256]{1,0:T(8,128)(2,1)S(1)} %add_convert_fusion.2), channel_id=1, source_target_pairs={{0,192},{32,96},{64,0},{96,160},{128,64},{160,224},{192,128},{224,... | collective-permute-start | bytes 1572872 | tf_op jit(solution)/shard_map/ppermute | solution.py:320
  14.9 1.4 %collective-permute-start.4 = (f16[256,256]{1,0:T(8,128)(2,1)S(1)}, f16[256,256]{1,0:T(8,128)(2,1)S(1)}, u32[]{:S(2)}, u32[]{:S(2)}) collective-permute-start(f16[256,256]{1,0:T(8,128)(2,1)S(1)} %get-tuple-element.58), channel_id=1, source_target_pairs={{0,32},{32,0},{1,33},{33,1},{2,34},{34,2},{3,35},{35,3},{4,36},{36... | collective-permute-start | bytes 393224 | tf_op jit(solution)/shard_map/ppermute | solution.py:289
  15.0 1.5 %collective-permute-start.1 = (f16[256,256]{1,0:T(8,128)(2,1)S(1)}, f16[256,256]{1,0:T(8,128)(2,1)S(1)}, u32[]{:S(2)}, u32[]{:S(2)}) collective-permute-start(f16[256,256]{1,0:T(8,128)(2,1)S(1)} %get-tuple-element.57), channel_id=1, source_target_pairs={{0,32},{32,0},{1,33},{33,1},{2,34},{34,2},{3,35},{35,3},{4,36},{36... | collective-permute-start | bytes 393224 | tf_op jit(solution)/shard_map/ppermute | solution.py:289
  15.5 1.4 %collective-permute-start.3 = (f16[256,256]{1,0:T(8,128)(2,1)S(1)}, f16[256,256]{1,0:T(8,128)(2,1)S(1)}, u32[]{:S(2)}, u32[]{:S(2)}) collective-permute-start(f16[256,256]{1,0:T(8,128)(2,1)S(1)} %get-tuple-element.59), channel_id=1, source_target_pairs={{0,32},{32,0},{1,33},{33,1},{2,34},{34,2},{3,35},{35,3},{4,36},{36... | collective-permute-start | bytes 393224 | tf_op jit(solution)/shard_map/ppermute | solution.py:289
  15.6 1.4 %collective-permute-start.2 = (f16[256,256]{1,0:T(8,128)(2,1)S(1)}, f16[256,256]{1,0:T(8,128)(2,1)S(1)}, u32[]{:S(2)}, u32[]{:S(2)}) collective-permute-start(f16[256,256]{1,0:T(8,128)(2,1)S(1)} %get-tuple-element.60), channel_id=1, source_target_pairs={{0,32},{32,0},{1,33},{33,1},{2,34},{34,2},{3,35},{35,3},{4,36},{36... | collective-permute-start | bytes 393224 | tf_op jit(solution)/shard_map/ppermute | solution.py:289
  16.3 1.3 %collective-permute-start.8 = (f16[256,256]{1,0:T(8,128)(2,1)S(1)}, f16[256,256]{1,0:T(8,128)(2,1)S(1)}, u32[]{:S(2)}, u32[]{:S(2)}) collective-permute-start(f16[256,256]{1,0:T(8,128)(2,1)S(1)} %get-tuple-element.62), channel_id=1, source_target_pairs={{0,32},{32,0},{1,33},{33,1},{2,34},{34,2},{3,35},{35,3},{4,36},{36... | collective-permute-start | bytes 393224 | tf_op jit(solution)/shard_map/ppermute | solution.py:289
  16.5 1.3 %collective-permute-start.5 = (f16[256,256]{1,0:T(8,128)(2,1)S(1)}, f16[256,256]{1,0:T(8,128)(2,1)S(1)}, u32[]{:S(2)}, u32[]{:S(2)}) collective-permute-start(f16[256,256]{1,0:T(8,128)(2,1)S(1)} %get-tuple-element.61), channel_id=1, source_target_pairs={{0,32},{32,0},{1,33},{33,1},{2,34},{34,2},{3,35},{35,3},{4,36},{36... | collective-permute-start | bytes 393224 | tf_op jit(solution)/shard_map/ppermute | solution.py:289
  16.8 1.3 %collective-permute-start.7 = (f16[256,256]{1,0:T(8,128)(2,1)S(1)}, f16[256,256]{1,0:T(8,128)(2,1)S(1)}, u32[]{:S(2)}, u32[]{:S(2)}) collective-permute-start(f16[256,256]{1,0:T(8,128)(2,1)S(1)} %get-tuple-element.63), channel_id=1, source_target_pairs={{0,32},{32,0},{1,33},{33,1},{2,34},{34,2},{3,35},{35,3},{4,36},{36... | collective-permute-start | bytes 393224 | tf_op jit(solution)/shard_map/ppermute | solution.py:289
  17.0 1.4 %collective-permute-start.6 = (f16[256,256]{1,0:T(8,128)(2,1)S(1)}, f16[256,256]{1,0:T(8,128)(2,1)S(1)}, u32[]{:S(2)}, u32[]{:S(2)}) collective-permute-start(f16[256,256]{1,0:T(8,128)(2,1)S(1)} %get-tuple-element.64), channel_id=1, source_target_pairs={{0,32},{32,0},{1,33},{33,1},{2,34},{34,2},{3,35},{35,3},{4,36},{36... | collective-permute-start | bytes 393224 | tf_op jit(solution)/shard_map/ppermute | solution.py:289
  17.6 15.7 %collective-permute-start.12 = (f16[1024,256]{1,0:T(8,128)(2,1)S(1)}, f16[1024,256]{1,0:T(8,128)(2,1)S(1)}, u32[]{:S(2)}, u32[]{:S(2)}) collective-permute-start(f16[1024,256]{1,0:T(8,128)(2,1)S(1)} %add_convert_fusion.1), channel_id=1, source_target_pairs={{0,64},{32,224},{64,128},{96,32},{128,192},{160,96},{192,0},{224,1... | collective-permute-start | bytes 1572872 | tf_op jit(solution)/shard_map/ppermute | solution.py:340
  18.7 14.6 %collective-permute-start.13 = (f16[1024,256]{1,0:T(8,128)(2,1)S(1)}, f16[1024,256]{1,0:T(8,128)(2,1)S(1)}, u32[]{:S(2)}, u32[]{:S(2)}) collective-permute-start(f16[1024,256]{1,0:T(8,128)(2,1)S(1)} %add_convert_fusion), channel_id=1, source_target_pairs={{0,192},{32,96},{64,0},{96,160},{128,64},{160,224},{192,128},{224,... | collective-permute-start | bytes 1572872 | tf_op jit(solution)/shard_map/ppermute | solution.py:342
  23.3 10.0 %collective-permute-start.11 = (f16[512,256]{1,0:T(8,128)(2,1)S(1)}, f16[512,256]{1,0:T(8,128)(2,1)S(1)}, u32[]{:S(2)}, u32[]{:S(2)}) collective-permute-start(f16[512,256]{1,0:T(8,128)(2,1)S(1)} %get-tuple-element.56), channel_id=1, source_target_pairs={{0,32},{32,0},{1,33},{33,1},{2,34},{34,2},{3,35},{35,3},{4,36},{36... | collective-permute-start | bytes 786440 | tf_op jit(solution)/shard_map/ppermute | solution.py:289
  23.4 9.9 %collective-permute-start.10 = (f16[512,256]{1,0:T(8,128)(2,1)S(1)}, f16[512,256]{1,0:T(8,128)(2,1)S(1)}, u32[]{:S(2)}, u32[]{:S(2)}) collective-permute-start(f16[512,256]{1,0:T(8,128)(2,1)S(1)} %get-tuple-element.55), channel_id=1, source_target_pairs={{0,32},{32,0},{1,33},{33,1},{2,34},{34,2},{3,35},{35,3},{4,36},{36... | collective-permute-start | bytes 786440 | tf_op jit(solution)/shard_map/ppermute | solution.py:289
  33.3 6.8 %copy-start = (f32[1024,256]{1,0:T(8,128)S(1)}, f32[1024,256]{1,0:T(8,128)}, u32[]{:S(2)}) copy-start(f32[1024,256]{1,0:T(8,128)} %param.13) | copy-start | bytes 3145732
  33.6 8.5 %copy-start.3 = (f32[256]{0:T(256)S(1)}, f32[256]{0:T(256)}, u32[]{:S(2)}) copy-start(f32[256]{0:T(256)} %param.11) | copy-start | bytes 3076
  33.7 3.7 %collective-permute-start.14 = (f32[1,256]{1,0:T(1,128)S(1)}, f32[1,256]{1,0:T(1,128)S(1)}, u32[]{:S(2)}, u32[]{:S(2)}) collective-permute-start(f32[1,256]{1,0:T(1,128)S(1)} %bitcast.14), channel_id=1, source_target_pairs={{0,8},{8,0},{16,24},{24,16},{1,9},{9,1},{17,25},{25,17},{2,10},{10... | collective-permute-start | bytes 3080 | tf_op jit(solution)/shard_map/ppermute | solution.py:351
  37.3 4.8 %collective-permute-start.15 = (f32[1,256]{1,0:T(1,128)S(1)}, f32[1,256]{1,0:T(1,128)S(1)}, u32[]{:S(2)}, u32[]{:S(2)}) collective-permute-start(f32[1,256]{1,0:T(1,128)S(1)} %add.59.col_a), channel_id=1, source_target_pairs={{0,24},{8,16},{16,8},{24,0},{1,25},{9,17},{17,9},{25,1},{2,26},{10... | collective-permute-start | bytes 3080 | tf_op jit(solution)/shard_map/ppermute | solution.py:352
  40.1 22.5 %copy-start.2 = (f32[1024]{0:T(1024)S(1)}, f32[1024]{0:T(1024)}, u32[]{:S(2)}) copy-start(f32[1024]{0:T(1024)} %param.10) | copy-start | bytes 12292
  42.8 1.2 %collective-permute-start.16 = (f32[16,128]{1,0:T(8,128)S(1)}, f32[16,128]{1,0:T(8,128)S(1)}, u32[]{:S(2)}, u32[]{:S(2)}) collective-permute-start(f32[16,128]{1,0:T(8,128)S(1)} %get-tuple-element.51), channel_id=1, source_target_pairs={{0,32},{32,0},{1,33},{33,1},{2,34},{34,2},{3,35},{35,3},{4,36},{36... | collective-permute-start | bytes 24584 | tf_op jit(solution)/shard_map/ppermute | solution.py:369
  62.7 1.3 %collective-permute-start.17 = (f32[8,128]{1,0:T(8,128)S(1)}, f32[8,128]{1,0:T(8,128)S(1)}, u32[]{:S(2)}, u32[]{:S(2)}) collective-permute-start(f32[8,128]{1,0:T(8,128)S(1)} %row_reduce.1.mine), channel_id=1, source_target_pairs={{0,32},{32,0},{1,33},{33,1},{2,34},{34,2},{3,35},{35,3},{4,36},{36... | collective-permute-start | bytes 12296 | tf_op jit(solution)/shard_map/ppermute | solution.py:381
  64.0 3.6 %collective-permute-start.18 = (f32[8,128]{1,0:T(8,128)S(1)}, f32[8,128]{1,0:T(8,128)S(1)}, u32[]{:S(2)}, u32[]{:S(2)}) collective-permute-start(f32[8,128]{1,0:T(8,128)S(1)} %add.60), channel_id=1, source_target_pairs={{0,8},{8,0},{16,24},{24,16},{1,9},{9,1},{17,25},{25,17},{2,10},{10... | collective-permute-start | bytes 12296 | tf_op jit(solution)/shard_map/ppermute | solution.py:384
  67.6 4.9 %collective-permute-start.19 = (f32[8,128]{1,0:T(8,128)S(1)}, f32[8,128]{1,0:T(8,128)S(1)}, u32[]{:S(2)}, u32[]{:S(2)}) collective-permute-start(f32[8,128]{1,0:T(8,128)S(1)} %add.61.scalars_a), channel_id=1, source_target_pairs={{0,24},{8,16},{16,8},{24,0},{1,25},{9,17},{17,9},{25,1},{2,26},{10... | collective-permute-start | bytes 12296 | tf_op jit(solution)/shard_map/ppermute | solution.py:385
  71.0 0.7 copy-start.1
  71.6 0.7 copy-start.4

commit v4 on v3

--- a/solution.py
+++ b/solution.py
@@ -32,6 +32,7 @@
 to_behind = [(i * C + k, (i - turn[k]) % Y * C + k) for i in range(Y) for k in range(C)]
 pair_near = [(i, i ^ 1) for i in range(X)]
 pair_wrap = [(i, X - 1 - i) for i in range(X)]
+pair_cross = [(i, (i + 2) % X) for i in range(X)]
 
 VMEM = pl.BlockSpec(memory_space=pltpu.VMEM)
 SMEM = pl.BlockSpec(memory_space=pltpu.SMEM)
@@ -39,7 +40,7 @@
 LIMIT = 14 * 2**20
 FIRST_LIMIT = 48 * 2**20
 SECOND_LIMIT = 43 * 2**20
-THIRD_LIMIT = 39 * 2**20
+LAST_LIMIT = 43 * 2**20
 NO_COST = pl.CostEstimate(flops=1, bytes_accessed=1, transcendentals=0)
 
 
@@ -59,12 +60,11 @@
     return pl.ds(k * DEPTH // STEPS, DEPTH // STEPS)
 
 
-def pair_copies(owner, cotangent, pair, landed):
-    width = C * OWN
-    columns = pl.ds(pl.multiple_of(owner * width, width), width)
+def column_copies(place, width, cotangent, block, landed):
+    columns = pl.ds(pl.multiple_of(place * width, width), width)
     return [
         pltpu.make_async_copy(
-            cotangent.at[load_rows(k), columns], pair.at[load_rows(k), :], landed.at[k]
+            cotangent.at[load_rows(k), columns], block.at[load_rows(k), :], landed.at[k]
         )
         for k in range(STEPS)
     ]
@@ -89,7 +89,7 @@
 
 
 def first_kernel(owner, core, activations, cotangent, out, kept, pair, arrived, landed):
-    blocks = pair_copies(owner[0], cotangent, pair, landed)
+    blocks = column_copies(owner[0], C * OWN, cotangent, pair, landed)
     wholes = [
         pltpu.make_async_copy(
             activations.at[load_rows(k), :], kept.at[load_rows(k), :], arrived.at[k]
@@ -111,30 +111,30 @@
             out[...] += value
 
 
+def block_loads(owner_a, owner_b, core, cotangent, block_a, block_b, landed_a, landed_b):
+    loads = column_copies(owner_a[0] * C + core, OWN, cotangent, block_a, landed_a)
+    return loads + column_copies(owner_b[0] * C + core, OWN, cotangent, block_b, landed_b)
+
+
 def second_kernel(
-    core, owner_a, owner_b, kept, pair, cotangent, out, pair_a, pair_b, landed_a, landed_b
+    core, behind, ahead, kept, pair, cotangent, out, a, b, mine_a, mine_b, *landed
 ):
-    loads = pair_copies(owner_a[0], cotangent, pair_a, landed_a)
-    loads += pair_copies(owner_b[0], cotangent, pair_b, landed_b)
+    loads = block_loads(ahead, behind, 1 - core[0], cotangent, a, b, *landed[:2])
+    loads += block_loads(behind, ahead, core[0], cotangent, mine_a, mine_b, *landed[2:])
     start_all(loads)
     out[...] = product(kept[...], pair[:, core_columns(core[0])])
     wait_all(loads)
 
 
-def middle_kernel(
-    core, owner, kept, pair_a, pair_b, cotangent, away_a, away_b, out_a, out_b, pair, landed
-):
-    loads = pair_copies(owner[0], cotangent, pair, landed)
+def two_kernel(kept, a, b, out_a, out_b):
+    out_a[...] = product(kept[...], a[...])
+    out_b[...] = product(kept[...], b[...])
+
+
+def last_kernel(core, owner, kept, cotangent, away, out, pair, landed):
+    loads = column_copies(owner[0], C * OWN, cotangent, pair, landed)
     start_all(loads)
-    mine, twin = core_columns(core[0]), core_columns(1 - core[0])
-    away_a[...] = product(kept[...], pair_b[:, twin])
-    away_b[...] = product(kept[...], pair_a[:, twin])
-    out_a[...] = product(kept[...], pair_a[:, mine])
-    out_b[...] = product(kept[...], pair_b[:, mine])
     wait_all(loads)
-
-
-def last_kernel(core, kept, pair, away, out):
     away[...] = product(kept[...], pair[:, core_columns(1 - core[0])])
     out[...] = product(kept[...], pair[:, core_columns(core[0])])
 
@@ -142,6 +142,7 @@
 BLOCK = ((ROWS, OWN), F32)
 KEPT = ((DEPTH, ROWS), BF16)
 PAIR = ((DEPTH, C * OWN), BF16)
+HALF = ((DEPTH, OWN), BF16)
 
 
 def loading_call(kernel, name, limit, in_specs, outs, semaphores, *operands):
@@ -188,12 +189,12 @@
     away[SHARE:, :] = total
 
 
-def weighted_rows_kernel(
-    core, gradient, col_a, col_b, col_state, mine_in, away_in, new_col, mine, away
-):
-    col = decay_rate * col_state[...] + (1.0 - decay_rate) * (col_a[...] + col_b[...]) / D
-    new_col[...] = col
-    inverse = 1.0 / col
+def column_state(col_a, col_b, col_state):
+    return decay_rate * col_state[...] + (1.0 - decay_rate) * (col_a[...] + col_b[...]) / D
+
+
+def weighted_rows_kernel(core, gradient, col_a, col_b, col_state, mine_in, away_in, mine, away):
+    inverse = 1.0 / column_state(col_a, col_b, col_state)
     halves = []
     for half in range(C):
         blocks = [gradient_rows(gradient, half, group) for group in range(SHARE)]
@@ -234,16 +235,21 @@
     out[SHARE + 2 :, :] = jnp.broadcast_to(0.5 * param_total, (2, LANES))
 
 
-def merge_kernel(core, mine, twin, new_row):
+def whole_rows(core, mine, twin):
     first = core[0] == 0
     a, b = mine[:SHARE, :], twin[:SHARE, :]
-    new_row[:SHARE, :] = jnp.where(first, a, b)
-    new_row[SHARE:, :] = jnp.where(first, b, a)
-
-
-def normalise_kernel(gradient, new_row, new_col, update):
-    col_factor = lax.rsqrt(new_col[...])
-    row_factor = lax.rsqrt(new_row[...])
+    return jnp.concatenate([jnp.where(first, a, b), jnp.where(first, b, a)], axis=0)
+
+
+def normalise_kernel(
+    core, gradient, mine, twin, col_a, col_b, col_state, update, new_row, new_col
+):
+    col = column_state(col_a, col_b, col_state)
+    row = whole_rows(core, mine, twin)
+    new_col[...] = col
+    new_row[...] = row
+    col_factor = lax.rsqrt(col)
+    row_factor = lax.rsqrt(row)
     for group in range(GROUPS):
         block = gradient[group * LANES : (group + 1) * LANES, :]
         along = jnp.broadcast_to(row_factor[group : group + 1, :], (LANES, LANES)).T
@@ -284,8 +290,8 @@
         return barrier(value.astype(WIRE))
 
     def swapped(value, count):
-        size = ROWS // count
-        parts = [narrow(value[k * size : (k + 1) * size]) for k in range(count)]
+        cuts = [ROWS * k // count // 16 * 16 for k in range(count + 1)]
+        parts = [narrow(value[a:b]) for a, b in zip(cuts, cuts[1:])]
         parts = [lax.ppermute(part, "c", swap_core) for part in parts]
         return wide(jnp.concatenate(parts))
 
@@ -302,13 +308,13 @@
         cotangent,
     )
     far_came = swapped(far_away, 1)
-    far, behind_pair, ahead_pair = loading_call(
+    far, away_a, away_b, mine_a, mine_b = loading_call(
         second_kernel,
         "second_matmul",
         SECOND_LIMIT,
         [SMEM, SMEM, SMEM, VMEM, VMEM, HBM],
-        [BLOCK, PAIR, PAIR],
-        [STEPS, STEPS],
+        [BLOCK, HALF, HALF, HALF, HALF],
+        [STEPS] * 4,
         core,
         hops[1],
         hops[2],
@@ -319,49 +325,52 @@
     far = narrow(far + far_came)
     far_sent = lax.ppermute(far, ("y", "c"), to_ahead)
 
-    behind_pair, _ = barrier((behind_pair, far))
-    behind_away, ahead_away, behind, ahead, own_pair = loading_call(
-        middle_kernel,
-        "middle_matmul",
-        THIRD_LIMIT,
-        [SMEM, SMEM, VMEM, VMEM, VMEM, HBM],
-        [BLOCK, BLOCK, BLOCK, BLOCK, PAIR],
-        [STEPS],
-        core,
-        hops[3],
-        kept,
-        behind_pair,
-        ahead_pair,
-        cotangent,
-    )
-    behind_came = swapped(behind_away, 4)
-    ahead_came = swapped(ahead_away, 4)
+    away_a, _ = barrier((away_a, far))
+    behind_away, ahead_away = call(
+        two_kernel, "third_matmul", [BLOCK, BLOCK], kept, away_a, away_b
+    )
+    behind_came = swapped(behind_away, 3)
+    ahead_came = swapped(ahead_away, 2)
+    mine_a, _, _ = barrier((mine_a, behind_away, ahead_away))
+    behind, ahead = call(two_kernel, "fourth_matmul", [BLOCK, BLOCK], kept, mine_a, mine_b)
     behind = narrow(behind + behind_came)
     behind_sent = lax.ppermute(behind, ("y", "c"), to_behind)
+    ahead, _ = barrier((ahead, behind))
     ahead = narrow(ahead + ahead_came + wide(far_sent))
     ahead_sent = lax.ppermute(ahead, ("y", "c"), to_ahead)
 
-    own_pair, _, _ = barrier((own_pair, behind, ahead))
-    own_away, own = call(last_kernel, "last_matmul", [BLOCK, BLOCK], core, kept, own_pair, scalars=1)
+    kept, _ = barrier((kept, ahead))
+    own_away, own = pl.pallas_call(
+        last_kernel,
+        name="last_matmul",
+        in_specs=[SMEM, SMEM, VMEM, HBM],
+        out_specs=[VMEM, VMEM],
+        out_shape=[jax.ShapeDtypeStruct(*BLOCK)] * 2,
+        scratch_shapes=[pltpu.VMEM(*PAIR), pltpu.SemaphoreType.DMA((STEPS,))],
+        compiler_params=pltpu.CompilerParams(vmem_limit_bytes=LAST_LIMIT),
+        cost_estimate=NO_COST,
+    )(core, hops[3], kept, cotangent)
     own_came = swapped(own_away, 2)
     gradient = own + own_came + wide(behind_sent) + wide(ahead_sent)
 
     col_part = jnp.sum(gradient * gradient, axis=0)
     col_part = col_part.reshape(1, OWN)
-    col_part = col_part + lax.ppermute(col_part, "x", pair_near)
-    col_came = lax.ppermute(col_part, "x", pair_wrap)
+    col_came = (
+        lax.ppermute(col_part, "x", pair_cross)
+        + lax.ppermute(col_part, "x", pair_near)
+        + lax.ppermute(col_part, "x", pair_wrap)
+    )
     mine, away = call(
         square_rows_kernel, "square_rows", [TILE32, TILE32], core, gradient, param, scalars=1
     )
-    new_col, mine, away = call(
+    columns = (col_part, col_came, col_state.reshape(1, OWN))
+    mine, away = call(
         weighted_rows_kernel,
         "weighted_rows",
-        [((1, OWN), F32), ((2 * 8, LANES), F32), ((2 * 8, LANES), F32)],
+        [((2 * 8, LANES), F32), ((2 * 8, LANES), F32)],
         core,
         gradient,
-        col_part,
-        col_came,
-        col_state.reshape(1, OWN),
+        *columns,
         mine,
         away,
         scalars=1,
@@ -379,12 +388,22 @@
         scalars=1,
     )
     twin = lax.ppermute(reduced, "c", swap_core)
-    (new_row,) = call(merge_kernel, "merge", [TILE32], core, reduced, twin, scalars=1)
     scalars = reduced + twin
-    scalars = scalars + lax.ppermute(scalars, "x", pair_near)
-    scalars_came = lax.ppermute(scalars, "x", pair_wrap)
-    (update,) = call(
-        normalise_kernel, "normalise", [BLOCK], gradient, new_row, new_col
+    scalars_came = (
+        lax.ppermute(scalars, "x", pair_cross)
+        + lax.ppermute(scalars, "x", pair_near)
+        + lax.ppermute(scalars, "x", pair_wrap)
+    )
+    update, new_row, new_col = call(
+        normalise_kernel,
+        "normalise",
+        [BLOCK, TILE32, ((1, OWN), F32)],
+        core,
+        gradient,
+        reduced,
+        twin,
+        *columns,
+        scalars=1,
     )
     new_param = pl.pallas_call(
         step_kernel,

time: 74.6 us -> 70.9 us (0.950)
  waiting for transfers between devices: 19.6 us -> 14.2 us
  starting transfers between devices: 16 us -> 18.8 us
  local copies, waits for them, and re-layouts: 1.72 us -> 0.35 us
    pallas_call x3 -> x2, Pallas kernels: 10.5 us -> 6.3 us  [loading_call(): pl.pallas_call(kernel, name=name, in_specs=in_specs, out_specs=[VMEM] * l...]
    pallas_call x0 -> x1, Pallas kernels: none -> 3.25 us  [per_device(): pl.pallas_call(last_kernel, name='last_matmul', in_specs=[SMEM, SMEM, VME...]
    ppermute x1, waiting for transfers between devices: 9.38 us -> 6.69 us  [per_device(): behind_sent = lax.ppermute(behind, ('y', 'c'), to_behind)]
    ppermute x4 -> x6, waiting for transfers between devices: 7 us -> 4.44 us  [the longest x1 1.73 us: per_device(): lax.ppermute(col_part, 'x', pair_cross)]
    ppermute x4 -> x6, starting transfers between devices: 7.37 us -> 9.48 us  [the longest x1 2.89 us: per_device(): lax.ppermute(scalars, 'x', pair_cross)]
    unnamed x10 -> x6, local copies, waits for them, and re-layouts: 1.38 us -> 0.02 us
    pallas_call x7, Pallas kernels: 3.96 us -> 5.24 us  [call(): pl.pallas_call(kernel, name=name, in_specs=[SMEM] * scalars + [VMEM] * (l...]
    ppermute x1, starting transfers between devices: 2.54 us -> 3.51 us  [per_device(): ahead_sent = lax.ppermute(ahead, ('y', 'c'), to_ahead)]
  transfers between devices with their start and end apart: 20 -> 19, of which waited for: 11 -> 7; matrix products, arithmetic and copies ran while one was open for 2% -> 2% of each run, Pallas kernels for 14% -> 16%
where the time goes in v4:
time: 70.9 us; the launch traced here: 70.2 us
  starting transfers between devices  18.8 us (27%)
  blocking collectives  18.6 us (26%)
  Pallas kernels  15.9 us (22%)
  waiting for transfers between devices  14.2 us (20%)
  other arithmetic  1.36 us (2%)
  between operations  1.01 us (1%)
    all_to_all x1, blocking collectives, per_device(): came = lax.all_to_all(message, ('y', 'z'), 0, 0, tiled=True)  18.6 us
    ppermute x1, waiting for transfers between devices, per_device(): behind_sent = lax.ppermute(behind, ('y', 'c'), to_behind)  6.69 us
    pallas_call x2, Pallas kernels, loading_call(): pl.pallas_call(kernel, name=name, in_specs=in_specs, out_specs=[VMEM] * l...  6.3 us
    pallas_call x7, Pallas kernels, call(): pl.pallas_call(kernel, name=name, in_specs=[SMEM] * scalars + [VMEM] * (l...  5.24 us
    ppermute x1, starting transfers between devices, per_device(): ahead_sent = lax.ppermute(ahead, ('y', 'c'), to_ahead)  3.51 us
    pallas_call x1, Pallas kernels, per_device(): pl.pallas_call(last_kernel, name='last_matmul', in_specs=[SMEM, SMEM, VME...  3.25 us
    ppermute x1, starting transfers between devices, per_device(): far_sent = lax.ppermute(far, ('y', 'c'), to_ahead)  3.09 us
    ppermute x1, starting transfers between devices, per_device(): lax.ppermute(scalars, 'x', pair_cross)  2.89 us
  transfers between devices with their start and end apart: 19, of which 7 were waited for; matrix products, arithmetic and copies ran while one was open for 2% of the time, Pallas kernels for 16%

profile of v4, /device:TPU:32, one launch (start us, length us, event | category | flops | bytes accessed | tf_op | source)
XLA Modules:
  0.0 70.2 jit_solution(9813648770509715945)
XLA Ops:
  0.6 3.3 %first_matmul.1 = (f32[1024,256]{1,0:T(8,128)S(1)}, bf16[1536,1024]{1,0:T(8,128)(2,1)S(1)}, bf16[1536,512]{1,0:T(8,128)(2,1)S(1)}) custom-call(s32[1]{0:T(128)} %bitcast.owner, s32[1]{0:T(128)} %bitcast.4.core, bf16[1536,1024]{1,0:T(8,128)(2,1)} %activations.1, bf16[1536,2048]{1,0:T(8,128)(2,1)} %cotangent.5), custom_call_target="tpu_custom_call" | custom-call | flops 1 | bytes 1 | tf_op jit(solution)/shard_map/first_matmul/pallas_call | solution.py:149
  3.9 0.1 convert_element_type.40
  4.0 0.1 collective-permute-start
  4.1 3.0 %second_matmul.1 = (f32[1024,256]{1,0:T(8,128)S(1)}, bf16[1536,256]{1,0:T(8,128)(2,1)S(1)}, bf16[1536,256]{1,0:T(8,128)(2,1)S(1)}, bf16[1536,256]{1,0:T(8,128)(2,1)S(1)}, bf16[1536,256]{1,0:T(8,128)(2,1)S(1)}) custom-call(s32[1]{0:T(128)} %bitcast.4.core, s32[1]{0:T(128)} %bitcast.1.behind, s32[1]{0:T(128)} %bitcast.2.ahead, ...), custom_call_target="tpu_custom_call" | custom-call | flops 1 | bytes 1 | tf_op jit(solution)/shard_map/second_matmul/pallas_call | solution.py:149
  7.2 0.2 add_convert_fusion.2
  7.4 3.1 %collective-permute-start.6 = (f16[1024,256]{1,0:T(8,128)(2,1)S(1)}, f16[1024,256]{1,0:T(8,128)(2,1)S(1)}, u32[]{:S(2)}, u32[]{:S(2)}) collective-permute-start(f16[1024,256]{1,0:T(8,128)(2,1)S(1)} %add_convert_fusion.2), channel_id=1, source_target_pairs={{0,192},{32,96},{64,0},{96,160},{128,64},{160,224},{192,128},{224,... | collective-permute-start | bytes 1572872 | tf_op jit(solution)/shard_map/ppermute | solution.py:326
  10.5 1.9 %third_matmul.1 = (f32[1024,256]{1,0:T(8,128)S(1)}, f32[1024,256]{1,0:T(8,128)S(1)}) custom-call(bf16[1536,1024]{1,0:T(8,128)(2,1)S(1)} %get-tuple-element.53.kept, bf16[1536,256]{1,0:T(8,128)(2,1)S(1)} %get-tuple-element.44.a, bf16[1536,256]{1,0:T(8,128)(2,1)S(1)} %get-tuple-element.45.b), custom_call_target="tpu_custom_call" | custom-call | flops 1 | bytes 1 | tf_op jit(solution)/shard_map/third_matmul/pallas_call | solution.py:48
  12.3 0.1 convert.13
  12.4 0.1 fusion.2
  12.5 0.1 convert.14
  12.6 0.1 collective-permute-start.2
  12.7 0.5 collective-permute-start.1
  13.2 0.1 collective-permute-start.3
  13.3 0.1 fusion.1
  13.4 0.5 collective-permute-start.5
  13.9 1.8 %fourth_matmul.1 = (f32[1024,256]{1,0:T(8,128)S(1)}, f32[1024,256]{1,0:T(8,128)S(1)}) custom-call(bf16[1536,1024]{1,0:T(8,128)(2,1)S(1)} %get-tuple-element.53.kept, bf16[1536,256]{1,0:T(8,128)(2,1)S(1)} %get-tuple-element.48.a, bf16[1536,256]{1,0:T(8,128)(2,1)S(1)} %get-tuple-element.49.b), custom_call_target="tpu_custom_call" | custom-call | flops 1 | bytes 1 | tf_op jit(solution)/shard_map/fourth_matmul/pallas_call | solution.py:48
  15.8 0.2 collective-permute-start.4
  16.0 0.2 add_convert_fusion.1
  16.2 0.5 collective-permute-start.9
  16.7 0.8 %collective-permute-done.4 = f16[512,256]{1,0:T(8,128)(2,1)S(1)} collective-permute-done((f16[512,256]{1,0:T(8,128)(2,1)S(1)}, f16[512,256]{1,0:T(8,128)(2,1)S(1)}, u32[]{:S(2)}, u32[]{:S(2)}) %collective-permute-start.4) | collective-permute-done | bytes 262176 | tf_op jit(solution)/shard_map/ppermute | solution.py:295
  17.4 0.3 add_convert_fusion
  17.7 3.5 %collective-permute-start.10 = (f16[1024,256]{1,0:T(8,128)(2,1)S(1)}, f16[1024,256]{1,0:T(8,128)(2,1)S(1)}, u32[]{:S(2)}, u32[]{:S(2)}) collective-permute-start(f16[1024,256]{1,0:T(8,128)(2,1)S(1)} %add_convert_fusion), channel_id=1, source_target_pairs={{0,192},{32,96},{64,0},{96,160},{128,64},{160,224},{192,128},{224,... | collective-permute-start | bytes 1572872 | tf_op jit(solution)/shard_map/ppermute | solution.py:340
  21.2 3.3 %last_matmul.1 = (f32[1024,256]{1,0:T(8,128)S(1)}, f32[1024,256]{1,0:T(8,128)S(1)}) custom-call(s32[1]{0:T(128)} %bitcast.4.core, s32[1]{0:T(128)} %bitcast.3.owner, bf16[1536,1024]{1,0:T(8,128)(2,1)S(1)} %get-tuple-element.53.kept, bf16[1536,2048]{1,0:T(8,128)(2,1)} %cotangent.5), custom_call_target="tpu_custom_call" | custom-call | flops 1 | bytes 1 | tf_op jit(solution)/shard_map/last_matmul/pallas_call | solution.py:343
  24.5 0.1 convert.15
  24.6 0.1 fusion
  24.7 0.1 collective-permute-start.8
  24.8 0.5 collective-permute-start.7
  25.3 6.7 %collective-permute-done.9 = f16[1024,256]{1,0:T(8,128)(2,1)S(1)} collective-permute-done((f16[1024,256]{1,0:T(8,128)(2,1)S(1)}, f16[1024,256]{1,0:T(8,128)(2,1)S(1)}, u32[]{:S(2)}, u32[]{:S(2)}) %collective-permute-start.9) | collective-permute-done | bytes 524320 | tf_op jit(solution)/shard_map/ppermute | solution.py:337
  32.0 0.3 multiply_reduce_fusion
  32.4 2.8 %collective-permute-start.13 = (f32[1,256]{1,0:T(1,128)S(1)}, f32[1,256]{1,0:T(1,128)S(1)}, u32[]{:S(2)}, u32[]{:S(2)}) collective-permute-start(f32[1,256]{1,0:T(1,128)S(1)} %bitcast.10), channel_id=1, source_target_pairs={{0,24},{8,16},{16,8},{24,0},{1,25},{9,17},{17,9},{25,1},{2,26},{10... | collective-permute-start | bytes 3080 | tf_op jit(solution)/shard_map/ppermute | solution.py:361
  35.2 0.2 collective-permute-start.12
  35.4 1.7 %collective-permute-start.11 = (f32[1,256]{1,0:T(1,128)S(1)}, f32[1,256]{1,0:T(1,128)S(1)}, u32[]{:S(2)}, u32[]{:S(2)}) collective-permute-start(f32[1,256]{1,0:T(1,128)S(1)} %bitcast.12), channel_id=1, source_target_pairs={{0,16},{8,24},{16,0},{24,8},{1,17},{9,25},{17,1},{25,9},{2,18},{10... | collective-permute-start | bytes 3080 | tf_op jit(solution)/shard_map/ppermute | solution.py:359
  37.1 0.4 square_rows.1
  37.6 1.2 %collective-permute-done.12 = f32[1,256]{1,0:T(1,128)S(1)} collective-permute-done((f32[1,256]{1,0:T(1,128)S(1)}, f32[1,256]{1,0:T(1,128)S(1)}, u32[]{:S(2)}, u32[]{:S(2)}) %collective-permute-start.12) | collective-permute-done | bytes 1056 | tf_op jit(solution)/shard_map/ppermute | solution.py:360
  38.8 1.7 %collective-permute-done.11 = f32[1,256]{1,0:T(1,128)S(1)} collective-permute-done((f32[1,256]{1,0:T(1,128)S(1)}, f32[1,256]{1,0:T(1,128)S(1)}, u32[]{:S(2)}, u32[]{:S(2)}) %collective-permute-start.11) | collective-permute-done | bytes 1056 | tf_op jit(solution)/shard_map/ppermute | solution.py:359
  40.5 0.2 weighted_rows.1
  40.7 0.1 collective-permute-start.14
  40.8 1.2 %collective-permute-done.14.came = f32[16,128]{1,0:T(8,128)S(1)} collective-permute-done((f32[16,128]{1,0:T(8,128)S(1)}, f32[16,128]{1,0:T(8,128)S(1)}, u32[]{:S(2)}, u32[]{:S(2)}) %collective-permute-start.14) | collective-permute-done | bytes 8224 | tf_op jit(solution)/shard_map/ppermute | solution.py:378
  42.0 18.6 %all_to_all.5.came = bf16[32,16,128]{2,1,0:T(8,128)(2,1)S(1)} all-to-all(bf16[32,16,128]{2,1,0:T(8,128)(2,1)S(1)} %message.1), channel_id=1, replica_groups=mesh['y'=4,'c'=2,'x'=4,'z'=8] {'y','z'}, dimensions={0} | all-to-all | bytes 262144 | tf_op jit(solution)/shard_map/all_to_all | solution.py:380
  60.6 0.2 row_reduce.1.mine
  60.8 0.1 collective-permute-start.15
  60.9 1.2 %collective-permute-done.15.twin = f32[8,128]{1,0:T(8,128)S(1)} collective-permute-done((f32[8,128]{1,0:T(8,128)S(1)}, f32[8,128]{1,0:T(8,128)S(1)}, u32[]{:S(2)}, u32[]{:S(2)}) %collective-permute-start.15) | collective-permute-done | bytes 4128 | tf_op jit(solution)/shard_map/ppermute | solution.py:390
  62.0 1.1 %collective-permute-start.18 = (f32[8,128]{1,0:T(8,128)S(1)}, f32[8,128]{1,0:T(8,128)S(1)}, u32[]{:S(2)}, u32[]{:S(2)}) collective-permute-start(f32[8,128]{1,0:T(8,128)S(1)} %add.67.scalars_a), channel_id=1, source_target_pairs={{0,24},{8,16},{16,8},{24,0},{1,25},{9,17},{17,9},{25,1},{2,26},{10... | collective-permute-start | bytes 12296 | tf_op jit(solution)/shard_map/ppermute | solution.py:395
  63.2 0.7 collective-permute-start.17
  63.8 2.9 %collective-permute-start.16 = (f32[8,128]{1,0:T(8,128)S(1)}, f32[8,128]{1,0:T(8,128)S(1)}, u32[]{:S(2)}, u32[]{:S(2)}) collective-permute-start(f32[8,128]{1,0:T(8,128)S(1)} %add.67.scalars_a), channel_id=1, source_target_pairs={{0,16},{8,24},{16,0},{24,8},{1,17},{9,25},{17,1},{25,9},{2,18},{10... | collective-permute-start | bytes 12296 | tf_op jit(solution)/shard_map/ppermute | solution.py:393
  66.7 0.7 %normalise.1 = (f32[1024,256]{1,0:T(8,128)S(1)}, f32[8,128]{1,0:T(8,128)}, f32[1,256]{1,0:T(1,128)}) custom-call(s32[1]{0:T(128)} %bitcast.4.core, f32[1024,256]{1,0:T(8,128)S(1)} %get-tuple-element.64.gradient, f32[8,128]{1,0:T(8,128)S(1)} %row_reduce.1.mine, f32[8,128]{1,0:T(8,128)S(1)} %collective-permute-done.15.twin, f32[1,256]{1,0:T(1,128)S(1)} %bitcast.14, ...), custom_call_target="tpu_custom_call" | custom-call | flops 1 | bytes 1 | tf_op jit(solution)/shard_map/normalise/pallas_call | solution.py:48
  67.4 1.5 %collective-permute-done.16 = f32[8,128]{1,0:T(8,128)S(1)} collective-permute-done((f32[8,128]{1,0:T(8,128)S(1)}, f32[8,128]{1,0:T(8,128)S(1)}, u32[]{:S(2)}, u32[]{:S(2)}) %collective-permute-start.16) | collective-permute-done | bytes 4128 | tf_op jit(solution)/shard_map/ppermute | solution.py:393
  69.0 1.1 %step.1 = f32[1024,256]{1,0:T(8,128)} custom-call(f32[8,128]{1,0:T(8,128)S(1)} %add.67.scalars_a, f32[8,128]{1,0:T(8,128)S(1)} %add_add_fusion.scalars_b, f32[1024,256]{1,0:T(8,128)S(1)} %copy-done, f32[1024,256]{1,0:T(8,128)S(1)} %get-tuple-element.60.update), custom_call_target="tpu_custom_call" | custom-call | flops 1 | bytes 1 | tf_op jit(solution)/shard_map/step/pallas_call | solution.py:408
  (23 shorter events, 0.1 us)
Async XLA Ops:
  4.0 3.2 %collective-permute-start = (f16[1024,256]{1,0:T(8,128)(2,1)S(1)}, f16[1024,256]{1,0:T(8,128)(2,1)S(1)}, u32[]{:S(2)}, u32[]{:S(2)}) collective-permute-start(f16[1024,256]{1,0:T(8,128)(2,1)S(1)} %convert_element_type.40), channel_id=1, source_target_pairs={{0,32},{32,0},{1,33},{33,1},{2,34},{34,2},{3,35},{35,3},{4,36},{36... | collective-permute-start | bytes 1572872 | tf_op jit(solution)/shard_map/ppermute | solution.py:295
  7.4 10.0 %collective-permute-start.6 = (f16[1024,256]{1,0:T(8,128)(2,1)S(1)}, f16[1024,256]{1,0:T(8,128)(2,1)S(1)}, u32[]{:S(2)}, u32[]{:S(2)}) collective-permute-start(f16[1024,256]{1,0:T(8,128)(2,1)S(1)} %add_convert_fusion.2), channel_id=1, source_target_pairs={{0,192},{32,96},{64,0},{96,160},{128,64},{160,224},{192,128},{224,... | collective-permute-start | bytes 1572872 | tf_op jit(solution)/shard_map/ppermute | solution.py:326
  12.6 3.2 %collective-permute-start.2 = (f16[336,256]{1,0:T(8,128)(2,1)S(1)}, f16[336,256]{1,0:T(8,128)(2,1)S(1)}, u32[]{:S(2)}, u32[]{:S(2)}) collective-permute-start(f16[336,256]{1,0:T(8,128)(2,1)S(1)} %get-tuple-element.70), channel_id=1, source_target_pairs={{0,32},{32,0},{1,33},{33,1},{2,34},{34,2},{3,35},{35,3},{4,36},{36... | collective-permute-start | bytes 516104 | tf_op jit(solution)/shard_map/ppermute | solution.py:295
  12.7 3.3 %collective-permute-start.1 = (f16[336,256]{1,0:T(8,128)(2,1)S(1)}, f16[336,256]{1,0:T(8,128)(2,1)S(1)}, u32[]{:S(2)}, u32[]{:S(2)}) collective-permute-start(f16[336,256]{1,0:T(8,128)(2,1)S(1)} %get-tuple-element.69), channel_id=1, source_target_pairs={{0,32},{32,0},{1,33},{33,1},{2,34},{34,2},{3,35},{35,3},{4,36},{36... | collective-permute-start | bytes 516104 | tf_op jit(solution)/shard_map/ppermute | solution.py:295
  13.2 2.8 %collective-permute-start.3 = (f16[352,256]{1,0:T(8,128)(2,1)S(1)}, f16[352,256]{1,0:T(8,128)(2,1)S(1)}, u32[]{:S(2)}, u32[]{:S(2)}) collective-permute-start(f16[352,256]{1,0:T(8,128)(2,1)S(1)} %slice.37), channel_id=1, source_target_pairs={{0,32},{32,0},{1,33},{33,1},{2,34},{34,2},{3,35},{35,3},{4,36},{36... | collective-permute-start | bytes 540680 | tf_op jit(solution)/shard_map/ppermute | solution.py:295
  13.4 3.2 %collective-permute-start.5 = (f16[512,256]{1,0:T(8,128)(2,1)S(1)}, f16[512,256]{1,0:T(8,128)(2,1)S(1)}, u32[]{:S(2)}, u32[]{:S(2)}) collective-permute-start(f16[512,256]{1,0:T(8,128)(2,1)S(1)} %get-tuple-element.68), channel_id=1, source_target_pairs={{0,32},{32,0},{1,33},{33,1},{2,34},{34,2},{3,35},{35,3},{4,36},{36... | collective-permute-start | bytes 786440 | tf_op jit(solution)/shard_map/ppermute | solution.py:295
  15.8 1.6 %collective-permute-start.4 = (f16[512,256]{1,0:T(8,128)(2,1)S(1)}, f16[512,256]{1,0:T(8,128)(2,1)S(1)}, u32[]{:S(2)}, u32[]{:S(2)}) collective-permute-start(f16[512,256]{1,0:T(8,128)(2,1)S(1)} %get-tuple-element.67), channel_id=1, source_target_pairs={{0,32},{32,0},{1,33},{33,1},{2,34},{34,2},{3,35},{35,3},{4,36},{36... | collective-permute-start | bytes 786440 | tf_op jit(solution)/shard_map/ppermute | solution.py:295
  16.2 15.8 %collective-permute-start.9 = (f16[1024,256]{1,0:T(8,128)(2,1)S(1)}, f16[1024,256]{1,0:T(8,128)(2,1)S(1)}, u32[]{:S(2)}, u32[]{:S(2)}) collective-permute-start(f16[1024,256]{1,0:T(8,128)(2,1)S(1)} %add_convert_fusion.1), channel_id=1, source_target_pairs={{0,64},{32,224},{64,128},{96,32},{128,192},{160,96},{192,0},{224,1... | collective-permute-start | bytes 1572872 | tf_op jit(solution)/shard_map/ppermute | solution.py:337
  17.7 14.3 %collective-permute-start.10 = (f16[1024,256]{1,0:T(8,128)(2,1)S(1)}, f16[1024,256]{1,0:T(8,128)(2,1)S(1)}, u32[]{:S(2)}, u32[]{:S(2)}) collective-permute-start(f16[1024,256]{1,0:T(8,128)(2,1)S(1)} %add_convert_fusion), channel_id=1, source_target_pairs={{0,192},{32,96},{64,0},{96,160},{128,64},{160,224},{192,128},{224,... | collective-permute-start | bytes 1572872 | tf_op jit(solution)/shard_map/ppermute | solution.py:340
  24.5 12.7 %copy-start = (f32[1024,256]{1,0:T(8,128)S(1)}, f32[1024,256]{1,0:T(8,128)}, u32[]{:S(2)}) copy-start(f32[1024,256]{1,0:T(8,128)} %param.13) | copy-start | bytes 3145732
  24.7 15.8 %copy-start.1 = (f32[256]{0:T(256)S(1)}, f32[256]{0:T(256)}, u32[]{:S(2)}) copy-start(f32[256]{0:T(256)} %param.11) | copy-start | bytes 3076
  24.7 7.3 %collective-permute-start.8 = (f16[512,256]{1,0:T(8,128)(2,1)S(1)}, f16[512,256]{1,0:T(8,128)(2,1)S(1)}, u32[]{:S(2)}, u32[]{:S(2)}) collective-permute-start(f16[512,256]{1,0:T(8,128)(2,1)S(1)} %get-tuple-element.66), channel_id=1, source_target_pairs={{0,32},{32,0},{1,33},{33,1},{2,34},{34,2},{3,35},{35,3},{4,36},{36... | collective-permute-start | bytes 786440 | tf_op jit(solution)/shard_map/ppermute | solution.py:295
  24.8 7.2 %collective-permute-start.7 = (f16[512,256]{1,0:T(8,128)(2,1)S(1)}, f16[512,256]{1,0:T(8,128)(2,1)S(1)}, u32[]{:S(2)}, u32[]{:S(2)}) collective-permute-start(f16[512,256]{1,0:T(8,128)(2,1)S(1)} %get-tuple-element.65), channel_id=1, source_target_pairs={{0,32},{32,0},{1,33},{33,1},{2,34},{34,2},{3,35},{35,3},{4,36},{36... | collective-permute-start | bytes 786440 | tf_op jit(solution)/shard_map/ppermute | solution.py:295
  32.0 28.6 %copy-start.2 = (f32[1024]{0:T(1024)S(1)}, f32[1024]{0:T(1024)}, u32[]{:S(2)}) copy-start(f32[1024]{0:T(1024)} %param.10) | copy-start | bytes 12292
  32.4 5.2 %collective-permute-start.13 = (f32[1,256]{1,0:T(1,128)S(1)}, f32[1,256]{1,0:T(1,128)S(1)}, u32[]{:S(2)}, u32[]{:S(2)}) collective-permute-start(f32[1,256]{1,0:T(1,128)S(1)} %bitcast.10), channel_id=1, source_target_pairs={{0,24},{8,16},{16,8},{24,0},{1,25},{9,17},{17,9},{25,1},{2,26},{10... | collective-permute-start | bytes 3080 | tf_op jit(solution)/shard_map/ppermute | solution.py:361
  35.2 3.6 %collective-permute-start.12 = (f32[1,256]{1,0:T(1,128)S(1)}, f32[1,256]{1,0:T(1,128)S(1)}, u32[]{:S(2)}, u32[]{:S(2)}) collective-permute-start(f32[1,256]{1,0:T(1,128)S(1)} %bitcast.11), channel_id=1, source_target_pairs={{0,8},{8,0},{16,24},{24,16},{1,9},{9,1},{17,25},{25,17},{2,10},{10... | collective-permute-start | bytes 3080 | tf_op jit(solution)/shard_map/ppermute | solution.py:360
  35.4 5.1 %collective-permute-start.11 = (f32[1,256]{1,0:T(1,128)S(1)}, f32[1,256]{1,0:T(1,128)S(1)}, u32[]{:S(2)}, u32[]{:S(2)}) collective-permute-start(f32[1,256]{1,0:T(1,128)S(1)} %bitcast.12), channel_id=1, source_target_pairs={{0,16},{8,24},{16,0},{24,8},{1,17},{9,25},{17,1},{25,9},{2,18},{10... | collective-permute-start | bytes 3080 | tf_op jit(solution)/shard_map/ppermute | solution.py:359
  40.7 1.3 %collective-permute-start.14 = (f32[16,128]{1,0:T(8,128)S(1)}, f32[16,128]{1,0:T(8,128)S(1)}, u32[]{:S(2)}, u32[]{:S(2)}) collective-permute-start(f32[16,128]{1,0:T(8,128)S(1)} %get-tuple-element.59), channel_id=1, source_target_pairs={{0,32},{32,0},{1,33},{33,1},{2,34},{34,2},{3,35},{35,3},{4,36},{36... | collective-permute-start | bytes 24584 | tf_op jit(solution)/shard_map/ppermute | solution.py:378
  60.8 1.3 %collective-permute-start.15 = (f32[8,128]{1,0:T(8,128)S(1)}, f32[8,128]{1,0:T(8,128)S(1)}, u32[]{:S(2)}, u32[]{:S(2)}) collective-permute-start(f32[8,128]{1,0:T(8,128)S(1)} %row_reduce.1.mine), channel_id=1, source_target_pairs={{0,32},{32,0},{1,33},{33,1},{2,34},{34,2},{3,35},{35,3},{4,36},{36... | collective-permute-start | bytes 12296 | tf_op jit(solution)/shard_map/ppermute | solution.py:390
  62.0 5.4 %collective-permute-start.18 = (f32[8,128]{1,0:T(8,128)S(1)}, f32[8,128]{1,0:T(8,128)S(1)}, u32[]{:S(2)}, u32[]{:S(2)}) collective-permute-start(f32[8,128]{1,0:T(8,128)S(1)} %add.67.scalars_a), channel_id=1, source_target_pairs={{0,24},{8,16},{16,8},{24,0},{1,25},{9,17},{17,9},{25,1},{2,26},{10... | collective-permute-start | bytes 12296 | tf_op jit(solution)/shard_map/ppermute | solution.py:395
  63.2 4.3 %collective-permute-start.17 = (f32[8,128]{1,0:T(8,128)S(1)}, f32[8,128]{1,0:T(8,128)S(1)}, u32[]{:S(2)}, u32[]{:S(2)}) collective-permute-start(f32[8,128]{1,0:T(8,128)S(1)} %add.67.scalars_a), channel_id=1, source_target_pairs={{0,8},{8,0},{16,24},{24,16},{1,9},{9,1},{17,25},{25,17},{2,10},{10... | collective-permute-start | bytes 12296 | tf_op jit(solution)/shard_map/ppermute | solution.py:394
  63.8 5.1 %collective-permute-start.16 = (f32[8,128]{1,0:T(8,128)S(1)}, f32[8,128]{1,0:T(8,128)S(1)}, u32[]{:S(2)}, u32[]{:S(2)}) collective-permute-start(f32[8,128]{1,0:T(8,128)S(1)} %add.67.scalars_a), channel_id=1, source_target_pairs={{0,16},{8,24},{16,0},{24,8},{1,17},{9,25},{17,1},{25,9},{2,18},{10... | collective-permute-start | bytes 12296 | tf_op jit(solution)/shard_map/ppermute | solution.py:393

commit v5 on v4

--- a/solution.py
+++ b/solution.py
@@ -41,6 +41,7 @@
 FIRST_LIMIT = 48 * 2**20
 SECOND_LIMIT = 43 * 2**20
 LAST_LIMIT = 43 * 2**20
+MIDDLE_LIMIT = 42 * 2**20
 NO_COST = pl.CostEstimate(flops=1, bytes_accessed=1, transcendentals=0)
 
 
@@ -117,16 +118,24 @@
 
 
 def second_kernel(
-    core, behind, ahead, kept, pair, cotangent, out, a, b, mine_a, mine_b, *landed
+    core, behind, ahead, kept, pair, cotangent, out, a, b, mine, landed_a, landed_b, landed
 ):
-    loads = block_loads(ahead, behind, 1 - core[0], cotangent, a, b, *landed[:2])
-    loads += block_loads(behind, ahead, core[0], cotangent, mine_a, mine_b, *landed[2:])
+    loads = block_loads(ahead, behind, 1 - core[0], cotangent, a, b, landed_a, landed_b)
+    loads += column_copies(ahead[0] * C + core[0], OWN, cotangent, mine, landed)
     start_all(loads)
     out[...] = product(kept[...], pair[:, core_columns(core[0])])
     wait_all(loads)
 
 
-def two_kernel(kept, a, b, out_a, out_b):
+def third_kernel(core, behind, kept, a, b, cotangent, out_a, out_b, mine, landed):
+    loads = column_copies(behind[0] * C + core[0], OWN, cotangent, mine, landed)
+    start_all(loads)
+    out_a[...] = product(kept[...], a[...])
+    out_b[...] = product(kept[...], b[...])
+    wait_all(loads)
+
+
+def fourth_kernel(kept, a, b, out_a, out_b):
     out_a[...] = product(kept[...], a[...])
     out_b[...] = product(kept[...], b[...])
 
@@ -308,13 +317,13 @@
         cotangent,
     )
     far_came = swapped(far_away, 1)
-    far, away_a, away_b, mine_a, mine_b = loading_call(
+    far, away_a, away_b, mine_b = loading_call(
         second_kernel,
         "second_matmul",
         SECOND_LIMIT,
         [SMEM, SMEM, SMEM, VMEM, VMEM, HBM],
-        [BLOCK, HALF, HALF, HALF, HALF],
-        [STEPS] * 4,
+        [BLOCK, HALF, HALF, HALF],
+        [STEPS] * 3,
         core,
         hops[1],
         hops[2],
@@ -326,13 +335,23 @@
     far_sent = lax.ppermute(far, ("y", "c"), to_ahead)
 
     away_a, _ = barrier((away_a, far))
-    behind_away, ahead_away = call(
-        two_kernel, "third_matmul", [BLOCK, BLOCK], kept, away_a, away_b
+    behind_away, ahead_away, mine_a = loading_call(
+        third_kernel,
+        "third_matmul",
+        MIDDLE_LIMIT,
+        [SMEM, SMEM, VMEM, VMEM, VMEM, HBM],
+        [BLOCK, BLOCK, HALF],
+        [STEPS],
+        core,
+        hops[1],
+        kept,
+        away_a,
+        away_b,
+        cotangent,
     )
     behind_came = swapped(behind_away, 3)
-    ahead_came = swapped(ahead_away, 2)
-    mine_a, _, _ = barrier((mine_a, behind_away, ahead_away))
-    behind, ahead = call(two_kernel, "fourth_matmul", [BLOCK, BLOCK], kept, mine_a, mine_b)
+    ahead_came = swapped(ahead_away, 1)
+    behind, ahead = call(fourth_kernel, "fourth_matmul", [BLOCK, BLOCK], kept, mine_a, mine_b)
     behind = narrow(behind + behind_came)
     behind_sent = lax.ppermute(behind, ("y", "c"), to_behind)
     ahead, _ = barrier((ahead, behind))
@@ -356,9 +375,9 @@
     col_part = jnp.sum(gradient * gradient, axis=0)
     col_part = col_part.reshape(1, OWN)
     col_came = (
-        lax.ppermute(col_part, "x", pair_cross)
-        + lax.ppermute(col_part, "x", pair_near)
+        lax.ppermute(col_part, "x", pair_near)
         + lax.ppermute(col_part, "x", pair_wrap)
+        + lax.ppermute(col_part, "x", pair_cross)
     )
     mine, away = call(
         square_rows_kernel, "square_rows", [TILE32, TILE32], core, gradient, param, scalars=1
@@ -390,9 +409,9 @@
     twin = lax.ppermute(reduced, "c", swap_core)
     scalars = reduced + twin
     scalars_came = (
-        lax.ppermute(scalars, "x", pair_cross)
-        + lax.ppermute(scalars, "x", pair_near)
+        lax.ppermute(scalars, "x", pair_near)
         + lax.ppermute(scalars, "x", pair_wrap)
+        + lax.ppermute(scalars, "x", pair_cross)
     )
     update, new_row, new_col = call(
         normalise_kernel,

time: 70.9 us -> 69.3 us (0.977)
  starting transfers between devices: 18.8 us -> 17 us
    ppermute x1, waiting for transfers between devices: 0.01 us -> 2.72 us  [per_device(): lax.ppermute(col_part, 'x', pair_wrap)]
    pallas_call x7 -> x6, Pallas kernels: 5.24 us -> 3.39 us  [call(): pl.pallas_call(kernel, name=name, in_specs=[SMEM] * scalars + [VMEM] * (l...]
    ppermute x1, starting transfers between devices: 2.85 us -> 1.15 us  [per_device(): lax.ppermute(col_part, 'x', pair_wrap)]
    pallas_call x2 -> x3, Pallas kernels: 6.3 us -> 7.8 us  [loading_call(): pl.pallas_call(kernel, name=name, in_specs=in_specs, out_specs=[VMEM] * l...]
    ppermute x1, starting transfers between devices: 2.89 us -> 1.46 us  [per_device(): lax.ppermute(scalars, 'x', pair_cross)]
    ppermute x1, starting transfers between devices: 1.71 us -> 3.1 us  [per_device(): lax.ppermute(col_part, 'x', pair_cross)]
    ppermute x1, waiting for transfers between devices: 1.73 us -> 0.47 us  [per_device(): lax.ppermute(col_part, 'x', pair_cross)]
    ppermute x1, waiting for transfers between devices: 1.19 us -> 0.01 us  [per_device(): lax.ppermute(col_part, 'x', pair_near)]
  transfers between devices with their start and end apart: 19 -> 18, of which waited for: 7 -> 8; matrix products, arithmetic and copies ran while one was open for 2% -> 1% of each run, Pallas kernels for 16% -> 16%
where the time goes in v5:
time: 69.3 us; the launch traced here: 68.4 us
  blocking collectives  18.6 us (27%)
  starting transfers between devices  17 us (25%)
  Pallas kernels  15.5 us (22%)
  waiting for transfers between devices  14.8 us (21%)
  other arithmetic  1.36 us (2%)
  between operations  1.01 us (1%)
    all_to_all x1, blocking collectives, per_device(): came = lax.all_to_all(message, ('y', 'z'), 0, 0, tiled=True)  18.6 us
    pallas_call x3, Pallas kernels, loading_call(): pl.pallas_call(kernel, name=name, in_specs=in_specs, out_specs=[VMEM] * l...  7.8 us
    ppermute x1, waiting for transfers between devices, per_device(): behind_sent = lax.ppermute(behind, ('y', 'c'), to_behind)  6.16 us
    ppermute x1, starting transfers between devices, per_device(): ahead_sent = lax.ppermute(ahead, ('y', 'c'), to_ahead)  3.95 us
    pallas_call x6, Pallas kernels, call(): pl.pallas_call(kernel, name=name, in_specs=[SMEM] * scalars + [VMEM] * (l...  3.39 us
    pallas_call x1, Pallas kernels, per_device(): pl.pallas_call(last_kernel, name='last_matmul', in_specs=[SMEM, SMEM, VME...  3.25 us
    ppermute x1, starting transfers between devices, per_device(): lax.ppermute(col_part, 'x', pair_cross)  3.1 us
    ppermute x1, starting transfers between devices, per_device(): far_sent = lax.ppermute(far, ('y', 'c'), to_ahead)  3.09 us
  transfers between devices with their start and end apart: 18, of which 8 were waited for; matrix products, arithmetic and copies ran while one was open for 1% of the time, Pallas kernels for 16%

profile of v5, /device:TPU:32, one launch (start us, length us, event | category | flops | bytes accessed | tf_op | source)
XLA Modules:
  0.0 68.4 jit_solution(13787311460871939911)
XLA Ops:
  0.6 3.3 %first_matmul.1 = (f32[1024,256]{1,0:T(8,128)S(1)}, bf16[1536,1024]{1,0:T(8,128)(2,1)S(1)}, bf16[1536,512]{1,0:T(8,128)(2,1)S(1)}) custom-call(s32[1]{0:T(128)} %bitcast.owner, s32[1]{0:T(128)} %bitcast.4.core, bf16[1536,1024]{1,0:T(8,128)(2,1)} %activations.1, bf16[1536,2048]{1,0:T(8,128)(2,1)} %cotangent.7), custom_call_target="tpu_custom_call" | custom-call | flops 1 | bytes 1 | tf_op jit(solution)/shard_map/first_matmul/pallas_call | solution.py:158
  3.9 0.1 convert_element_type.41
  4.0 0.1 collective-permute-start
  4.1 2.6 %second_matmul.1 = (f32[1024,256]{1,0:T(8,128)S(1)}, bf16[1536,256]{1,0:T(8,128)(2,1)S(1)}, bf16[1536,256]{1,0:T(8,128)(2,1)S(1)}, bf16[1536,256]{1,0:T(8,128)(2,1)S(1)}) custom-call(s32[1]{0:T(128)} %bitcast.4.core, s32[1]{0:T(128)} %bitcast.1.behind, s32[1]{0:T(128)} %bitcast.2.ahead, bf16[1536,1024]{1,0:T(8,128)(2,1)S(1)} %get-tuple-element.51.kept, ...), custom_call_target="tpu_custom_call" | custom-call | flops 1 | bytes 1 | tf_op jit(solution)/shard_map/second_matmul/pallas_call | solution.py:158
  6.8 0.2 add_convert_fusion.2
  6.9 3.1 %collective-permute-start.5 = (f16[1024,256]{1,0:T(8,128)(2,1)S(1)}, f16[1024,256]{1,0:T(8,128)(2,1)S(1)}, u32[]{:S(2)}, u32[]{:S(2)}) collective-permute-start(f16[1024,256]{1,0:T(8,128)(2,1)S(1)} %add_convert_fusion.2), channel_id=1, source_target_pairs={{0,192},{32,96},{64,0},{96,160},{128,64},{160,224},{192,128},{224,... | collective-permute-start | bytes 1572872 | tf_op jit(solution)/shard_map/ppermute | solution.py:335
  10.0 1.9 %third_matmul.1 = (f32[1024,256]{1,0:T(8,128)S(1)}, f32[1024,256]{1,0:T(8,128)S(1)}, bf16[1536,256]{1,0:T(8,128)(2,1)S(1)}) custom-call(s32[1]{0:T(128)} %bitcast.4.core, s32[1]{0:T(128)} %bitcast.1.behind, bf16[1536,1024]{1,0:T(8,128)(2,1)S(1)} %get-tuple-element.51.kept, bf16[1536,256]{1,0:T(8,128)(2,1)S(1)} %get-tuple-element.42.a, ...), custom_call_target="tpu_custom_call" | custom-call | flops 1 | bytes 1 | tf_op jit(solution)/shard_map/third_matmul/pallas_call | solution.py:158
  11.9 0.1 convert.9
  12.1 0.1 collective-permute-start.3
  12.2 0.1 convert_element_type.46
  12.3 0.6 collective-permute-start.4
  12.8 0.1 fusion.1
  12.9 0.1 collective-permute-start.2
  13.0 0.5 collective-permute-start.1
  13.5 1.9 %fourth_matmul.1 = (f32[1024,256]{1,0:T(8,128)S(1)}, f32[1024,256]{1,0:T(8,128)S(1)}) custom-call(bf16[1536,1024]{1,0:T(8,128)(2,1)S(1)} %get-tuple-element.51.kept, bf16[1536,256]{1,0:T(8,128)(2,1)S(1)} %get-tuple-element.44.a, bf16[1536,256]{1,0:T(8,128)(2,1)S(1)} %get-tuple-element.45.b), custom_call_target="tpu_custom_call" | custom-call | flops 1 | bytes 1 | tf_op jit(solution)/shard_map/fourth_matmul/pallas_call | solution.py:49
  15.4 0.2 add_convert_fusion.1
  15.6 0.1 collective-permute-start.8
  15.7 1.0 %collective-permute-done.5 = f16[1024,256]{1,0:T(8,128)(2,1)S(1)} collective-permute-done((f16[1024,256]{1,0:T(8,128)(2,1)S(1)}, f16[1024,256]{1,0:T(8,128)(2,1)S(1)}, u32[]{:S(2)}, u32[]{:S(2)}) %collective-permute-start.5) | collective-permute-done | bytes 524320 | tf_op jit(solution)/shard_map/ppermute | solution.py:335
  16.7 0.2 add_convert_fusion
  17.0 3.9 %collective-permute-start.9 = (f16[1024,256]{1,0:T(8,128)(2,1)S(1)}, f16[1024,256]{1,0:T(8,128)(2,1)S(1)}, u32[]{:S(2)}, u32[]{:S(2)}) collective-permute-start(f16[1024,256]{1,0:T(8,128)(2,1)S(1)} %add_convert_fusion), channel_id=1, source_target_pairs={{0,192},{32,96},{64,0},{96,160},{128,64},{160,224},{192,128},{224,... | collective-permute-start | bytes 1572872 | tf_op jit(solution)/shard_map/ppermute | solution.py:359
  20.9 3.3 %last_matmul.1 = (f32[1024,256]{1,0:T(8,128)S(1)}, f32[1024,256]{1,0:T(8,128)S(1)}) custom-call(s32[1]{0:T(128)} %bitcast.4.core, s32[1]{0:T(128)} %bitcast.3.owner, bf16[1536,1024]{1,0:T(8,128)(2,1)S(1)} %get-tuple-element.51.kept, bf16[1536,2048]{1,0:T(8,128)(2,1)} %cotangent.7), custom_call_target="tpu_custom_call" | custom-call | flops 1 | bytes 1 | tf_op jit(solution)/shard_map/last_matmul/pallas_call | solution.py:362
  24.2 0.0 copy-start
  24.2 0.1 convert.10
  24.3 0.1 fusion
  24.4 0.0 copy-start.1
  24.4 0.1 collective-permute-start.7
  24.5 0.5 collective-permute-start.6
  25.0 6.2 %collective-permute-done.8 = f16[1024,256]{1,0:T(8,128)(2,1)S(1)} collective-permute-done((f16[1024,256]{1,0:T(8,128)(2,1)S(1)}, f16[1024,256]{1,0:T(8,128)(2,1)S(1)}, u32[]{:S(2)}, u32[]{:S(2)}) %collective-permute-start.8) | collective-permute-done | bytes 524320 | tf_op jit(solution)/shard_map/ppermute | solution.py:356
  31.2 0.4 multiply_reduce_fusion
  31.6 3.1 %collective-permute-start.12 = (f32[1,256]{1,0:T(1,128)S(1)}, f32[1,256]{1,0:T(1,128)S(1)}, u32[]{:S(2)}, u32[]{:S(2)}) collective-permute-start(f32[1,256]{1,0:T(1,128)S(1)} %bitcast.10), channel_id=1, source_target_pairs={{0,16},{8,24},{16,0},{24,8},{1,17},{9,25},{17,1},{25,9},{2,18},{10... | collective-permute-start | bytes 3080 | tf_op jit(solution)/shard_map/ppermute | solution.py:380
  34.6 1.1 %collective-permute-start.11 = (f32[1,256]{1,0:T(1,128)S(1)}, f32[1,256]{1,0:T(1,128)S(1)}, u32[]{:S(2)}, u32[]{:S(2)}) collective-permute-start(f32[1,256]{1,0:T(1,128)S(1)} %bitcast.11), channel_id=1, source_target_pairs={{0,24},{8,16},{16,8},{24,0},{1,25},{9,17},{17,9},{25,1},{2,26},{10... | collective-permute-start | bytes 3080 | tf_op jit(solution)/shard_map/ppermute | solution.py:379
  35.8 0.4 square_rows.1
  36.2 0.5 collective-permute-done.12
  36.7 2.7 %collective-permute-done.11 = f32[1,256]{1,0:T(1,128)S(1)} collective-permute-done((f32[1,256]{1,0:T(1,128)S(1)}, f32[1,256]{1,0:T(1,128)S(1)}, u32[]{:S(2)}, u32[]{:S(2)}) %collective-permute-start.11) | collective-permute-done | bytes 1056 | tf_op jit(solution)/shard_map/ppermute | solution.py:379
  39.4 0.2 weighted_rows.1
  39.7 0.1 collective-permute-start.13
  39.8 1.2 %collective-permute-done.13.came = f32[16,128]{1,0:T(8,128)S(1)} collective-permute-done((f32[16,128]{1,0:T(8,128)S(1)}, f32[16,128]{1,0:T(8,128)S(1)}, u32[]{:S(2)}, u32[]{:S(2)}) %collective-permute-start.13) | collective-permute-done | bytes 8224 | tf_op jit(solution)/shard_map/ppermute | solution.py:397
  40.9 18.6 %all_to_all.5.came = bf16[32,16,128]{2,1,0:T(8,128)(2,1)S(1)} all-to-all(bf16[32,16,128]{2,1,0:T(8,128)(2,1)S(1)} %message.1), channel_id=1, replica_groups=mesh['y'=4,'c'=2,'x'=4,'z'=8] {'y','z'}, dimensions={0} | all-to-all | bytes 262144 | tf_op jit(solution)/shard_map/all_to_all | solution.py:399
  59.5 0.2 row_reduce.1.mine
  59.7 0.1 collective-permute-start.14
  59.8 1.2 %collective-permute-done.14.twin = f32[8,128]{1,0:T(8,128)S(1)} collective-permute-done((f32[8,128]{1,0:T(8,128)S(1)}, f32[8,128]{1,0:T(8,128)S(1)}, u32[]{:S(2)}, u32[]{:S(2)}) %collective-permute-start.14) | collective-permute-done | bytes 4128 | tf_op jit(solution)/shard_map/ppermute | solution.py:409
  60.9 1.5 %collective-permute-start.17 = (f32[8,128]{1,0:T(8,128)S(1)}, f32[8,128]{1,0:T(8,128)S(1)}, u32[]{:S(2)}, u32[]{:S(2)}) collective-permute-start(f32[8,128]{1,0:T(8,128)S(1)} %add.67.scalars_a), channel_id=1, source_target_pairs={{0,16},{8,24},{16,0},{24,8},{1,17},{9,25},{17,1},{25,9},{2,18},{10... | collective-permute-start | bytes 12296 | tf_op jit(solution)/shard_map/ppermute | solution.py:414
  62.4 1.2 %collective-permute-start.16 = (f32[8,128]{1,0:T(8,128)S(1)}, f32[8,128]{1,0:T(8,128)S(1)}, u32[]{:S(2)}, u32[]{:S(2)}) collective-permute-start(f32[8,128]{1,0:T(8,128)S(1)} %add.67.scalars_a), channel_id=1, source_target_pairs={{0,24},{8,16},{16,8},{24,0},{1,25},{9,17},{17,9},{25,1},{2,26},{10... | collective-permute-start | bytes 12296 | tf_op jit(solution)/shard_map/ppermute | solution.py:413
  63.5 0.9 %collective-permute-start.15 = (f32[8,128]{1,0:T(8,128)S(1)}, f32[8,128]{1,0:T(8,128)S(1)}, u32[]{:S(2)}, u32[]{:S(2)}) collective-permute-start(f32[8,128]{1,0:T(8,128)S(1)} %add.67.scalars_a), channel_id=1, source_target_pairs={{0,8},{8,0},{16,24},{24,16},{1,9},{9,1},{17,25},{25,17},{2,10},{10... | collective-permute-start | bytes 12296 | tf_op jit(solution)/shard_map/ppermute | solution.py:412
  64.4 0.7 %normalise.1 = (f32[1024,256]{1,0:T(8,128)S(1)}, f32[8,128]{1,0:T(8,128)}, f32[1,256]{1,0:T(1,128)}) custom-call(s32[1]{0:T(128)} %bitcast.4.core, f32[1024,256]{1,0:T(8,128)S(1)} %get-tuple-element.62.gradient, f32[8,128]{1,0:T(8,128)S(1)} %row_reduce.1.mine, f32[8,128]{1,0:T(8,128)S(1)} %collective-permute-done.14.twin, f32[1,256]{1,0:T(1,128)S(1)} %bitcast.14, ...), custom_call_target="tpu_custom_call" | custom-call | flops 1 | bytes 1 | tf_op jit(solution)/shard_map/normalise/pallas_call | solution.py:49
  65.1 0.9 %collective-permute-done.17 = f32[8,128]{1,0:T(8,128)S(1)} collective-permute-done((f32[8,128]{1,0:T(8,128)S(1)}, f32[8,128]{1,0:T(8,128)S(1)}, u32[]{:S(2)}, u32[]{:S(2)}) %collective-permute-start.17) | collective-permute-done | bytes 4128 | tf_op jit(solution)/shard_map/ppermute | solution.py:414
  66.0 1.2 %collective-permute-done.16 = f32[8,128]{1,0:T(8,128)S(1)} collective-permute-done((f32[8,128]{1,0:T(8,128)S(1)}, f32[8,128]{1,0:T(8,128)S(1)}, u32[]{:S(2)}, u32[]{:S(2)}) %collective-permute-start.16) | collective-permute-done | bytes 4128 | tf_op jit(solution)/shard_map/ppermute | solution.py:413
  67.2 1.1 %step.1 = f32[1024,256]{1,0:T(8,128)} custom-call(f32[8,128]{1,0:T(8,128)S(1)} %add.67.scalars_a, f32[8,128]{1,0:T(8,128)S(1)} %add_add_fusion.scalars_b, f32[1024,256]{1,0:T(8,128)S(1)} %copy-done, f32[1024,256]{1,0:T(8,128)S(1)} %get-tuple-element.58.update), custom_call_target="tpu_custom_call" | custom-call | flops 1 | bytes 1 | tf_op jit(solution)/shard_map/step/pallas_call | solution.py:427
  (20 shorter events, 0.1 us)
Async XLA Ops:
  4.0 2.8 %collective-permute-start = (f16[1024,256]{1,0:T(8,128)(2,1)S(1)}, f16[1024,256]{1,0:T(8,128)(2,1)S(1)}, u32[]{:S(2)}, u32[]{:S(2)}) collective-permute-start(f16[1024,256]{1,0:T(8,128)(2,1)S(1)} %convert_element_type.41), channel_id=1, source_target_pairs={{0,32},{32,0},{1,33},{33,1},{2,34},{34,2},{3,35},{35,3},{4,36},{36... | collective-permute-start | bytes 1572872 | tf_op jit(solution)/shard_map/ppermute | solution.py:304
  6.9 9.8 %collective-permute-start.5 = (f16[1024,256]{1,0:T(8,128)(2,1)S(1)}, f16[1024,256]{1,0:T(8,128)(2,1)S(1)}, u32[]{:S(2)}, u32[]{:S(2)}) collective-permute-start(f16[1024,256]{1,0:T(8,128)(2,1)S(1)} %add_convert_fusion.2), channel_id=1, source_target_pairs={{0,192},{32,96},{64,0},{96,160},{128,64},{160,224},{192,128},{224,... | collective-permute-start | bytes 1572872 | tf_op jit(solution)/shard_map/ppermute | solution.py:335
  12.1 3.3 %collective-permute-start.3 = (f16[352,256]{1,0:T(8,128)(2,1)S(1)}, f16[352,256]{1,0:T(8,128)(2,1)S(1)}, u32[]{:S(2)}, u32[]{:S(2)}) collective-permute-start(f16[352,256]{1,0:T(8,128)(2,1)S(1)} %slice.27), channel_id=1, source_target_pairs={{0,32},{32,0},{1,33},{33,1},{2,34},{34,2},{3,35},{35,3},{4,36},{36... | collective-permute-start | bytes 540680 | tf_op jit(solution)/shard_map/ppermute | solution.py:304
  12.3 4.5 %collective-permute-start.4 = (f16[1024,256]{1,0:T(8,128)(2,1)S(1)}, f16[1024,256]{1,0:T(8,128)(2,1)S(1)}, u32[]{:S(2)}, u32[]{:S(2)}) collective-permute-start(f16[1024,256]{1,0:T(8,128)(2,1)S(1)} %convert_element_type.46), channel_id=1, source_target_pairs={{0,32},{32,0},{1,33},{33,1},{2,34},{34,2},{3,35},{35,3},{4,36},{36... | collective-permute-start | bytes 1572872 | tf_op jit(solution)/shard_map/ppermute | solution.py:304
  12.9 2.5 %collective-permute-start.2 = (f16[336,256]{1,0:T(8,128)(2,1)S(1)}, f16[336,256]{1,0:T(8,128)(2,1)S(1)}, u32[]{:S(2)}, u32[]{:S(2)}) collective-permute-start(f16[336,256]{1,0:T(8,128)(2,1)S(1)} %get-tuple-element.66), channel_id=1, source_target_pairs={{0,32},{32,0},{1,33},{33,1},{2,34},{34,2},{3,35},{35,3},{4,36},{36... | collective-permute-start | bytes 516104 | tf_op jit(solution)/shard_map/ppermute | solution.py:304
  13.0 2.4 %collective-permute-start.1 = (f16[336,256]{1,0:T(8,128)(2,1)S(1)}, f16[336,256]{1,0:T(8,128)(2,1)S(1)}, u32[]{:S(2)}, u32[]{:S(2)}) collective-permute-start(f16[336,256]{1,0:T(8,128)(2,1)S(1)} %get-tuple-element.65), channel_id=1, source_target_pairs={{0,32},{32,0},{1,33},{33,1},{2,34},{34,2},{3,35},{35,3},{4,36},{36... | collective-permute-start | bytes 516104 | tf_op jit(solution)/shard_map/ppermute | solution.py:304
  15.6 15.5 %collective-permute-start.8 = (f16[1024,256]{1,0:T(8,128)(2,1)S(1)}, f16[1024,256]{1,0:T(8,128)(2,1)S(1)}, u32[]{:S(2)}, u32[]{:S(2)}) collective-permute-start(f16[1024,256]{1,0:T(8,128)(2,1)S(1)} %add_convert_fusion.1), channel_id=1, source_target_pairs={{0,64},{32,224},{64,128},{96,32},{128,192},{160,96},{192,0},{224,1... | collective-permute-start | bytes 1572872 | tf_op jit(solution)/shard_map/ppermute | solution.py:356
  17.0 14.2 %collective-permute-start.9 = (f16[1024,256]{1,0:T(8,128)(2,1)S(1)}, f16[1024,256]{1,0:T(8,128)(2,1)S(1)}, u32[]{:S(2)}, u32[]{:S(2)}) collective-permute-start(f16[1024,256]{1,0:T(8,128)(2,1)S(1)} %add_convert_fusion), channel_id=1, source_target_pairs={{0,192},{32,96},{64,0},{96,160},{128,64},{160,224},{192,128},{224,... | collective-permute-start | bytes 1572872 | tf_op jit(solution)/shard_map/ppermute | solution.py:359
  24.2 11.6 %copy-start = (f32[1024,256]{1,0:T(8,128)S(1)}, f32[1024,256]{1,0:T(8,128)}, u32[]{:S(2)}) copy-start(f32[1024,256]{1,0:T(8,128)} %param.13) | copy-start | bytes 3145732
  24.4 15.0 %copy-start.1 = (f32[256]{0:T(256)S(1)}, f32[256]{0:T(256)}, u32[]{:S(2)}) copy-start(f32[256]{0:T(256)} %param.11) | copy-start | bytes 3076
  24.4 6.8 %collective-permute-start.7 = (f16[512,256]{1,0:T(8,128)(2,1)S(1)}, f16[512,256]{1,0:T(8,128)(2,1)S(1)}, u32[]{:S(2)}, u32[]{:S(2)}) collective-permute-start(f16[512,256]{1,0:T(8,128)(2,1)S(1)} %get-tuple-element.64), channel_id=1, source_target_pairs={{0,32},{32,0},{1,33},{33,1},{2,34},{34,2},{3,35},{35,3},{4,36},{36... | collective-permute-start | bytes 786440 | tf_op jit(solution)/shard_map/ppermute | solution.py:304
  24.5 6.7 %collective-permute-start.6 = (f16[512,256]{1,0:T(8,128)(2,1)S(1)}, f16[512,256]{1,0:T(8,128)(2,1)S(1)}, u32[]{:S(2)}, u32[]{:S(2)}) collective-permute-start(f16[512,256]{1,0:T(8,128)(2,1)S(1)} %get-tuple-element.63), channel_id=1, source_target_pairs={{0,32},{32,0},{1,33},{33,1},{2,34},{34,2},{3,35},{35,3},{4,36},{36... | collective-permute-start | bytes 786440 | tf_op jit(solution)/shard_map/ppermute | solution.py:304
  31.2 28.3 %copy-start.2 = (f32[1024]{0:T(1024)S(1)}, f32[1024]{0:T(1024)}, u32[]{:S(2)}) copy-start(f32[1024]{0:T(1024)} %param.10) | copy-start | bytes 12292
  31.6 5.2 %collective-permute-start.12 = (f32[1,256]{1,0:T(1,128)S(1)}, f32[1,256]{1,0:T(1,128)S(1)}, u32[]{:S(2)}, u32[]{:S(2)}) collective-permute-start(f32[1,256]{1,0:T(1,128)S(1)} %bitcast.10), channel_id=1, source_target_pairs={{0,16},{8,24},{16,0},{24,8},{1,17},{9,25},{17,1},{25,9},{2,18},{10... | collective-permute-start | bytes 3080 | tf_op jit(solution)/shard_map/ppermute | solution.py:380
  34.6 4.8 %collective-permute-start.11 = (f32[1,256]{1,0:T(1,128)S(1)}, f32[1,256]{1,0:T(1,128)S(1)}, u32[]{:S(2)}, u32[]{:S(2)}) collective-permute-start(f32[1,256]{1,0:T(1,128)S(1)} %bitcast.11), channel_id=1, source_target_pairs={{0,24},{8,16},{16,8},{24,0},{1,25},{9,17},{17,9},{25,1},{2,26},{10... | collective-permute-start | bytes 3080 | tf_op jit(solution)/shard_map/ppermute | solution.py:379
  35.8 3.6 %collective-permute-start.10 = (f32[1,256]{1,0:T(1,128)S(1)}, f32[1,256]{1,0:T(1,128)S(1)}, u32[]{:S(2)}, u32[]{:S(2)}) collective-permute-start(f32[1,256]{1,0:T(1,128)S(1)} %bitcast.12), channel_id=1, source_target_pairs={{0,8},{8,0},{16,24},{24,16},{1,9},{9,1},{17,25},{25,17},{2,10},{10... | collective-permute-start | bytes 3080 | tf_op jit(solution)/shard_map/ppermute | solution.py:378
  39.7 1.3 %collective-permute-start.13 = (f32[16,128]{1,0:T(8,128)S(1)}, f32[16,128]{1,0:T(8,128)S(1)}, u32[]{:S(2)}, u32[]{:S(2)}) collective-permute-start(f32[16,128]{1,0:T(8,128)S(1)} %get-tuple-element.57), channel_id=1, source_target_pairs={{0,32},{32,0},{1,33},{33,1},{2,34},{34,2},{3,35},{35,3},{4,36},{36... | collective-permute-start | bytes 24584 | tf_op jit(solution)/shard_map/ppermute | solution.py:397
  59.7 1.3 %collective-permute-start.14 = (f32[8,128]{1,0:T(8,128)S(1)}, f32[8,128]{1,0:T(8,128)S(1)}, u32[]{:S(2)}, u32[]{:S(2)}) collective-permute-start(f32[8,128]{1,0:T(8,128)S(1)} %row_reduce.1.mine), channel_id=1, source_target_pairs={{0,32},{32,0},{1,33},{33,1},{2,34},{34,2},{3,35},{35,3},{4,36},{36... | collective-permute-start | bytes 12296 | tf_op jit(solution)/shard_map/ppermute | solution.py:409
  60.9 5.1 %collective-permute-start.17 = (f32[8,128]{1,0:T(8,128)S(1)}, f32[8,128]{1,0:T(8,128)S(1)}, u32[]{:S(2)}, u32[]{:S(2)}) collective-permute-start(f32[8,128]{1,0:T(8,128)S(1)} %add.67.scalars_a), channel_id=1, source_target_pairs={{0,16},{8,24},{16,0},{24,8},{1,17},{9,25},{17,1},{25,9},{2,18},{10... | collective-permute-start | bytes 12296 | tf_op jit(solution)/shard_map/ppermute | solution.py:414
  62.4 4.8 %collective-permute-start.16 = (f32[8,128]{1,0:T(8,128)S(1)}, f32[8,128]{1,0:T(8,128)S(1)}, u32[]{:S(2)}, u32[]{:S(2)}) collective-permute-start(f32[8,128]{1,0:T(8,128)S(1)} %add.67.scalars_a), channel_id=1, source_target_pairs={{0,24},{8,16},{16,8},{24,0},{1,25},{9,17},{17,9},{25,1},{2,26},{10... | collective-permute-start | bytes 12296 | tf_op jit(solution)/shard_map/ppermute | solution.py:413
  63.5 3.7 %collective-permute-start.15 = (f32[8,128]{1,0:T(8,128)S(1)}, f32[8,128]{1,0:T(8,128)S(1)}, u32[]{:S(2)}, u32[]{:S(2)}) collective-permute-start(f32[8,128]{1,0:T(8,128)S(1)} %add.67.scalars_a), channel_id=1, source_target_pairs={{0,8},{8,0},{16,24},{24,16},{1,9},{9,1},{17,25},{25,17},{2,10},{10... | collective-permute-start | bytes 12296 | tf_op jit(solution)/shard_map/ppermute | solution.py:412

commit v6 on v5

--- a/solution.py
+++ b/solution.py
@@ -316,7 +316,7 @@
         activations,
         cotangent,
     )
-    far_came = swapped(far_away, 1)
+    far_came = lax.ppermute(far_away, "c", swap_core)
     far, away_a, away_b, mine_b = loading_call(
         second_kernel,
         "second_matmul",

time: 69.3 us -> 69.2 us (level)
    ppermute x7 -> x6, starting transfers between devices: 1.95 us -> 1.86 us  [swapped(): parts = [lax.ppermute(part, 'c', swap_core) for part in parts]]
where the time goes in v6:
time: 69.2 us; the launch traced here: 68.4 us
  blocking collectives  18.6 us (27%)
  starting transfers between devices  17 us (25%)
  Pallas kernels  15.5 us (22%)
  waiting for transfers between devices  14.8 us (21%)
  other arithmetic  1.28 us (2%)
  between operations  1.01 us (1%)
    all_to_all x1, blocking collectives, per_device(): came = lax.all_to_all(message, ('y', 'z'), 0, 0, tiled=True)  18.6 us
    pallas_call x3, Pallas kernels, loading_call(): pl.pallas_call(kernel, name=name, in_specs=in_specs, out_specs=[VMEM] * l...  7.8 us
    ppermute x1, waiting for transfers between devices, per_device(): behind_sent = lax.ppermute(behind, ('y', 'c'), to_behind)  6.15 us
    ppermute x1, starting transfers between devices, per_device(): ahead_sent = lax.ppermute(ahead, ('y', 'c'), to_ahead)  3.95 us
    pallas_call x6, Pallas kernels, call(): pl.pallas_call(kernel, name=name, in_specs=[SMEM] * scalars + [VMEM] * (l...  3.39 us
    pallas_call x1, Pallas kernels, per_device(): pl.pallas_call(last_kernel, name='last_matmul', in_specs=[SMEM, SMEM, VME...  3.25 us
    ppermute x1, starting transfers between devices, per_device(): lax.ppermute(col_part, 'x', pair_cross)  3.11 us
    ppermute x1, starting transfers between devices, per_device(): far_sent = lax.ppermute(far, ('y', 'c'), to_ahead)  3.1 us
  transfers between devices with their start and end apart: 18, of which 8 were waited for; matrix products, arithmetic and copies ran while one was open for 1% of the time, Pallas kernels for 16%

profile of v6, /device:TPU:32, one launch (start us, length us, event | category | flops | bytes accessed | tf_op | source)
XLA Modules:
  0.0 68.4 jit_solution(18233995041308999904)
XLA Ops:
  0.6 3.3 %first_matmul.1 = (f32[1024,256]{1,0:T(8,128)S(1)}, bf16[1536,1024]{1,0:T(8,128)(2,1)S(1)}, bf16[1536,512]{1,0:T(8,128)(2,1)S(1)}) custom-call(s32[1]{0:T(128)} %bitcast.owner, s32[1]{0:T(128)} %bitcast.4.core, bf16[1536,1024]{1,0:T(8,128)(2,1)} %activations.1, bf16[1536,2048]{1,0:T(8,128)(2,1)} %cotangent.7), custom_call_target="tpu_custom_call" | custom-call | flops 1 | bytes 1 | tf_op jit(solution)/shard_map/first_matmul/pallas_call | solution.py:158
  3.9 0.1 collective-permute-start
  4.0 2.6 %second_matmul.1 = (f32[1024,256]{1,0:T(8,128)S(1)}, bf16[1536,256]{1,0:T(8,128)(2,1)S(1)}, bf16[1536,256]{1,0:T(8,128)(2,1)S(1)}, bf16[1536,256]{1,0:T(8,128)(2,1)S(1)}) custom-call(s32[1]{0:T(128)} %bitcast.4.core, s32[1]{0:T(128)} %bitcast.1.behind, s32[1]{0:T(128)} %bitcast.2.ahead, bf16[1536,1024]{1,0:T(8,128)(2,1)S(1)} %get-tuple-element.51.kept, ...), custom_call_target="tpu_custom_call" | custom-call | flops 1 | bytes 1 | tf_op jit(solution)/shard_map/second_matmul/pallas_call | solution.py:158
  6.7 0.2 add_convert_fusion.2
  6.8 3.1 %collective-permute-start.5 = (f16[1024,256]{1,0:T(8,128)(2,1)S(1)}, f16[1024,256]{1,0:T(8,128)(2,1)S(1)}, u32[]{:S(2)}, u32[]{:S(2)}) collective-permute-start(f16[1024,256]{1,0:T(8,128)(2,1)S(1)} %add_convert_fusion.2), channel_id=1, source_target_pairs={{0,192},{32,96},{64,0},{96,160},{128,64},{160,224},{192,128},{224,... | collective-permute-start | bytes 1572872 | tf_op jit(solution)/shard_map/ppermute | solution.py:335
  9.9 1.9 %third_matmul.1 = (f32[1024,256]{1,0:T(8,128)S(1)}, f32[1024,256]{1,0:T(8,128)S(1)}, bf16[1536,256]{1,0:T(8,128)(2,1)S(1)}) custom-call(s32[1]{0:T(128)} %bitcast.4.core, s32[1]{0:T(128)} %bitcast.1.behind, bf16[1536,1024]{1,0:T(8,128)(2,1)S(1)} %get-tuple-element.51.kept, bf16[1536,256]{1,0:T(8,128)(2,1)S(1)} %get-tuple-element.42.a, ...), custom_call_target="tpu_custom_call" | custom-call | flops 1 | bytes 1 | tf_op jit(solution)/shard_map/third_matmul/pallas_call | solution.py:158
  11.8 0.1 convert.9
  12.0 0.1 collective-permute-start.3
  12.1 0.1 convert_element_type.38
  12.2 0.6 collective-permute-start.4
  12.8 0.1 fusion.1
  12.8 0.1 collective-permute-start.2
  12.9 0.5 collective-permute-start.1
  13.4 1.9 %fourth_matmul.1 = (f32[1024,256]{1,0:T(8,128)S(1)}, f32[1024,256]{1,0:T(8,128)S(1)}) custom-call(bf16[1536,1024]{1,0:T(8,128)(2,1)S(1)} %get-tuple-element.51.kept, bf16[1536,256]{1,0:T(8,128)(2,1)S(1)} %get-tuple-element.44.a, bf16[1536,256]{1,0:T(8,128)(2,1)S(1)} %get-tuple-element.45.b), custom_call_target="tpu_custom_call" | custom-call | flops 1 | bytes 1 | tf_op jit(solution)/shard_map/fourth_matmul/pallas_call | solution.py:49
  15.3 0.2 add_convert_fusion.1
  15.5 0.1 collective-permute-start.8
  15.6 1.0 %collective-permute-done.5 = f16[1024,256]{1,0:T(8,128)(2,1)S(1)} collective-permute-done((f16[1024,256]{1,0:T(8,128)(2,1)S(1)}, f16[1024,256]{1,0:T(8,128)(2,1)S(1)}, u32[]{:S(2)}, u32[]{:S(2)}) %collective-permute-start.5) | collective-permute-done | bytes 524320 | tf_op jit(solution)/shard_map/ppermute | solution.py:335
  16.6 0.2 add_convert_fusion
  16.9 3.9 %collective-permute-start.9 = (f16[1024,256]{1,0:T(8,128)(2,1)S(1)}, f16[1024,256]{1,0:T(8,128)(2,1)S(1)}, u32[]{:S(2)}, u32[]{:S(2)}) collective-permute-start(f16[1024,256]{1,0:T(8,128)(2,1)S(1)} %add_convert_fusion), channel_id=1, source_target_pairs={{0,192},{32,96},{64,0},{96,160},{128,64},{160,224},{192,128},{224,... | collective-permute-start | bytes 1572872 | tf_op jit(solution)/shard_map/ppermute | solution.py:359
  20.8 3.3 %last_matmul.1 = (f32[1024,256]{1,0:T(8,128)S(1)}, f32[1024,256]{1,0:T(8,128)S(1)}) custom-call(s32[1]{0:T(128)} %bitcast.4.core, s32[1]{0:T(128)} %bitcast.3.owner, bf16[1536,1024]{1,0:T(8,128)(2,1)S(1)} %get-tuple-element.51.kept, bf16[1536,2048]{1,0:T(8,128)(2,1)} %cotangent.7), custom_call_target="tpu_custom_call" | custom-call | flops 1 | bytes 1 | tf_op jit(solution)/shard_map/last_matmul/pallas_call | solution.py:362
  24.1 0.0 copy-start
  24.1 0.1 convert.10
  24.2 0.1 fusion
  24.3 0.0 copy-start.1
  24.3 0.1 collective-permute-start.7
  24.4 0.5 collective-permute-start.6
  24.9 6.1 %collective-permute-done.8 = f16[1024,256]{1,0:T(8,128)(2,1)S(1)} collective-permute-done((f16[1024,256]{1,0:T(8,128)(2,1)S(1)}, f16[1024,256]{1,0:T(8,128)(2,1)S(1)}, u32[]{:S(2)}, u32[]{:S(2)}) %collective-permute-start.8) | collective-permute-done | bytes 524320 | tf_op jit(solution)/shard_map/ppermute | solution.py:356
  31.1 0.0 copy-start.2
  31.1 0.4 multiply_reduce_fusion
  31.5 3.1 %collective-permute-start.12 = (f32[1,256]{1,0:T(1,128)S(1)}, f32[1,256]{1,0:T(1,128)S(1)}, u32[]{:S(2)}, u32[]{:S(2)}) collective-permute-start(f32[1,256]{1,0:T(1,128)S(1)} %bitcast.10), channel_id=1, source_target_pairs={{0,16},{8,24},{16,0},{24,8},{1,17},{9,25},{17,1},{25,9},{2,18},{10... | collective-permute-start | bytes 3080 | tf_op jit(solution)/shard_map/ppermute | solution.py:380
  34.6 1.1 %collective-permute-start.11 = (f32[1,256]{1,0:T(1,128)S(1)}, f32[1,256]{1,0:T(1,128)S(1)}, u32[]{:S(2)}, u32[]{:S(2)}) collective-permute-start(f32[1,256]{1,0:T(1,128)S(1)} %bitcast.11), channel_id=1, source_target_pairs={{0,24},{8,16},{16,8},{24,0},{1,25},{9,17},{17,9},{25,1},{2,26},{10... | collective-permute-start | bytes 3080 | tf_op jit(solution)/shard_map/ppermute | solution.py:379
  35.7 0.4 square_rows.1
  36.1 0.5 collective-permute-done.12
  36.6 2.7 %collective-permute-done.11 = f32[1,256]{1,0:T(1,128)S(1)} collective-permute-done((f32[1,256]{1,0:T(1,128)S(1)}, f32[1,256]{1,0:T(1,128)S(1)}, u32[]{:S(2)}, u32[]{:S(2)}) %collective-permute-start.11) | collective-permute-done | bytes 1056 | tf_op jit(solution)/shard_map/ppermute | solution.py:379
  39.4 0.2 weighted_rows.1
  39.6 0.1 collective-permute-start.13
  39.7 1.2 %collective-permute-done.13.came = f32[16,128]{1,0:T(8,128)S(1)} collective-permute-done((f32[16,128]{1,0:T(8,128)S(1)}, f32[16,128]{1,0:T(8,128)S(1)}, u32[]{:S(2)}, u32[]{:S(2)}) %collective-permute-start.13) | collective-permute-done | bytes 8224 | tf_op jit(solution)/shard_map/ppermute | solution.py:397
  40.9 18.6 %all_to_all.5.came = bf16[32,16,128]{2,1,0:T(8,128)(2,1)S(1)} all-to-all(bf16[32,16,128]{2,1,0:T(8,128)(2,1)S(1)} %message.1), channel_id=1, replica_groups=mesh['y'=4,'c'=2,'x'=4,'z'=8] {'y','z'}, dimensions={0} | all-to-all | bytes 262144 | tf_op jit(solution)/shard_map/all_to_all | solution.py:399
  59.4 0.2 row_reduce.1.mine
  59.6 0.1 collective-permute-start.14
  59.7 1.2 %collective-permute-done.14.twin = f32[8,128]{1,0:T(8,128)S(1)} collective-permute-done((f32[8,128]{1,0:T(8,128)S(1)}, f32[8,128]{1,0:T(8,128)S(1)}, u32[]{:S(2)}, u32[]{:S(2)}) %collective-permute-start.14) | collective-permute-done | bytes 4128 | tf_op jit(solution)/shard_map/ppermute | solution.py:409
  60.9 1.5 %collective-permute-start.17 = (f32[8,128]{1,0:T(8,128)S(1)}, f32[8,128]{1,0:T(8,128)S(1)}, u32[]{:S(2)}, u32[]{:S(2)}) collective-permute-start(f32[8,128]{1,0:T(8,128)S(1)} %add.67.scalars_a), channel_id=1, source_target_pairs={{0,16},{8,24},{16,0},{24,8},{1,17},{9,25},{17,1},{25,9},{2,18},{10... | collective-permute-start | bytes 12296 | tf_op jit(solution)/shard_map/ppermute | solution.py:414
  62.3 1.1 %collective-permute-start.16 = (f32[8,128]{1,0:T(8,128)S(1)}, f32[8,128]{1,0:T(8,128)S(1)}, u32[]{:S(2)}, u32[]{:S(2)}) collective-permute-start(f32[8,128]{1,0:T(8,128)S(1)} %add.67.scalars_a), channel_id=1, source_target_pairs={{0,24},{8,16},{16,8},{24,0},{1,25},{9,17},{17,9},{25,1},{2,26},{10... | collective-permute-start | bytes 12296 | tf_op jit(solution)/shard_map/ppermute | solution.py:413
  63.4 0.9 %collective-permute-start.15 = (f32[8,128]{1,0:T(8,128)S(1)}, f32[8,128]{1,0:T(8,128)S(1)}, u32[]{:S(2)}, u32[]{:S(2)}) collective-permute-start(f32[8,128]{1,0:T(8,128)S(1)} %add.67.scalars_a), channel_id=1, source_target_pairs={{0,8},{8,0},{16,24},{24,16},{1,9},{9,1},{17,25},{25,17},{2,10},{10... | collective-permute-start | bytes 12296 | tf_op jit(solution)/shard_map/ppermute | solution.py:412
  64.3 0.7 %normalise.1 = (f32[1024,256]{1,0:T(8,128)S(1)}, f32[8,128]{1,0:T(8,128)}, f32[1,256]{1,0:T(1,128)}) custom-call(s32[1]{0:T(128)} %bitcast.4.core, f32[1024,256]{1,0:T(8,128)S(1)} %get-tuple-element.62.gradient, f32[8,128]{1,0:T(8,128)S(1)} %row_reduce.1.mine, f32[8,128]{1,0:T(8,128)S(1)} %collective-permute-done.14.twin, f32[1,256]{1,0:T(1,128)S(1)} %bitcast.14, ...), custom_call_target="tpu_custom_call" | custom-call | flops 1 | bytes 1 | tf_op jit(solution)/shard_map/normalise/pallas_call | solution.py:49
  65.0 0.9 %collective-permute-done.17 = f32[8,128]{1,0:T(8,128)S(1)} collective-permute-done((f32[8,128]{1,0:T(8,128)S(1)}, f32[8,128]{1,0:T(8,128)S(1)}, u32[]{:S(2)}, u32[]{:S(2)}) %collective-permute-start.17) | collective-permute-done | bytes 4128 | tf_op jit(solution)/shard_map/ppermute | solution.py:414
  66.0 1.2 %collective-permute-done.16 = f32[8,128]{1,0:T(8,128)S(1)} collective-permute-done((f32[8,128]{1,0:T(8,128)S(1)}, f32[8,128]{1,0:T(8,128)S(1)}, u32[]{:S(2)}, u32[]{:S(2)}) %collective-permute-start.16) | collective-permute-done | bytes 4128 | tf_op jit(solution)/shard_map/ppermute | solution.py:413
  67.1 1.1 %step.1 = f32[1024,256]{1,0:T(8,128)} custom-call(f32[8,128]{1,0:T(8,128)S(1)} %add.67.scalars_a, f32[8,128]{1,0:T(8,128)S(1)} %add_add_fusion.scalars_b, f32[1024,256]{1,0:T(8,128)S(1)} %copy-done, f32[1024,256]{1,0:T(8,128)S(1)} %get-tuple-element.58.update), custom_call_target="tpu_custom_call" | custom-call | flops 1 | bytes 1 | tf_op jit(solution)/shard_map/step/pallas_call | solution.py:427
  (19 shorter events, 0.1 us)
Async XLA Ops:
  3.9 2.7 %collective-permute-start = (f32[1024,256]{1,0:T(8,128)S(1)}, f32[1024,256]{1,0:T(8,128)S(1)}, u32[]{:S(2)}, u32[]{:S(2)}) collective-permute-start(f32[1024,256]{1,0:T(8,128)S(1)} %get-tuple-element.41), channel_id=1, source_target_pairs={{0,32},{32,0},{1,33},{33,1},{2,34},{34,2},{3,35},{35,3},{4,36},{36... | collective-permute-start | bytes 3145736 | tf_op jit(solution)/shard_map/ppermute | solution.py:319
  6.8 9.8 %collective-permute-start.5 = (f16[1024,256]{1,0:T(8,128)(2,1)S(1)}, f16[1024,256]{1,0:T(8,128)(2,1)S(1)}, u32[]{:S(2)}, u32[]{:S(2)}) collective-permute-start(f16[1024,256]{1,0:T(8,128)(2,1)S(1)} %add_convert_fusion.2), channel_id=1, source_target_pairs={{0,192},{32,96},{64,0},{96,160},{128,64},{160,224},{192,128},{224,... | collective-permute-start | bytes 1572872 | tf_op jit(solution)/shard_map/ppermute | solution.py:335
  12.0 3.3 %collective-permute-start.3 = (f16[352,256]{1,0:T(8,128)(2,1)S(1)}, f16[352,256]{1,0:T(8,128)(2,1)S(1)}, u32[]{:S(2)}, u32[]{:S(2)}) collective-permute-start(f16[352,256]{1,0:T(8,128)(2,1)S(1)} %slice.27), channel_id=1, source_target_pairs={{0,32},{32,0},{1,33},{33,1},{2,34},{34,2},{3,35},{35,3},{4,36},{36... | collective-permute-start | bytes 540680 | tf_op jit(solution)/shard_map/ppermute | solution.py:304
  12.2 4.5 %collective-permute-start.4 = (f16[1024,256]{1,0:T(8,128)(2,1)S(1)}, f16[1024,256]{1,0:T(8,128)(2,1)S(1)}, u32[]{:S(2)}, u32[]{:S(2)}) collective-permute-start(f16[1024,256]{1,0:T(8,128)(2,1)S(1)} %convert_element_type.38), channel_id=1, source_target_pairs={{0,32},{32,0},{1,33},{33,1},{2,34},{34,2},{3,35},{35,3},{4,36},{36... | collective-permute-start | bytes 1572872 | tf_op jit(solution)/shard_map/ppermute | solution.py:304
  12.8 2.5 %collective-permute-start.2 = (f16[336,256]{1,0:T(8,128)(2,1)S(1)}, f16[336,256]{1,0:T(8,128)(2,1)S(1)}, u32[]{:S(2)}, u32[]{:S(2)}) collective-permute-start(f16[336,256]{1,0:T(8,128)(2,1)S(1)} %get-tuple-element.66), channel_id=1, source_target_pairs={{0,32},{32,0},{1,33},{33,1},{2,34},{34,2},{3,35},{35,3},{4,36},{36... | collective-permute-start | bytes 516104 | tf_op jit(solution)/shard_map/ppermute | solution.py:304
  12.9 2.4 %collective-permute-start.1 = (f16[336,256]{1,0:T(8,128)(2,1)S(1)}, f16[336,256]{1,0:T(8,128)(2,1)S(1)}, u32[]{:S(2)}, u32[]{:S(2)}) collective-permute-start(f16[336,256]{1,0:T(8,128)(2,1)S(1)} %get-tuple-element.65), channel_id=1, source_target_pairs={{0,32},{32,0},{1,33},{33,1},{2,34},{34,2},{3,35},{35,3},{4,36},{36... | collective-permute-start | bytes 516104 | tf_op jit(solution)/shard_map/ppermute | solution.py:304
  15.5 15.5 %collective-permute-start.8 = (f16[1024,256]{1,0:T(8,128)(2,1)S(1)}, f16[1024,256]{1,0:T(8,128)(2,1)S(1)}, u32[]{:S(2)}, u32[]{:S(2)}) collective-permute-start(f16[1024,256]{1,0:T(8,128)(2,1)S(1)} %add_convert_fusion.1), channel_id=1, source_target_pairs={{0,64},{32,224},{64,128},{96,32},{128,192},{160,96},{192,0},{224,1... | collective-permute-start | bytes 1572872 | tf_op jit(solution)/shard_map/ppermute | solution.py:356
  16.9 14.2 %collective-permute-start.9 = (f16[1024,256]{1,0:T(8,128)(2,1)S(1)}, f16[1024,256]{1,0:T(8,128)(2,1)S(1)}, u32[]{:S(2)}, u32[]{:S(2)}) collective-permute-start(f16[1024,256]{1,0:T(8,128)(2,1)S(1)} %add_convert_fusion), channel_id=1, source_target_pairs={{0,192},{32,96},{64,0},{96,160},{128,64},{160,224},{192,128},{224,... | collective-permute-start | bytes 1572872 | tf_op jit(solution)/shard_map/ppermute | solution.py:359
  24.1 11.6 %copy-start = (f32[1024,256]{1,0:T(8,128)S(1)}, f32[1024,256]{1,0:T(8,128)}, u32[]{:S(2)}) copy-start(f32[1024,256]{1,0:T(8,128)} %param.13) | copy-start | bytes 3145732
  24.3 15.0 %copy-start.1 = (f32[256]{0:T(256)S(1)}, f32[256]{0:T(256)}, u32[]{:S(2)}) copy-start(f32[256]{0:T(256)} %param.11) | copy-start | bytes 3076
  24.3 6.8 %collective-permute-start.7 = (f16[512,256]{1,0:T(8,128)(2,1)S(1)}, f16[512,256]{1,0:T(8,128)(2,1)S(1)}, u32[]{:S(2)}, u32[]{:S(2)}) collective-permute-start(f16[512,256]{1,0:T(8,128)(2,1)S(1)} %get-tuple-element.64), channel_id=1, source_target_pairs={{0,32},{32,0},{1,33},{33,1},{2,34},{34,2},{3,35},{35,3},{4,36},{36... | collective-permute-start | bytes 786440 | tf_op jit(solution)/shard_map/ppermute | solution.py:304
  24.4 6.7 %collective-permute-start.6 = (f16[512,256]{1,0:T(8,128)(2,1)S(1)}, f16[512,256]{1,0:T(8,128)(2,1)S(1)}, u32[]{:S(2)}, u32[]{:S(2)}) collective-permute-start(f16[512,256]{1,0:T(8,128)(2,1)S(1)} %get-tuple-element.63), channel_id=1, source_target_pairs={{0,32},{32,0},{1,33},{33,1},{2,34},{34,2},{3,35},{35,3},{4,36},{36... | collective-permute-start | bytes 786440 | tf_op jit(solution)/shard_map/ppermute | solution.py:304
  31.1 28.3 %copy-start.2 = (f32[1024]{0:T(1024)S(1)}, f32[1024]{0:T(1024)}, u32[]{:S(2)}) copy-start(f32[1024]{0:T(1024)} %param.10) | copy-start | bytes 12292
  31.5 5.2 %collective-permute-start.12 = (f32[1,256]{1,0:T(1,128)S(1)}, f32[1,256]{1,0:T(1,128)S(1)}, u32[]{:S(2)}, u32[]{:S(2)}) collective-permute-start(f32[1,256]{1,0:T(1,128)S(1)} %bitcast.10), channel_id=1, source_target_pairs={{0,16},{8,24},{16,0},{24,8},{1,17},{9,25},{17,1},{25,9},{2,18},{10... | collective-permute-start | bytes 3080 | tf_op jit(solution)/shard_map/ppermute | solution.py:380
  34.6 4.8 %collective-permute-start.11 = (f32[1,256]{1,0:T(1,128)S(1)}, f32[1,256]{1,0:T(1,128)S(1)}, u32[]{:S(2)}, u32[]{:S(2)}) collective-permute-start(f32[1,256]{1,0:T(1,128)S(1)} %bitcast.11), channel_id=1, source_target_pairs={{0,24},{8,16},{16,8},{24,0},{1,25},{9,17},{17,9},{25,1},{2,26},{10... | collective-permute-start | bytes 3080 | tf_op jit(solution)/shard_map/ppermute | solution.py:379
  35.7 3.7 %collective-permute-start.10 = (f32[1,256]{1,0:T(1,128)S(1)}, f32[1,256]{1,0:T(1,128)S(1)}, u32[]{:S(2)}, u32[]{:S(2)}) collective-permute-start(f32[1,256]{1,0:T(1,128)S(1)} %bitcast.12), channel_id=1, source_target_pairs={{0,8},{8,0},{16,24},{24,16},{1,9},{9,1},{17,25},{25,17},{2,10},{10... | collective-permute-start | bytes 3080 | tf_op jit(solution)/shard_map/ppermute | solution.py:378
  39.6 1.3 %collective-permute-start.13 = (f32[16,128]{1,0:T(8,128)S(1)}, f32[16,128]{1,0:T(8,128)S(1)}, u32[]{:S(2)}, u32[]{:S(2)}) collective-permute-start(f32[16,128]{1,0:T(8,128)S(1)} %get-tuple-element.57), channel_id=1, source_target_pairs={{0,32},{32,0},{1,33},{33,1},{2,34},{34,2},{3,35},{35,3},{4,36},{36... | collective-permute-start | bytes 24584 | tf_op jit(solution)/shard_map/ppermute | solution.py:397
  59.6 1.3 %collective-permute-start.14 = (f32[8,128]{1,0:T(8,128)S(1)}, f32[8,128]{1,0:T(8,128)S(1)}, u32[]{:S(2)}, u32[]{:S(2)}) collective-permute-start(f32[8,128]{1,0:T(8,128)S(1)} %row_reduce.1.mine), channel_id=1, source_target_pairs={{0,32},{32,0},{1,33},{33,1},{2,34},{34,2},{3,35},{35,3},{4,36},{36... | collective-permute-start | bytes 12296 | tf_op jit(solution)/shard_map/ppermute | solution.py:409
  60.9 5.1 %collective-permute-start.17 = (f32[8,128]{1,0:T(8,128)S(1)}, f32[8,128]{1,0:T(8,128)S(1)}, u32[]{:S(2)}, u32[]{:S(2)}) collective-permute-start(f32[8,128]{1,0:T(8,128)S(1)} %add.67.scalars_a), channel_id=1, source_target_pairs={{0,16},{8,24},{16,0},{24,8},{1,17},{9,25},{17,1},{25,9},{2,18},{10... | collective-permute-start | bytes 12296 | tf_op jit(solution)/shard_map/ppermute | solution.py:414
  62.3 4.8 %collective-permute-start.16 = (f32[8,128]{1,0:T(8,128)S(1)}, f32[8,128]{1,0:T(8,128)S(1)}, u32[]{:S(2)}, u32[]{:S(2)}) collective-permute-start(f32[8,128]{1,0:T(8,128)S(1)} %add.67.scalars_a), channel_id=1, source_target_pairs={{0,24},{8,16},{16,8},{24,0},{1,25},{9,17},{17,9},{25,1},{2,26},{10... | collective-permute-start | bytes 12296 | tf_op jit(solution)/shard_map/ppermute | solution.py:413
  63.4 3.7 %collective-permute-start.15 = (f32[8,128]{1,0:T(8,128)S(1)}, f32[8,128]{1,0:T(8,128)S(1)}, u32[]{:S(2)}, u32[]{:S(2)}) collective-permute-start(f32[8,128]{1,0:T(8,128)S(1)} %add.67.scalars_a), channel_id=1, source_target_pairs={{0,8},{8,0},{16,24},{24,16},{1,9},{9,1},{17,25},{25,17},{2,10},{10... | collective-permute-start | bytes 12296 | tf_op jit(solution)/shard_map/ppermute | solution.py:412

commit v7 on v6

--- a/solution.py
+++ b/solution.py
@@ -275,8 +275,8 @@
     factor = step_size * scale * jnp.sqrt(row_level) / clip
     factor = jnp.concatenate([factor, factor], axis=1)
     copies = []
-    for group in range(GROUPS):
-        rows = pl.ds(group * LANES, LANES)
+    for group in range(GROUPS // 2):
+        rows = pl.ds(group * 2 * LANES, 2 * LANES)
         stage[rows, :] = param[rows, :] - factor * update[rows, :]
         copy = pltpu.make_async_copy(stage.at[rows, :], new_param.at[rows, :], sent.at[group])
         copy.start()

time: 69.2 us -> 69.2 us (level)
  no operation moved by 1% of the time
where the time goes in v7:
time: 69.2 us; the launch traced here: 68.4 us
  blocking collectives  18.6 us (27%)
  starting transfers between devices  17 us (25%)
  Pallas kernels  15.5 us (22%)
  waiting for transfers between devices  14.8 us (21%)
  other arithmetic  1.28 us (2%)
  between operations  1.01 us (1%)
    all_to_all x1, blocking collectives, per_device(): came = lax.all_to_all(message, ('y', 'z'), 0, 0, tiled=True)  18.6 us
    pallas_call x3, Pallas kernels, loading_call(): pl.pallas_call(kernel, name=name, in_specs=in_specs, out_specs=[VMEM] * l...  7.8 us
    ppermute x1, waiting for transfers between devices, per_device(): behind_sent = lax.ppermute(behind, ('y', 'c'), to_behind)  6.15 us
    ppermute x1, starting transfers between devices, per_device(): ahead_sent = lax.ppermute(ahead, ('y', 'c'), to_ahead)  3.95 us
    pallas_call x6, Pallas kernels, call(): pl.pallas_call(kernel, name=name, in_specs=[SMEM] * scalars + [VMEM] * (l...  3.39 us
    pallas_call x1, Pallas kernels, per_device(): pl.pallas_call(last_kernel, name='last_matmul', in_specs=[SMEM, SMEM, VME...  3.25 us
    ppermute x1, starting transfers between devices, per_device(): lax.ppermute(col_part, 'x', pair_cross)  3.11 us
    ppermute x1, starting transfers between devices, per_device(): far_sent = lax.ppermute(far, ('y', 'c'), to_ahead)  3.1 us
  transfers between devices with their start and end apart: 18, of which 8 were waited for; matrix products, arithmetic and copies ran while one was open for 1% of the time, Pallas kernels for 16%

profile of v7, /device:TPU:32, one launch (start us, length us, event | category | flops | bytes accessed | tf_op | source)
XLA Modules:
  0.0 68.4 jit_solution(2240220700086387406)
XLA Ops:
  0.6 3.3 %first_matmul.1 = (f32[1024,256]{1,0:T(8,128)S(1)}, bf16[1536,1024]{1,0:T(8,128)(2,1)S(1)}, bf16[1536,512]{1,0:T(8,128)(2,1)S(1)}) custom-call(s32[1]{0:T(128)} %bitcast.owner, s32[1]{0:T(128)} %bitcast.4.core, bf16[1536,1024]{1,0:T(8,128)(2,1)} %activations.1, bf16[1536,2048]{1,0:T(8,128)(2,1)} %cotangent.7), custom_call_target="tpu_custom_call" | custom-call | flops 1 | bytes 1 | tf_op jit(solution)/shard_map/first_matmul/pallas_call | solution.py:158
  3.9 0.1 collective-permute-start
  4.0 2.6 %second_matmul.1 = (f32[1024,256]{1,0:T(8,128)S(1)}, bf16[1536,256]{1,0:T(8,128)(2,1)S(1)}, bf16[1536,256]{1,0:T(8,128)(2,1)S(1)}, bf16[1536,256]{1,0:T(8,128)(2,1)S(1)}) custom-call(s32[1]{0:T(128)} %bitcast.4.core, s32[1]{0:T(128)} %bitcast.1.behind, s32[1]{0:T(128)} %bitcast.2.ahead, bf16[1536,1024]{1,0:T(8,128)(2,1)S(1)} %get-tuple-element.51.kept, ...), custom_call_target="tpu_custom_call" | custom-call | flops 1 | bytes 1 | tf_op jit(solution)/shard_map/second_matmul/pallas_call | solution.py:158
  6.7 0.2 add_convert_fusion.2
  6.8 3.1 %collective-permute-start.5 = (f16[1024,256]{1,0:T(8,128)(2,1)S(1)}, f16[1024,256]{1,0:T(8,128)(2,1)S(1)}, u32[]{:S(2)}, u32[]{:S(2)}) collective-permute-start(f16[1024,256]{1,0:T(8,128)(2,1)S(1)} %add_convert_fusion.2), channel_id=1, source_target_pairs={{0,192},{32,96},{64,0},{96,160},{128,64},{160,224},{192,128},{224,... | collective-permute-start | bytes 1572872 | tf_op jit(solution)/shard_map/ppermute | solution.py:335
  9.9 1.9 %third_matmul.1 = (f32[1024,256]{1,0:T(8,128)S(1)}, f32[1024,256]{1,0:T(8,128)S(1)}, bf16[1536,256]{1,0:T(8,128)(2,1)S(1)}) custom-call(s32[1]{0:T(128)} %bitcast.4.core, s32[1]{0:T(128)} %bitcast.1.behind, bf16[1536,1024]{1,0:T(8,128)(2,1)S(1)} %get-tuple-element.51.kept, bf16[1536,256]{1,0:T(8,128)(2,1)S(1)} %get-tuple-element.42.a, ...), custom_call_target="tpu_custom_call" | custom-call | flops 1 | bytes 1 | tf_op jit(solution)/shard_map/third_matmul/pallas_call | solution.py:158
  11.8 0.1 convert.9
  12.0 0.1 collective-permute-start.3
  12.1 0.1 convert_element_type.38
  12.2 0.6 collective-permute-start.4
  12.8 0.1 fusion.1
  12.8 0.1 collective-permute-start.2
  12.9 0.5 collective-permute-start.1
  13.4 1.9 %fourth_matmul.1 = (f32[1024,256]{1,0:T(8,128)S(1)}, f32[1024,256]{1,0:T(8,128)S(1)}) custom-call(bf16[1536,1024]{1,0:T(8,128)(2,1)S(1)} %get-tuple-element.51.kept, bf16[1536,256]{1,0:T(8,128)(2,1)S(1)} %get-tuple-element.44.a, bf16[1536,256]{1,0:T(8,128)(2,1)S(1)} %get-tuple-element.45.b), custom_call_target="tpu_custom_call" | custom-call | flops 1 | bytes 1 | tf_op jit(solution)/shard_map/fourth_matmul/pallas_call | solution.py:49
  15.3 0.2 add_convert_fusion.1
  15.5 0.1 collective-permute-start.8
  15.6 1.0 %collective-permute-done.5 = f16[1024,256]{1,0:T(8,128)(2,1)S(1)} collective-permute-done((f16[1024,256]{1,0:T(8,128)(2,1)S(1)}, f16[1024,256]{1,0:T(8,128)(2,1)S(1)}, u32[]{:S(2)}, u32[]{:S(2)}) %collective-permute-start.5) | collective-permute-done | bytes 524320 | tf_op jit(solution)/shard_map/ppermute | solution.py:335
  16.6 0.2 add_convert_fusion
  16.9 3.9 %collective-permute-start.9 = (f16[1024,256]{1,0:T(8,128)(2,1)S(1)}, f16[1024,256]{1,0:T(8,128)(2,1)S(1)}, u32[]{:S(2)}, u32[]{:S(2)}) collective-permute-start(f16[1024,256]{1,0:T(8,128)(2,1)S(1)} %add_convert_fusion), channel_id=1, source_target_pairs={{0,192},{32,96},{64,0},{96,160},{128,64},{160,224},{192,128},{224,... | collective-permute-start | bytes 1572872 | tf_op jit(solution)/shard_map/ppermute | solution.py:359
  20.8 3.3 %last_matmul.1 = (f32[1024,256]{1,0:T(8,128)S(1)}, f32[1024,256]{1,0:T(8,128)S(1)}) custom-call(s32[1]{0:T(128)} %bitcast.4.core, s32[1]{0:T(128)} %bitcast.3.owner, bf16[1536,1024]{1,0:T(8,128)(2,1)S(1)} %get-tuple-element.51.kept, bf16[1536,2048]{1,0:T(8,128)(2,1)} %cotangent.7), custom_call_target="tpu_custom_call" | custom-call | flops 1 | bytes 1 | tf_op jit(solution)/shard_map/last_matmul/pallas_call | solution.py:362
  24.1 0.0 copy-start
  24.1 0.1 convert.10
  24.2 0.1 fusion
  24.3 0.0 copy-start.1
  24.3 0.1 collective-permute-start.7
  24.4 0.5 collective-permute-start.6
  24.9 6.1 %collective-permute-done.8 = f16[1024,256]{1,0:T(8,128)(2,1)S(1)} collective-permute-done((f16[1024,256]{1,0:T(8,128)(2,1)S(1)}, f16[1024,256]{1,0:T(8,128)(2,1)S(1)}, u32[]{:S(2)}, u32[]{:S(2)}) %collective-permute-start.8) | collective-permute-done | bytes 524320 | tf_op jit(solution)/shard_map/ppermute | solution.py:356
  31.1 0.0 copy-start.2
  31.1 0.4 multiply_reduce_fusion
  31.5 3.1 %collective-permute-start.12 = (f32[1,256]{1,0:T(1,128)S(1)}, f32[1,256]{1,0:T(1,128)S(1)}, u32[]{:S(2)}, u32[]{:S(2)}) collective-permute-start(f32[1,256]{1,0:T(1,128)S(1)} %bitcast.10), channel_id=1, source_target_pairs={{0,16},{8,24},{16,0},{24,8},{1,17},{9,25},{17,1},{25,9},{2,18},{10... | collective-permute-start | bytes 3080 | tf_op jit(solution)/shard_map/ppermute | solution.py:380
  34.6 1.1 %collective-permute-start.11 = (f32[1,256]{1,0:T(1,128)S(1)}, f32[1,256]{1,0:T(1,128)S(1)}, u32[]{:S(2)}, u32[]{:S(2)}) collective-permute-start(f32[1,256]{1,0:T(1,128)S(1)} %bitcast.11), channel_id=1, source_target_pairs={{0,24},{8,16},{16,8},{24,0},{1,25},{9,17},{17,9},{25,1},{2,26},{10... | collective-permute-start | bytes 3080 | tf_op jit(solution)/shard_map/ppermute | solution.py:379
  35.7 0.4 square_rows.1
  36.1 0.5 collective-permute-done.12
  36.6 2.7 %collective-permute-done.11 = f32[1,256]{1,0:T(1,128)S(1)} collective-permute-done((f32[1,256]{1,0:T(1,128)S(1)}, f32[1,256]{1,0:T(1,128)S(1)}, u32[]{:S(2)}, u32[]{:S(2)}) %collective-permute-start.11) | collective-permute-done | bytes 1056 | tf_op jit(solution)/shard_map/ppermute | solution.py:379
  39.4 0.2 weighted_rows.1
  39.6 0.1 collective-permute-start.13
  39.7 1.2 %collective-permute-done.13.came = f32[16,128]{1,0:T(8,128)S(1)} collective-permute-done((f32[16,128]{1,0:T(8,128)S(1)}, f32[16,128]{1,0:T(8,128)S(1)}, u32[]{:S(2)}, u32[]{:S(2)}) %collective-permute-start.13) | collective-permute-done | bytes 8224 | tf_op jit(solution)/shard_map/ppermute | solution.py:397
  40.9 18.6 %all_to_all.5.came = bf16[32,16,128]{2,1,0:T(8,128)(2,1)S(1)} all-to-all(bf16[32,16,128]{2,1,0:T(8,128)(2,1)S(1)} %message.1), channel_id=1, replica_groups=mesh['y'=4,'c'=2,'x'=4,'z'=8] {'y','z'}, dimensions={0} | all-to-all | bytes 262144 | tf_op jit(solution)/shard_map/all_to_all | solution.py:399
  59.4 0.2 row_reduce.1.mine
  59.6 0.1 collective-permute-start.14
  59.7 1.2 %collective-permute-done.14.twin = f32[8,128]{1,0:T(8,128)S(1)} collective-permute-done((f32[8,128]{1,0:T(8,128)S(1)}, f32[8,128]{1,0:T(8,128)S(1)}, u32[]{:S(2)}, u32[]{:S(2)}) %collective-permute-start.14) | collective-permute-done | bytes 4128 | tf_op jit(solution)/shard_map/ppermute | solution.py:409
  60.9 1.5 %collective-permute-start.17 = (f32[8,128]{1,0:T(8,128)S(1)}, f32[8,128]{1,0:T(8,128)S(1)}, u32[]{:S(2)}, u32[]{:S(2)}) collective-permute-start(f32[8,128]{1,0:T(8,128)S(1)} %add.67.scalars_a), channel_id=1, source_target_pairs={{0,16},{8,24},{16,0},{24,8},{1,17},{9,25},{17,1},{25,9},{2,18},{10... | collective-permute-start | bytes 12296 | tf_op jit(solution)/shard_map/ppermute | solution.py:414
  62.3 1.1 %collective-permute-start.16 = (f32[8,128]{1,0:T(8,128)S(1)}, f32[8,128]{1,0:T(8,128)S(1)}, u32[]{:S(2)}, u32[]{:S(2)}) collective-permute-start(f32[8,128]{1,0:T(8,128)S(1)} %add.67.scalars_a), channel_id=1, source_target_pairs={{0,24},{8,16},{16,8},{24,0},{1,25},{9,17},{17,9},{25,1},{2,26},{10... | collective-permute-start | bytes 12296 | tf_op jit(solution)/shard_map/ppermute | solution.py:413
  63.4 0.9 %collective-permute-start.15 = (f32[8,128]{1,0:T(8,128)S(1)}, f32[8,128]{1,0:T(8,128)S(1)}, u32[]{:S(2)}, u32[]{:S(2)}) collective-permute-start(f32[8,128]{1,0:T(8,128)S(1)} %add.67.scalars_a), channel_id=1, source_target_pairs={{0,8},{8,0},{16,24},{24,16},{1,9},{9,1},{17,25},{25,17},{2,10},{10... | collective-permute-start | bytes 12296 | tf_op jit(solution)/shard_map/ppermute | solution.py:412
  64.3 0.7 %normalise.1 = (f32[1024,256]{1,0:T(8,128)S(1)}, f32[8,128]{1,0:T(8,128)}, f32[1,256]{1,0:T(1,128)}) custom-call(s32[1]{0:T(128)} %bitcast.4.core, f32[1024,256]{1,0:T(8,128)S(1)} %get-tuple-element.62.gradient, f32[8,128]{1,0:T(8,128)S(1)} %row_reduce.1.mine, f32[8,128]{1,0:T(8,128)S(1)} %collective-permute-done.14.twin, f32[1,256]{1,0:T(1,128)S(1)} %bitcast.14, ...), custom_call_target="tpu_custom_call" | custom-call | flops 1 | bytes 1 | tf_op jit(solution)/shard_map/normalise/pallas_call | solution.py:49
  65.0 0.9 %collective-permute-done.17 = f32[8,128]{1,0:T(8,128)S(1)} collective-permute-done((f32[8,128]{1,0:T(8,128)S(1)}, f32[8,128]{1,0:T(8,128)S(1)}, u32[]{:S(2)}, u32[]{:S(2)}) %collective-permute-start.17) | collective-permute-done | bytes 4128 | tf_op jit(solution)/shard_map/ppermute | solution.py:414
  66.0 1.2 %collective-permute-done.16 = f32[8,128]{1,0:T(8,128)S(1)} collective-permute-done((f32[8,128]{1,0:T(8,128)S(1)}, f32[8,128]{1,0:T(8,128)S(1)}, u32[]{:S(2)}, u32[]{:S(2)}) %collective-permute-start.16) | collective-permute-done | bytes 4128 | tf_op jit(solution)/shard_map/ppermute | solution.py:413
  67.1 1.1 %step.1 = f32[1024,256]{1,0:T(8,128)} custom-call(f32[8,128]{1,0:T(8,128)S(1)} %add.67.scalars_a, f32[8,128]{1,0:T(8,128)S(1)} %add_add_fusion.scalars_b, f32[1024,256]{1,0:T(8,128)S(1)} %copy-done, f32[1024,256]{1,0:T(8,128)S(1)} %get-tuple-element.58.update), custom_call_target="tpu_custom_call" | custom-call | flops 1 | bytes 1 | tf_op jit(solution)/shard_map/step/pallas_call | solution.py:427
  (19 shorter events, 0.1 us)
Async XLA Ops:
  3.9 2.7 %collective-permute-start = (f32[1024,256]{1,0:T(8,128)S(1)}, f32[1024,256]{1,0:T(8,128)S(1)}, u32[]{:S(2)}, u32[]{:S(2)}) collective-permute-start(f32[1024,256]{1,0:T(8,128)S(1)} %get-tuple-element.41), channel_id=1, source_target_pairs={{0,32},{32,0},{1,33},{33,1},{2,34},{34,2},{3,35},{35,3},{4,36},{36... | collective-permute-start | bytes 3145736 | tf_op jit(solution)/shard_map/ppermute | solution.py:319
  6.8 9.8 %collective-permute-start.5 = (f16[1024,256]{1,0:T(8,128)(2,1)S(1)}, f16[1024,256]{1,0:T(8,128)(2,1)S(1)}, u32[]{:S(2)}, u32[]{:S(2)}) collective-permute-start(f16[1024,256]{1,0:T(8,128)(2,1)S(1)} %add_convert_fusion.2), channel_id=1, source_target_pairs={{0,192},{32,96},{64,0},{96,160},{128,64},{160,224},{192,128},{224,... | collective-permute-start | bytes 1572872 | tf_op jit(solution)/shard_map/ppermute | solution.py:335
  12.0 3.3 %collective-permute-start.3 = (f16[352,256]{1,0:T(8,128)(2,1)S(1)}, f16[352,256]{1,0:T(8,128)(2,1)S(1)}, u32[]{:S(2)}, u32[]{:S(2)}) collective-permute-start(f16[352,256]{1,0:T(8,128)(2,1)S(1)} %slice.27), channel_id=1, source_target_pairs={{0,32},{32,0},{1,33},{33,1},{2,34},{34,2},{3,35},{35,3},{4,36},{36... | collective-permute-start | bytes 540680 | tf_op jit(solution)/shard_map/ppermute | solution.py:304
  12.2 4.5 %collective-permute-start.4 = (f16[1024,256]{1,0:T(8,128)(2,1)S(1)}, f16[1024,256]{1,0:T(8,128)(2,1)S(1)}, u32[]{:S(2)}, u32[]{:S(2)}) collective-permute-start(f16[1024,256]{1,0:T(8,128)(2,1)S(1)} %convert_element_type.38), channel_id=1, source_target_pairs={{0,32},{32,0},{1,33},{33,1},{2,34},{34,2},{3,35},{35,3},{4,36},{36... | collective-permute-start | bytes 1572872 | tf_op jit(solution)/shard_map/ppermute | solution.py:304
  12.8 2.5 %collective-permute-start.2 = (f16[336,256]{1,0:T(8,128)(2,1)S(1)}, f16[336,256]{1,0:T(8,128)(2,1)S(1)}, u32[]{:S(2)}, u32[]{:S(2)}) collective-permute-start(f16[336,256]{1,0:T(8,128)(2,1)S(1)} %get-tuple-element.66), channel_id=1, source_target_pairs={{0,32},{32,0},{1,33},{33,1},{2,34},{34,2},{3,35},{35,3},{4,36},{36... | collective-permute-start | bytes 516104 | tf_op jit(solution)/shard_map/ppermute | solution.py:304
  12.9 2.4 %collective-permute-start.1 = (f16[336,256]{1,0:T(8,128)(2,1)S(1)}, f16[336,256]{1,0:T(8,128)(2,1)S(1)}, u32[]{:S(2)}, u32[]{:S(2)}) collective-permute-start(f16[336,256]{1,0:T(8,128)(2,1)S(1)} %get-tuple-element.65), channel_id=1, source_target_pairs={{0,32},{32,0},{1,33},{33,1},{2,34},{34,2},{3,35},{35,3},{4,36},{36... | collective-permute-start | bytes 516104 | tf_op jit(solution)/shard_map/ppermute | solution.py:304
  15.5 15.5 %collective-permute-start.8 = (f16[1024,256]{1,0:T(8,128)(2,1)S(1)}, f16[1024,256]{1,0:T(8,128)(2,1)S(1)}, u32[]{:S(2)}, u32[]{:S(2)}) collective-permute-start(f16[1024,256]{1,0:T(8,128)(2,1)S(1)} %add_convert_fusion.1), channel_id=1, source_target_pairs={{0,64},{32,224},{64,128},{96,32},{128,192},{160,96},{192,0},{224,1... | collective-permute-start | bytes 1572872 | tf_op jit(solution)/shard_map/ppermute | solution.py:356
  16.9 14.2 %collective-permute-start.9 = (f16[1024,256]{1,0:T(8,128)(2,1)S(1)}, f16[1024,256]{1,0:T(8,128)(2,1)S(1)}, u32[]{:S(2)}, u32[]{:S(2)}) collective-permute-start(f16[1024,256]{1,0:T(8,128)(2,1)S(1)} %add_convert_fusion), channel_id=1, source_target_pairs={{0,192},{32,96},{64,0},{96,160},{128,64},{160,224},{192,128},{224,... | collective-permute-start | bytes 1572872 | tf_op jit(solution)/shard_map/ppermute | solution.py:359
  24.1 11.6 %copy-start = (f32[1024,256]{1,0:T(8,128)S(1)}, f32[1024,256]{1,0:T(8,128)}, u32[]{:S(2)}) copy-start(f32[1024,256]{1,0:T(8,128)} %param.13) | copy-start | bytes 3145732
  24.3 15.0 %copy-start.1 = (f32[256]{0:T(256)S(1)}, f32[256]{0:T(256)}, u32[]{:S(2)}) copy-start(f32[256]{0:T(256)} %param.11) | copy-start | bytes 3076
  24.3 6.8 %collective-permute-start.7 = (f16[512,256]{1,0:T(8,128)(2,1)S(1)}, f16[512,256]{1,0:T(8,128)(2,1)S(1)}, u32[]{:S(2)}, u32[]{:S(2)}) collective-permute-start(f16[512,256]{1,0:T(8,128)(2,1)S(1)} %get-tuple-element.64), channel_id=1, source_target_pairs={{0,32},{32,0},{1,33},{33,1},{2,34},{34,2},{3,35},{35,3},{4,36},{36... | collective-permute-start | bytes 786440 | tf_op jit(solution)/shard_map/ppermute | solution.py:304
  24.4 6.7 %collective-permute-start.6 = (f16[512,256]{1,0:T(8,128)(2,1)S(1)}, f16[512,256]{1,0:T(8,128)(2,1)S(1)}, u32[]{:S(2)}, u32[]{:S(2)}) collective-permute-start(f16[512,256]{1,0:T(8,128)(2,1)S(1)} %get-tuple-element.63), channel_id=1, source_target_pairs={{0,32},{32,0},{1,33},{33,1},{2,34},{34,2},{3,35},{35,3},{4,36},{36... | collective-permute-start | bytes 786440 | tf_op jit(solution)/shard_map/ppermute | solution.py:304
  31.1 28.3 %copy-start.2 = (f32[1024]{0:T(1024)S(1)}, f32[1024]{0:T(1024)}, u32[]{:S(2)}) copy-start(f32[1024]{0:T(1024)} %param.10) | copy-start | bytes 12292
  31.5 5.2 %collective-permute-start.12 = (f32[1,256]{1,0:T(1,128)S(1)}, f32[1,256]{1,0:T(1,128)S(1)}, u32[]{:S(2)}, u32[]{:S(2)}) collective-permute-start(f32[1,256]{1,0:T(1,128)S(1)} %bitcast.10), channel_id=1, source_target_pairs={{0,16},{8,24},{16,0},{24,8},{1,17},{9,25},{17,1},{25,9},{2,18},{10... | collective-permute-start | bytes 3080 | tf_op jit(solution)/shard_map/ppermute | solution.py:380
  34.6 4.8 %collective-permute-start.11 = (f32[1,256]{1,0:T(1,128)S(1)}, f32[1,256]{1,0:T(1,128)S(1)}, u32[]{:S(2)}, u32[]{:S(2)}) collective-permute-start(f32[1,256]{1,0:T(1,128)S(1)} %bitcast.11), channel_id=1, source_target_pairs={{0,24},{8,16},{16,8},{24,0},{1,25},{9,17},{17,9},{25,1},{2,26},{10... | collective-permute-start | bytes 3080 | tf_op jit(solution)/shard_map/ppermute | solution.py:379
  35.7 3.7 %collective-permute-start.10 = (f32[1,256]{1,0:T(1,128)S(1)}, f32[1,256]{1,0:T(1,128)S(1)}, u32[]{:S(2)}, u32[]{:S(2)}) collective-permute-start(f32[1,256]{1,0:T(1,128)S(1)} %bitcast.12), channel_id=1, source_target_pairs={{0,8},{8,0},{16,24},{24,16},{1,9},{9,1},{17,25},{25,17},{2,10},{10... | collective-permute-start | bytes 3080 | tf_op jit(solution)/shard_map/ppermute | solution.py:378
  39.6 1.3 %collective-permute-start.13 = (f32[16,128]{1,0:T(8,128)S(1)}, f32[16,128]{1,0:T(8,128)S(1)}, u32[]{:S(2)}, u32[]{:S(2)}) collective-permute-start(f32[16,128]{1,0:T(8,128)S(1)} %get-tuple-element.57), channel_id=1, source_target_pairs={{0,32},{32,0},{1,33},{33,1},{2,34},{34,2},{3,35},{35,3},{4,36},{36... | collective-permute-start | bytes 24584 | tf_op jit(solution)/shard_map/ppermute | solution.py:397
  59.6 1.3 %collective-permute-start.14 = (f32[8,128]{1,0:T(8,128)S(1)}, f32[8,128]{1,0:T(8,128)S(1)}, u32[]{:S(2)}, u32[]{:S(2)}) collective-permute-start(f32[8,128]{1,0:T(8,128)S(1)} %row_reduce.1.mine), channel_id=1, source_target_pairs={{0,32},{32,0},{1,33},{33,1},{2,34},{34,2},{3,35},{35,3},{4,36},{36... | collective-permute-start | bytes 12296 | tf_op jit(solution)/shard_map/ppermute | solution.py:409
  60.9 5.1 %collective-permute-start.17 = (f32[8,128]{1,0:T(8,128)S(1)}, f32[8,128]{1,0:T(8,128)S(1)}, u32[]{:S(2)}, u32[]{:S(2)}) collective-permute-start(f32[8,128]{1,0:T(8,128)S(1)} %add.67.scalars_a), channel_id=1, source_target_pairs={{0,16},{8,24},{16,0},{24,8},{1,17},{9,25},{17,1},{25,9},{2,18},{10... | collective-permute-start | bytes 12296 | tf_op jit(solution)/shard_map/ppermute | solution.py:414
  62.3 4.8 %collective-permute-start.16 = (f32[8,128]{1,0:T(8,128)S(1)}, f32[8,128]{1,0:T(8,128)S(1)}, u32[]{:S(2)}, u32[]{:S(2)}) collective-permute-start(f32[8,128]{1,0:T(8,128)S(1)} %add.67.scalars_a), channel_id=1, source_target_pairs={{0,24},{8,16},{16,8},{24,0},{1,25},{9,17},{17,9},{25,1},{2,26},{10... | collective-permute-start | bytes 12296 | tf_op jit(solution)/shard_map/ppermute | solution.py:413
  63.4 3.7 %collective-permute-start.15 = (f32[8,128]{1,0:T(8,128)S(1)}, f32[8,128]{1,0:T(8,128)S(1)}, u32[]{:S(2)}, u32[]{:S(2)}) collective-permute-start(f32[8,128]{1,0:T(8,128)S(1)} %add.67.scalars_a), channel_id=1, source_target_pairs={{0,8},{8,0},{16,24},{24,16},{1,9},{9,1},{17,25},{25,17},{2,10},{10... | collective-permute-start | bytes 12296 | tf_op jit(solution)/shard_map/ppermute | solution.py:412
